TPU v7x, 256 devices: a whole 4x4x8 slice. The times are simulated.
256 devices in a mesh: group: 4 (over z_lo, core), dp: 64 (over z_hi, x, y).
Axes of the slice: x: 4, y: 4, z: 8 (z_hi: 4, z_lo: 2; z = z_hi * 2 + z_lo), core: 2. Of those that a mesh axis runs over, the one named last changes fastest.
Arguments:
- grads: bfloat16 [256, 12, 512, 512], P(('group', 'dp')), may hold values from -15000 to 15000
Outputs:
- roots: float32 [2, 12, 512, 512], P(None, None, 'dp', 'group')
All inputs are finite; a program needn't handle non-finite values.
Results may differ from a plain program's by a relative error of at most 0.0003.
Values sent between devices are 32-bit elements; how exact they have to be, the bound alone decides.
No kernel may reach another device: no remote copies, remote signals or barrier semaphores. Data moves between devices by JAX's collectives and lax.ppermute only.
A program may use at most 128 MiB of HBM per device.

v0:
```python
import jax
import jax.numpy as jnp
from jax import lax
from jax.sharding import PartitionSpec as P

ITERS = 4


def spread(value, axis, source):
    kept = jnp.where(lax.axis_index(axis) == source, value, 0).astype(value.dtype)
    return lax.psum(kept, axis)


def gram_rows(local_grads):
    left_gram = jnp.einsum(
        "nik,njk->inj", local_grads, local_grads, preferred_element_type=jnp.float32
    )
    right_gram = jnp.einsum(
        "nki,nkj->inj", local_grads, local_grads, preferred_element_type=jnp.float32
    )
    return jnp.concatenate([left_gram, right_gram], axis=1)


def inverse_root(matrices):
    size_n = matrices.shape[-1]
    identity = jnp.eye(size_n, dtype=jnp.float32)
    frobenius = jnp.sqrt(jnp.sum(matrices * matrices, axis=(1, 2)))
    scaling = 2.5 / frobenius
    iterate = jnp.sqrt(jnp.sqrt(scaling))[:, None, None] * identity
    coupled = scaling[:, None, None] * matrices
    for sweep in range(ITERS):
        step_matrix = (5.0 * identity - coupled) * 0.25
        iterate = jnp.einsum("kij,kjl->kil", iterate, step_matrix, precision=lax.Precision.HIGHEST)
        squared = jnp.einsum(
            "kij,kjl->kil", step_matrix, step_matrix, precision=lax.Precision.HIGHEST
        )
        fourth = jnp.einsum("kij,kjl->kil", squared, squared, precision=lax.Precision.HIGHEST)
        coupled = jnp.einsum("kij,kjl->kil", fourth, coupled, precision=lax.Precision.HIGHEST)
    return iterate


def body(grads):
    local_grads = grads[0]
    blocks = local_grads.shape[0]
    block_order = local_grads.shape[1]
    groups = lax.axis_size("group")
    owners = lax.axis_size("dp")
    row_share = block_order // owners
    matrix_count = 2 * blocks
    partial_value = lax.psum_scatter(gram_rows(local_grads), "dp", scatter_dimension=0, tiled=True)
    summed = lax.psum(partial_value, "group")
    stats_rows = summed * (1.0 / (groups * owners * block_order))
    slots = -(-matrix_count // owners)
    padding_count = slots * owners - matrix_count
    row_ids = lax.axis_index("dp") * row_share + lax.broadcasted_iota(
        jnp.int32, (row_share, block_order), 0
    )
    col_ids = lax.broadcasted_iota(jnp.int32, (row_share, block_order), 1)
    identity_rows = (row_ids == col_ids).astype(jnp.float32)
    filler = jnp.broadcast_to(identity_rows[:, None, :], (row_share, padding_count, block_order))
    stats_rows = jnp.concatenate([stats_rows, filler], axis=1)
    outgoing = jnp.transpose(
        stats_rows.reshape(row_share, slots, owners, block_order), (1, 2, 0, 3)
    )
    is_root = lax.axis_index("group") == groups - 1
    items = lax.all_to_all(outgoing, "dp", split_axis=1, concat_axis=1, tiled=True)
    item_count = items.shape[0]
    matrices = items.reshape(item_count, block_order, block_order)
    root_mats = lax.cond(is_root, inverse_root, jnp.zeros_like, matrices)
    returned = root_mats.reshape(item_count, owners, row_share, block_order)
    arrived = lax.all_to_all(returned, "dp", split_axis=1, concat_axis=1, tiled=True)
    my_rows = jnp.transpose(arrived, (2, 0, 1, 3)).reshape(row_share, slots * owners, block_order)
    my_rows = my_rows[:, :matrix_count].reshape(row_share, 2, blocks, block_order)
    result = jnp.transpose(my_rows, (1, 2, 0, 3))
    result = spread(result, "group", groups - 1)
    col_share = block_order // groups
    return lax.dynamic_slice_in_dim(result, lax.axis_index("group") * col_share, col_share, 3)


def solution(mesh):
    placed = (P(("group", "dp"), None, None, None),)
    return jax.shard_map(
        body, mesh=mesh, in_specs=placed, out_specs=P(None, None, "dp", "group"), check_vma=False
    )
```

profile of v0, /device:TPU:1, one launch (start us, length us, event | category | flops | bytes accessed | tf_op | source)
XLA Modules:
  0.0 561.2 jit_solution(10850743643554816120)
XLA Ops:
  6.5 12.8 %fusion.71 = f32[512,12,512]{0,2,1:T(8,128)} fusion(bf16[1,12,512,512]{3,2,1,0:T(8,128)(2,1)} %param.3), kind=kOutput, calls=%fused_computation.74 | convolution fusion | flops 3221225472 | bytes 18874368 | tf_op jit(solution)/shard_map/nki,nkj->inj/dot_general | solution.py:18
  19.3 6.3 %fusion.68 = f32[512,12,512]{0,2,1:T(8,128)} fusion(bf16[1,12,512,512]{3,2,1,0:T(8,128)(2,1)S(1)} %copy-done), kind=kOutput, calls=%fused_computation.73 | convolution fusion | flops 3221225472 | bytes 18874368 | tf_op jit(solution)/shard_map/nik,njk->inj/dot_general | solution.py:15
  25.6 18.1 %pad_maximum_fusion = f32[512,24,512]{0,2,1:T(8,128)} fusion(f32[512,12,512]{0,2,1:T(8,128)} %fusion.71, f32[512,12,512]{0,2,1:T(8,128)} %fusion.68), kind=kLoop, calls=%fused_computation.68 | loop fusion | flops 6291456 | bytes 50331648 | tf_op jit(solution)/shard_map/concatenate | solution.py:21
  43.7 25.1 %copy.5 = f32[512,24,512]{2,1,0:T(8,128)} copy(f32[512,24,512]{0,2,1:T(8,128)} %pad_maximum_fusion) | data formatting | bytes 50331648 | tf_op jit(solution)/shard_map/concatenate | solution.py:21
  68.8 0.0 reduce-scatter.2.cloned.1.call-update
  68.8 0.0 all-reduce.3.cloned.1.call-start
  68.9 309.8 %reduce-scatter.2.cloned.1.call-done = f32[8,24,512]{2,1,0:T(8,128)} async-done(((f32[512,24,512]{2,1,0:T(8,128)}), f32[8,24,512]{2,1,0:T(8,128)}) %reduce-scatter.2.cloned.1.call-update) | async-done | bytes 393232 | tf_op jit(solution)/shard_map/reduce_scatter | solution.py:50
  378.7 0.0 all-reduce.3.cloned.1.call-update
  378.7 0.1 fusion.74
  378.8 43.5 %all-reduce.3.cloned.1.call-done = f32[8,24,512]{2,1,0:T(8,128)} async-done(((f32[8,24,512]{2,1,0:T(8,128)}), f32[8,24,512]{2,1,0:T(8,128)}) %all-reduce.3.cloned.1.call-update) | async-done | bytes 393232 | tf_op jit(solution)/shard_map/psum | solution.py:51
  422.3 1.0 broadcast_multiply_fusion
  423.3 0.2 copy.6
  423.5 0.1 broadcast_in_dim.5
  423.6 1.1 maximum_bitcast_fusion
  424.7 11.7 %all-to-all-start = ((f32[1,64,8,512]{3,2,0,1:T(8,128)}), f32[1,64,8,512]{3,2,0,1:T(8,128)S(1)}, u32[]{:S(2)}, u32[]{:S(2)}) async-start(f32[1,64,8,512]{3,2,0,1:T(8,128)} %maximum_bitcast_fusion), calls=%async_computation.1 | async-start | bytes 2097152 | tf_op jit(solution)/shard_map/all_to_all | solution.py:66
  436.4 0.0 all-reduce.5.cloned.1.call-start
  436.4 24.6 %all-to-all-done = f32[1,64,8,512]{3,2,0,1:T(8,128)S(1)} async-done(((f32[1,64,8,512]{3,2,0,1:T(8,128)}), f32[1,64,8,512]{3,2,0,1:T(8,128)S(1)}, u32[]{:S(2)}, u32[]{:S(2)}) %all-to-all-start) | async-done | bytes 1048608 | tf_op jit(solution)/shard_map/all_to_all | solution.py:66
  461.0 0.3 conditional.1
  461.0 0.1 broadcast.107
  461.3 27.9 %all_to_all.11 = f32[1,64,8,512]{3,2,0,1:T(8,128)S(1)} all-to-all(f32[1,64,8,512]{3,2,0,1:T(8,128)S(1)} %bitcast.72), channel_id=1, replica_groups=mesh['group'=4,'dp'=64] {'dp'}, dimensions={1} | all-to-all | bytes 2097152 | tf_op jit(solution)/shard_map/all_to_all | solution.py:71
  489.2 0.8 slice_select_fusion
  490.0 0.0 all-reduce.5.cloned.1.call-update
  490.0 63.1 %all-reduce.5.cloned.1.call-done = f32[2,12,8,512]{3,2,1,0:T(8,128)} async-done(((f32[2,12,8,512]{3,2,1,0:T(8,128)}), f32[2,12,8,512]{3,2,1,0:T(8,128)}) %all-reduce.5.cloned.1.call-update) | async-done | bytes 393232 | tf_op jit(solution)/shard_map/psum | solution.py:11
  553.1 1.5 constant_dynamic-slice_fusion
  (4 shorter events, 0.0 us)
Async XLA Ops:
  6.5 372.1 %reduce-scatter.2.cloned.1.call-start = ((), (), s32[]{:S(2)}) async-start(), calls=%async_computation.3 | async-start | bytes 25559040 | tf_op jit(solution)/shard_map/reduce_scatter | solution.py:50
  6.5 12.8 %copy-start = (bf16[1,12,512,512]{3,2,1,0:T(8,128)(2,1)S(1)}, bf16[1,12,512,512]{3,2,1,0:T(8,128)(2,1)}, u32[]{:S(2)}) copy-start(bf16[1,12,512,512]{3,2,1,0:T(8,128)(2,1)} %param.3) | copy-start | bytes 18874372
  68.8 353.5 %all-reduce.3.cloned.1.call-start = ((), (), s32[]{:S(2)}) async-start(), calls=%async_computation.4 | async-start | bytes 786432 | tf_op jit(solution)/shard_map/psum | solution.py:51
  424.7 36.3 %all-to-all-start = ((f32[1,64,8,512]{3,2,0,1:T(8,128)}), f32[1,64,8,512]{3,2,0,1:T(8,128)S(1)}, u32[]{:S(2)}, u32[]{:S(2)}) async-start(f32[1,64,8,512]{3,2,0,1:T(8,128)} %maximum_bitcast_fusion), calls=%async_computation.1 | async-start | bytes 2097152 | tf_op jit(solution)/shard_map/all_to_all | solution.py:66
  436.4 116.8 %all-reduce.5.cloned.1.call-start = ((), (), s32[]{:S(2)}) async-start(), calls=%async_computation.5 | async-start | bytes 786432 | tf_op jit(solution)/shard_map/psum | solution.py:11
Sparse Core Ops, SparseCore 0:
  68.9 309.7 reduce-scatter.1
  381.3 40.9 all-reduce.2
  490.1 62.9 all-reduce.4
where the time goes:
time: 562 us; the launch traced here: 561 us
  waiting for transfers between devices  441 us (78%)
  blocking collectives  27.9 us (5%)
  local copies, waits for them, and re-layouts  27.1 us (5%)
  other arithmetic  21 us (4%)
  matrix products  19.1 us (3%)
  between operations  13.2 us (2%)
  starting transfers between devices  11.8 us (2%)
    reduce_scatter x1, waiting for transfers between devices, body(): lax.psum_scatter(gram_rows(local_grads), 'dp', scatter_dimension=0, tiled...  310 us
    psum x1, waiting for transfers between devices, spread(): return lax.psum(kept, axis)  63.1 us
    psum x1, waiting for transfers between devices, body(): summed = lax.psum(partial_value, 'group')  43.5 us
    all_to_all x1, blocking collectives, body(): lax.all_to_all(returned, 'dp', split_axis=1, concat_axis=1, tiled=True)  27.9 us
    concatenate x1, local copies, waits for them, and re-layouts, gram_rows(): return jnp.concatenate([left_gram, right_gram], axis=1)  25.1 us
    all_to_all x1, waiting for transfers between devices, body(): lax.all_to_all(outgoing, 'dp', split_axis=1, concat_axis=1, tiled=True)  24.6 us
    concatenate x1, other arithmetic, gram_rows(): return jnp.concatenate([left_gram, right_gram], axis=1)  18.1 us
    dot_general x1, matrix products, gram_rows(): jnp.einsum('nki,nkj->inj', local_grads, local_grads, preferred_element_ty...  12.8 us
  transfers between devices with their start and end apart: 4, of which 4 were waited for; matrix products, arithmetic and copies ran while one was open for 0% of the time, Pallas kernels for 0%

commit v1 on v0

v1 whole, which is shorter than its diff:
```python
import functools

import jax
import jax.numpy as jnp
from jax import lax
from jax.experimental import pallas as pl
from jax.experimental.pallas import tpu as pltpu
from jax.sharding import Mesh
from jax.sharding import PartitionSpec as P

ITERS = 4
TOP = 64
BOT = 72
UNIT = TOP + BOT
SLABS = 8
TOP_ORDERS = (("x1", "y1", "z", "x2", "y2"), ("y1", "z", "x1", "x2", "y2"), ("z", "x1", "y1", "x2", "y2"))
BOT_ORDERS = (("x2", "y2", "z", "x1", "y1"), ("y2", "z", "x2", "x1", "y1"), ("z", "x2", "y2", "x1", "y1"))
PARAMS = pltpu.CompilerParams(vmem_limit_bytes=48 * 1024 * 1024)


def place(order, flags):
    at = 0
    for name in order:
        at = at * 2 + flags[name]
    return at


def gram_kernel(part, where_ref, grads_ref, own_ref, away_ref):
    order_top, order_bot = TOP_ORDERS[part], BOT_ORDERS[part]
    step = pl.program_id(0)
    row_y, low_z, core = where_ref[1], where_ref[2], where_ref[3]
    block = grads_ref[0]
    flipped = block.T
    half = block.shape[0] // 2
    rows = lax.broadcasted_iota(jnp.int32, (half, half), 0)
    cols = lax.broadcasted_iota(jnp.int32, (half, half), 1)
    slab_rows = half // SLABS
    for side in range(2):
        lhs, rhs = (block, flipped) if side == 0 else (flipped, block)
        mult = functools.partial(jnp.dot, preferred_element_type=jnp.float32)
        corner = mult(lhs[:half], rhs[:, :half])
        cross = mult(lhs[:half], rhs[:, half:])
        last = mult(lhs[half:], rhs[:, half:])
        fold = jnp.where(rows <= cols, corner, last)
        diagonal = jnp.where(rows == cols, last, 0.0)

        def write(out_ref):
            for slab in range(SLABS):
                from_y = lax.bitwise_xor(row_y, slab // 2)
                high = lax.shift_right_logical(from_y, 1)
                flags = {
                    "x1": lax.bitwise_and(step, 1),
                    "x2": lax.shift_right_logical(step, 1),
                    "y1": lax.bitwise_xor(lax.bitwise_and(from_y, 1), high),
                    "y2": high,
                    "z": lax.bitwise_xor(low_z, slab % 2),
                }
                top = pl.multiple_of(place(order_top, flags) * TOP, 8)
                bot = pl.multiple_of(place(order_bot, flags) * BOT + 32 * TOP, 8)
                mine = slice(slab * slab_rows, (slab + 1) * slab_rows)
                out_ref[pl.ds(top, slab_rows), :] = cross[mine, :128]
                out_ref[pl.ds(top + slab_rows, slab_rows), :] = cross[mine, 128:]
                out_ref[pl.ds(bot, slab_rows), :] = fold[mine, :128]
                out_ref[pl.ds(bot + slab_rows, slab_rows), :] = fold[mine, 128:]
                side_cols = slice(0, 128) if slab < SLABS // 2 else slice(128, 256)
                line = jnp.sum(diagonal[mine, side_cols], axis=0, keepdims=True)
                out_ref[pl.ds(bot + 2 * slab_rows, 8), :] = jnp.broadcast_to(line, (8, 128))

        @pl.when(core == side)
        def _():
            write(own_ref)

        @pl.when(core != side)
        def _():
            write(away_ref)


def gram(part, where, grads):
    order = grads.shape[-1]

    def block_of(step, where_ref):
        high = lax.shift_right_logical(step, 1)
        relative = lax.bitwise_xor(lax.bitwise_and(step, 1), 3 * high)
        return (part * 4 + lax.bitwise_xor(where_ref[0], relative), 0, 0)

    shape = jax.ShapeDtypeStruct((32 * UNIT, 128), jnp.float32)
    whole = pl.BlockSpec((32 * UNIT, 128), lambda step, where_ref: (0, 0))
    return pl.pallas_call(
        functools.partial(gram_kernel, part),
        out_shape=(shape, shape),
        grid_spec=pltpu.PrefetchScalarGridSpec(
            num_scalar_prefetch=1,
            grid=(4,),
            in_specs=[pl.BlockSpec((1, order, order), block_of)],
            out_specs=(whole, whole),
        ),
        compiler_params=PARAMS,
        name=f"gram_{part}",
    )(where, grads)


def split(value):
    high = value.astype(jnp.bfloat16)
    return high, (value - high.astype(jnp.float32)).astype(jnp.bfloat16)


def product(left, right):
    mult = functools.partial(jnp.dot, preferred_element_type=jnp.float32)
    return mult(left[0], right[0]) + (mult(left[0], right[1]) + mult(left[1], right[0]))


def root_kernel(factor, where_ref, slabs_ref, out_ref, full, picked):
    half = 256
    order = 2 * half
    slab_rows = half // SLABS
    rows = lax.broadcasted_iota(jnp.int32, (half, half), 0)
    cols = lax.broadcasted_iota(jnp.int32, (half, half), 1)

    def gathered(first):
        left = jnp.concatenate([slabs_ref[s, first : first + slab_rows] for s in range(SLABS)], axis=0)
        right = jnp.concatenate(
            [slabs_ref[s, first + slab_rows : first + 2 * slab_rows] for s in range(SLABS)], axis=0
        )
        return jnp.concatenate([left, right], axis=1) * factor

    cross = gathered(0)
    fold = gathered(TOP)
    line = jnp.concatenate(
        [sum(slabs_ref[s, TOP + 64 : TOP + 65] for s in group) for group in (range(4), range(4, 8))], axis=1
    )
    turned = fold.T
    corner = jnp.where(rows <= cols, fold, turned)
    last = jnp.where(rows > cols, fold, jnp.where(rows == cols, line * factor, turned))
    matrix = jnp.concatenate(
        [jnp.concatenate([corner, cross], axis=1), jnp.concatenate([cross.T, last], axis=1)], axis=0
    )
    total = jnp.sum(jnp.sum(matrix * matrix, axis=0, keepdims=True), axis=1, keepdims=True)
    scaling = 2.5 / jnp.sqrt(total)
    coupled = scaling * matrix
    identity = (
        lax.broadcasted_iota(jnp.int32, (order, order), 0) == lax.broadcasted_iota(jnp.int32, (order, order), 1)
    ).astype(jnp.float32)
    row_y, low_z = where_ref[1], where_ref[2]
    iterate = None
    for sweep in range(ITERS):
        step_matrix = (5.0 * identity - coupled) * 0.25
        if sweep == 0:
            full[...] = jnp.sqrt(jnp.sqrt(scaling)) * step_matrix
            for chunk in range(16):
                start = pl.multiple_of(32 * chunk + 8 * row_y, 8)
                picked[8 * chunk : 8 * chunk + 8, :] = full[pl.ds(start, 8), :]
            iterate = picked[...]
        else:
            iterate = product(split(iterate), split(step_matrix))
        if sweep < ITERS - 1:
            parts = split(step_matrix)
            squared = split(product(parts, parts))
            fourth = split(product(squared, squared))
            coupled = product(fourth, split(coupled))
    for high in range(2):

        @pl.when(low_z == high)
        def _():
            for core in range(2):
                first = 128 * (2 * high + core)
                out_ref[16 * core : 16 * core + 16] = iterate[:, first : first + 128].reshape(16, 8, 128)


def inverse_root(where, slabs, factor):
    return pl.pallas_call(
        functools.partial(root_kernel, factor),
        out_shape=jax.ShapeDtypeStruct((32, 8, 128), jnp.float32),
        in_specs=[pl.BlockSpec(memory_space=pltpu.SMEM), pl.BlockSpec(memory_space=pltpu.VMEM)],
        out_specs=pl.BlockSpec(memory_space=pltpu.VMEM),
        scratch_shapes=[pltpu.VMEM((512, 512), jnp.float32), pltpu.VMEM((128, 512), jnp.float32)],
        compiler_params=PARAMS,
        name="inverse_root",
    )(where, slabs)


def swap(value, name, odd):
    if name in ("x1", "x2", "y1", "y2"):
        flip = 1 if name[1] == "1" else 3
        return lax.ppermute(value, name[0], [(i, i ^ flip) for i in range(4)])
    if not odd:
        return lax.ppermute(value, "z_lo", [(0, 1), (1, 0)])
    pairs = []
    for high in range(4):
        pairs += [(4 + high, (high + 1) % 4), ((high + 1) % 4, 4 + high)]
    return lax.ppermute(value, ("z_lo", "z_hi"), pairs)


def body(grads):
    local_grads = grads[0]
    order = local_grads.shape[1]
    where = jnp.stack([lax.axis_index(name).astype(jnp.int32) for name in ("x", "y", "z_lo", "core")])
    factor = 1.0 / (256 * order)
    lanes = []
    for part in range(3):
        own, away = gram(part, where, local_grads)
        came = lax.ppermute(away, "core", [(0, 1), (1, 0)])
        cut = 32 * TOP
        for odd, (first, size, orders) in enumerate(((0, cut, TOP_ORDERS), (cut, 32 * BOT, BOT_ORDERS))):
            middle = first + size // 2
            keep = own[first:middle] + came[first:middle]
            send = own[middle : first + size] + came[middle : first + size]
            lanes.append([orders[part], odd, keep, send])
    done = [[], []]
    for orders, odd, keep, send in lanes:
        for step in range(3):
            summed = keep + swap(send, orders[step], odd)
            middle = summed.shape[0] // 2
            if step < 2:
                keep, send = summed[:middle], summed[middle:]
        done[odd].append(summed)
    halves = []
    for odd in range(2):
        current = jnp.stack(done[odd])
        for name in ("x1", "y1") if odd else ("x2", "y2"):
            middle = current.shape[1] // 2
            current = current[:, :middle] + swap(current[:, middle:], name, odd)
        halves.append(current)
    parts = jnp.concatenate(halves, axis=1)
    parts = jnp.concatenate([parts, parts[:1]], axis=0)
    slab = jnp.sum(lax.all_to_all(parts, "z_hi", 0, 0, tiled=True), axis=0)
    slabs = lax.all_to_all(
        jnp.broadcast_to(slab[None], (SLABS, UNIT, 128)), ("y", "z_lo"), 0, 0, tiled=True
    )
    pieces = inverse_root(where, slabs, factor)
    arrived = lax.all_to_all(pieces, ("core", "z_hi", "x"), 0, 0, tiled=True)
    return arrived.reshape(2, 16, 8, 128)[:, :12]


def solution(mesh):
    axes = ("z_lo", "core", "z_hi", "x", "y")
    fine = Mesh(mesh.devices.reshape(2, 2, 4, 4, 4), axes)
    return jax.shard_map(
        body,
        mesh=fine,
        in_specs=(P(axes, None, None, None),),
        out_specs=P(None, None, ("z_hi", "x", "y"), ("z_lo", "core")),
        check_vma=False,
    )
```

time: 562 us -> 141 us (0.25)
  waiting for transfers between devices: 441 us -> 19.3 us
  Pallas kernels: 0 us -> 27.8 us
  local copies, waits for them, and re-layouts: 27.1 us -> 0.92 us
  starting transfers between devices: 11.8 us -> 33.4 us
  blocking collectives: 27.9 us -> 48.8 us
  matrix products: 19.1 us -> 0 us
  between operations: 13.2 us -> 0.49 us
  other arithmetic: 21 us -> 9.86 us
    reduce_scatter x1 -> x0, waiting for transfers between devices: 310 us -> none  [body(): lax.psum_scatter(gram_rows(local_grads), 'dp', scatter_dimension=0, tiled...]
    psum x2 -> x0, waiting for transfers between devices: 107 us -> none  [the longest x1 63.1 us: spread(): return lax.psum(kept, axis)]
    ppermute x0 -> x25, starting transfers between devices: none -> 33.4 us  [the longest x16 18.8 us: swap(): return lax.ppermute(value, name[0], [(i, i ^ flip) for i in range(4)])]
    pallas_call x0 -> x4, Pallas kernels: none -> 27.8 us  [the longest x3 18 us: gram(): pl.pallas_call(functools.partial(gram_kernel, part), out_shape=(shape, sh...]
    concatenate x1 -> x0, local copies, waits for them, and re-layouts: 25.1 us -> none  [gram_rows(): return jnp.concatenate([left_gram, right_gram], axis=1)]
    all_to_all x1 -> x0, waiting for transfers between devices: 24.6 us -> none  [body(): lax.all_to_all(outgoing, 'dp', split_axis=1, concat_axis=1, tiled=True)]
    all_to_all x1 -> x3, blocking collectives: 27.9 us -> 48.8 us  [the longest x1 25.7 us: body(): arrived = lax.all_to_all(pieces, ('core', 'z_hi', 'x'), 0, 0, tiled=True)]
    ppermute x0 -> x25, waiting for transfers between devices: none -> 19.3 us  [the longest x16 15.8 us: swap(): return lax.ppermute(value, name[0], [(i, i ^ flip) for i in range(4)])]
  transfers between devices with their start and end apart: 4 -> 25, of which waited for: 4 -> 8; matrix products, arithmetic and copies ran while one was open for 0% -> 7% of each run, Pallas kernels for 0% -> 9%
where the time goes in v1:
time: 141 us
  blocking collectives  48.8 us (35%)
  starting transfers between devices  33.4 us (24%)
  Pallas kernels  27.8 us (20%)
  waiting for transfers between devices  19.3 us (14%)
  other arithmetic  9.86 us (7%)
    all_to_all x1, blocking collectives, body(): arrived = lax.all_to_all(pieces, ('core', 'z_hi', 'x'), 0, 0, tiled=True)  25.7 us
    ppermute x16, starting transfers between devices, swap(): return lax.ppermute(value, name[0], [(i, i ^ flip) for i in range(4)])  18.8 us
    pallas_call x3, Pallas kernels, gram(): pl.pallas_call(functools.partial(gram_kernel, part), out_shape=(shape, sh...  18 us
    ppermute x16, waiting for transfers between devices, swap(): return lax.ppermute(value, name[0], [(i, i ^ flip) for i in range(4)])  15.8 us
    all_to_all x1, blocking collectives, body(): slab = jnp.sum(lax.all_to_all(parts, 'z_hi', 0, 0, tiled=True), axis=0)  12.8 us
    ppermute x3, starting transfers between devices, swap(): return lax.ppermute(value, ('z_lo', 'z_hi'), pairs)  10.4 us
    all_to_all x1, blocking collectives, body(): lax.all_to_all(jnp.broadcast_to(slab[None], (SLABS, UNIT, 128)), ('y', 'z...  10.3 us
    pallas_call x1, Pallas kernels, inverse_root(): pl.pallas_call(functools.partial(root_kernel, factor), out_shape=jax.Shap...  9.78 us
  transfers between devices with their start and end apart: 25, of which 8 were waited for; matrix products, arithmetic and copies ran while one was open for 7% of the time, Pallas kernels for 9%

profile of v1, /device:TPU:1, one launch (start us, length us, event | category | flops | bytes accessed | tf_op | source)
XLA Modules:
  0.0 140.6 jit_solution(15418199575478973011)
XLA Ops:
  0.1 6.0 %gram_2.1 = (f32[4352,128]{1,0:T(8,128)S(1)}, f32[4352,128]{1,0:T(8,128)S(1)}) custom-call(s32[4]{0:T(128)S(1)} %pad_add_fusion.where_ref, bf16[12,512,512]{2,1,0:T(8,128)(2,1)} %bitcast.18), custom_call_target="tpu_custom_call" | custom-call | tf_op jit(solution)/shard_map/gram_2/pallas_call | solution.py:88
  6.1 3.3 %collective-permute-start.8 = (f32[4352,128]{1,0:T(8,128)S(1)}, f32[4352,128]{1,0:T(8,128)}, u32[]{:S(2)}, u32[]{:S(2)}) collective-permute-start(f32[4352,128]{1,0:T(8,128)S(1)} %get-tuple-element.16), channel_id=1, source_target_pairs={{0,64},{64,0},{1,65},{65,1},{2,66},{66,2},{3,67},{67,3},{4,68},{68... | collective-permute-start | bytes 6684680 | tf_op jit(solution)/shard_map/ppermute | solution.py:201
  9.4 6.1 %gram_1.1 = (f32[4352,128]{1,0:T(8,128)S(1)}, f32[4352,128]{1,0:T(8,128)S(1)}) custom-call(s32[4]{0:T(128)S(1)} %pad_add_fusion.where_ref, bf16[12,512,512]{2,1,0:T(8,128)(2,1)} %bitcast.19), custom_call_target="tpu_custom_call" | custom-call | tf_op jit(solution)/shard_map/gram_1/pallas_call | solution.py:88
  15.5 6.0 %gram_0.1 = (f32[4352,128]{1,0:T(8,128)S(1)}, f32[4352,128]{1,0:T(8,128)S(1)}) custom-call(s32[4]{0:T(128)S(1)} %pad_add_fusion.where_ref, bf16[12,512,512]{2,1,0:T(8,128)(2,1)} %bitcast.20), custom_call_target="tpu_custom_call" | custom-call | tf_op jit(solution)/shard_map/gram_0/pallas_call | solution.py:88
  24.4 4.6 %collective-permute-start.20 = (f32[1152,128]{1,0:T(8,128)S(1)}, f32[1152,128]{1,0:T(8,128)S(1)}, u32[]{:S(2)}, u32[]{:S(2)}) collective-permute-start(f32[1152,128]{1,0:T(8,128)S(1)} %slice_add_fusion), channel_id=1, source_target_pairs={{128,16},{16,128},{144,32},{32,144},{160,48},{48,160},{176,0},{0,1... | collective-permute-start | bytes 1769480 | tf_op jit(solution)/shard_map/ppermute | solution.py:190
  30.2 1.4 collective-permute-start.5
  32.7 2.0 %collective-permute-start.17 = (f32[1152,128]{1,0:T(8,128)S(1)}, f32[1152,128]{1,0:T(8,128)S(1)}, u32[]{:S(2)}, u32[]{:S(2)}) collective-permute-start(f32[1152,128]{1,0:T(8,128)S(1)} %slice_add_fusion.2), channel_id=1, source_target_pairs={{0,3},{1,2},{2,1},{3,0},{4,7},{5,6},{6,5},{7,4},{8,11},{9,10},{10,... | collective-permute-start | bytes 1769480 | tf_op jit(solution)/shard_map/ppermute | solution.py:184
  34.8 1.3 collective-permute-start.1
  39.2 4.0 %collective-permute-done.5 = f32[1024,128]{1,0:T(8,128)S(1)} collective-permute-done((f32[1024,128]{1,0:T(8,128)S(1)}, f32[1024,128]{1,0:T(8,128)S(1)}, u32[]{:S(2)}, u32[]{:S(2)}) %collective-permute-start.5) | collective-permute-done | bytes 524320 | tf_op jit(solution)/shard_map/ppermute | solution.py:184
  43.1 1.2 collective-permute-start.10
  45.5 1.6 %collective-permute-done.1 = f32[1024,128]{1,0:T(8,128)S(1)} collective-permute-done((f32[1024,128]{1,0:T(8,128)S(1)}, f32[1024,128]{1,0:T(8,128)S(1)}, u32[]{:S(2)}, u32[]{:S(2)}) %collective-permute-start.1) | collective-permute-done | bytes 524320 | tf_op jit(solution)/shard_map/ppermute | solution.py:184
  48.9 2.6 %collective-permute-start.21 = (f32[576,128]{1,0:T(8,128)S(1)}, f32[576,128]{1,0:T(8,128)S(1)}, u32[]{:S(2)}, u32[]{:S(2)}) collective-permute-start(f32[576,128]{1,0:T(8,128)S(1)} %slice.269), channel_id=1, source_target_pairs={{0,12},{4,8},{8,4},{12,0},{1,13},{5,9},{9,5},{13,1},{2,14},{6,10},... | collective-permute-start | bytes 884744 | tf_op jit(solution)/shard_map/ppermute | solution.py:184
  52.7 3.1 %collective-permute-start.18 = (f32[576,128]{1,0:T(8,128)S(1)}, f32[576,128]{1,0:T(8,128)S(1)}, u32[]{:S(2)}, u32[]{:S(2)}) collective-permute-start(f32[576,128]{1,0:T(8,128)S(1)} %slice.263), channel_id=1, source_target_pairs={{128,16},{16,128},{144,32},{32,144},{160,48},{48,160},{176,0},{0,1... | collective-permute-start | bytes 884744 | tf_op jit(solution)/shard_map/ppermute | solution.py:190
  55.9 3.0 %collective-permute-start.15 = (f32[576,128]{1,0:T(8,128)S(1)}, f32[576,128]{1,0:T(8,128)S(1)}, u32[]{:S(2)}, u32[]{:S(2)}) collective-permute-start(f32[576,128]{1,0:T(8,128)S(1)} %slice.257), channel_id=1, source_target_pairs={{0,3},{1,2},{2,1},{3,0},{4,7},{5,6},{6,5},{7,4},{8,11},{9,10},{10,... | collective-permute-start | bytes 884744 | tf_op jit(solution)/shard_map/ppermute | solution.py:184
  60.2 2.5 %collective-permute-start.22 = (f32[288,128]{1,0:T(8,128)S(1)}, f32[288,128]{1,0:T(8,128)S(1)}, u32[]{:S(2)}, u32[]{:S(2)}) collective-permute-start(f32[288,128]{1,0:T(8,128)S(1)} %slice.271), channel_id=1, source_target_pairs={{0,3},{1,2},{2,1},{3,0},{4,7},{5,6},{6,5},{7,4},{8,11},{9,10},{10,... | collective-permute-start | bytes 442376 | tf_op jit(solution)/shard_map/ppermute | solution.py:184
  63.3 2.5 %collective-permute-start.19 = (f32[288,128]{1,0:T(8,128)S(1)}, f32[288,128]{1,0:T(8,128)S(1)}, u32[]{:S(2)}, u32[]{:S(2)}) collective-permute-start(f32[288,128]{1,0:T(8,128)S(1)} %slice.265), channel_id=1, source_target_pairs={{0,12},{4,8},{8,4},{12,0},{1,13},{5,9},{9,5},{13,1},{2,14},{6,10},... | collective-permute-start | bytes 442376 | tf_op jit(solution)/shard_map/ppermute | solution.py:184
  65.9 2.7 %collective-permute-start.16 = (f32[288,128]{1,0:T(8,128)S(1)}, f32[288,128]{1,0:T(8,128)S(1)}, u32[]{:S(2)}, u32[]{:S(2)}) collective-permute-start(f32[288,128]{1,0:T(8,128)S(1)} %slice.259), channel_id=1, source_target_pairs={{128,16},{16,128},{144,32},{32,144},{160,48},{48,160},{176,0},{0,1... | collective-permute-start | bytes 442376 | tf_op jit(solution)/shard_map/ppermute | solution.py:190
  69.1 2.1 %collective-permute-done.16 = f32[288,128]{1,0:T(8,128)S(1)} collective-permute-done((f32[288,128]{1,0:T(8,128)S(1)}, f32[288,128]{1,0:T(8,128)S(1)}, u32[]{:S(2)}, u32[]{:S(2)}) %collective-permute-start.16) | collective-permute-done | bytes 147488 | tf_op jit(solution)/shard_map/ppermute | solution.py:190
  71.4 5.0 %collective-permute-done.12 = f32[3,128,128]{2,1,0:T(8,128)S(1)} collective-permute-done((f32[3,128,128]{2,1,0:T(8,128)S(1)}, f32[3,128,128]{2,1,0:T(8,128)S(1)}, u32[]{:S(2)}, u32[]{:S(2)}) %collective-permute-start.12) | collective-permute-done | bytes 196640 | tf_op jit(solution)/shard_map/ppermute | solution.py:184
  76.7 4.5 %collective-permute-done.13 = f32[3,64,128]{2,1,0:T(8,128)S(1)} collective-permute-done((f32[3,64,128]{2,1,0:T(8,128)S(1)}, f32[3,64,128]{2,1,0:T(8,128)S(1)}, u32[]{:S(2)}, u32[]{:S(2)}) %collective-permute-start.13) | collective-permute-done | bytes 98336 | tf_op jit(solution)/shard_map/ppermute | solution.py:184
  81.3 12.8 %all_to_all.15 = f32[4,136,128]{2,1,0:T(8,128)S(1)} all-to-all(f32[4,136,128]{2,1,0:T(8,128)S(1)} %fusion.6), channel_id=1, replica_groups=mesh['z_lo'=2,'core'=2,'z_hi'=4,'x'=4,'y'=4] {'z_hi'}, dimensions={0} | all-to-all | bytes 557056 | tf_op jit(solution)/shard_map/all_to_all | solution.py:225
  94.2 10.3 %all_to_all.16.slabs_ref = f32[8,136,128]{2,1,0:T(8,128)S(1)} all-to-all(f32[8,136,128]{2,1,0:T(8,128)S(1)} %broadcast_in_dim.2), channel_id=1, replica_groups=mesh['z_lo'=2,'core'=2,'z_hi'=4,'x'=4,'y'=4] {'y','z_lo'}, dimensions={0} | all-to-all | bytes 1114112 | tf_op jit(solution)/shard_map/all_to_all | solution.py:226
  104.5 9.8 %inverse_root.1 = f32[32,8,128]{2,1,0:T(8,128)S(1)} custom-call(s32[4]{0:T(128)S(1)} %pad_add_fusion.where_ref, f32[8,136,128]{2,1,0:T(8,128)S(1)} %all_to_all.16.slabs_ref), custom_call_target="tpu_custom_call" | custom-call | tf_op jit(solution)/shard_map/inverse_root/pallas_call | solution.py:170
  114.3 25.7 %all_to_all.17 = f32[32,8,128]{2,1,0:T(8,128)S(1)} all-to-all(f32[32,8,128]{2,1,0:T(8,128)S(1)} %inverse_root.1), channel_id=1, replica_groups=mesh['z_lo'=2,'core'=2,'z_hi'=4,'x'=4,'y'=4] {'core','z_hi','x'}, dimensions={0} | all-to-all | bytes 262144 | tf_op jit(solution)/shard_map/all_to_all | solution.py:230
  (84 shorter events, 16.2 us)
Async XLA Ops:
  6.1 16.0 %collective-permute-start.8 = (f32[4352,128]{1,0:T(8,128)S(1)}, f32[4352,128]{1,0:T(8,128)}, u32[]{:S(2)}, u32[]{:S(2)}) collective-permute-start(f32[4352,128]{1,0:T(8,128)S(1)} %get-tuple-element.16), channel_id=1, source_target_pairs={{0,64},{64,0},{1,65},{65,1},{2,66},{66,2},{3,67},{67,3},{4,68},{68... | collective-permute-start | bytes 6684680 | tf_op jit(solution)/shard_map/ppermute | solution.py:201
  15.4 13.6 %collective-permute-start.4 = (f32[4352,128]{1,0:T(8,128)S(1)}, f32[4352,128]{1,0:T(8,128)}, u32[]{:S(2)}, u32[]{:S(2)}) collective-permute-start(f32[4352,128]{1,0:T(8,128)S(1)} %get-tuple-element.14), channel_id=1, source_target_pairs={{0,64},{64,0},{1,65},{65,1},{2,66},{66,2},{3,67},{67,3},{4,68},{68... | collective-permute-start | bytes 6684680 | tf_op jit(solution)/shard_map/ppermute | solution.py:201
  21.5 13.2 %collective-permute-start = (f32[4352,128]{1,0:T(8,128)S(1)}, f32[4352,128]{1,0:T(8,128)S(1)}, u32[]{:S(2)}, u32[]{:S(2)}) collective-permute-start(f32[4352,128]{1,0:T(8,128)S(1)} %get-tuple-element.12), channel_id=1, source_target_pairs={{0,64},{64,0},{1,65},{65,1},{2,66},{66,2},{3,67},{67,3},{4,68},{68... | collective-permute-start | bytes 6684680 | tf_op jit(solution)/shard_map/ppermute | solution.py:201
  23.2 13.6 %collective-permute-start.9 = (f32[1024,128]{1,0:T(8,128)S(1)}, f32[1024,128]{1,0:T(8,128)S(1)}, u32[]{:S(2)}, u32[]{:S(2)}) collective-permute-start(f32[1024,128]{1,0:T(8,128)S(1)} %slice_add_fusion.6), channel_id=1, source_target_pairs={{0,128},{128,0},{1,129},{129,1},{2,130},{130,2},{3,131},{131,3},{4... | collective-permute-start | bytes 1572872 | tf_op jit(solution)/shard_map/ppermute | solution.py:186
  24.4 22.8 %collective-permute-start.20 = (f32[1152,128]{1,0:T(8,128)S(1)}, f32[1152,128]{1,0:T(8,128)S(1)}, u32[]{:S(2)}, u32[]{:S(2)}) collective-permute-start(f32[1152,128]{1,0:T(8,128)S(1)} %slice_add_fusion), channel_id=1, source_target_pairs={{128,16},{16,128},{144,32},{32,144},{160,48},{48,160},{176,0},{0,1... | collective-permute-start | bytes 1769480 | tf_op jit(solution)/shard_map/ppermute | solution.py:190
  30.2 13.0 %collective-permute-start.5 = (f32[1024,128]{1,0:T(8,128)S(1)}, f32[1024,128]{1,0:T(8,128)S(1)}, u32[]{:S(2)}, u32[]{:S(2)}) collective-permute-start(f32[1024,128]{1,0:T(8,128)S(1)} %slice_add_fusion.8), channel_id=1, source_target_pairs={{0,1},{1,0},{2,3},{3,2},{4,5},{5,4},{6,7},{7,6},{8,9},{9,8},{10,11... | collective-permute-start | bytes 1572872 | tf_op jit(solution)/shard_map/ppermute | solution.py:184
  32.7 16.3 %collective-permute-start.17 = (f32[1152,128]{1,0:T(8,128)S(1)}, f32[1152,128]{1,0:T(8,128)S(1)}, u32[]{:S(2)}, u32[]{:S(2)}) collective-permute-start(f32[1152,128]{1,0:T(8,128)S(1)} %slice_add_fusion.2), channel_id=1, source_target_pairs={{0,3},{1,2},{2,1},{3,0},{4,7},{5,6},{6,5},{7,4},{8,11},{9,10},{10,... | collective-permute-start | bytes 1769480 | tf_op jit(solution)/shard_map/ppermute | solution.py:184
  34.8 12.4 %collective-permute-start.1 = (f32[1024,128]{1,0:T(8,128)S(1)}, f32[1024,128]{1,0:T(8,128)S(1)}, u32[]{:S(2)}, u32[]{:S(2)}) collective-permute-start(f32[1024,128]{1,0:T(8,128)S(1)} %slice_add_fusion.10), channel_id=1, source_target_pairs={{0,4},{4,0},{8,12},{12,8},{1,5},{5,1},{9,13},{13,9},{2,6},{6,2},{1... | collective-permute-start | bytes 1572872 | tf_op jit(solution)/shard_map/ppermute | solution.py:184
  36.8 15.9 %collective-permute-start.14 = (f32[1152,128]{1,0:T(8,128)S(1)}, f32[1152,128]{1,0:T(8,128)S(1)}, u32[]{:S(2)}, u32[]{:S(2)}) collective-permute-start(f32[1152,128]{1,0:T(8,128)S(1)} %slice_add_fusion.4), channel_id=1, source_target_pairs={{0,12},{4,8},{8,4},{12,0},{1,13},{5,9},{9,5},{13,1},{2,14},{6,10},... | collective-permute-start | bytes 1769480 | tf_op jit(solution)/shard_map/ppermute | solution.py:184
  43.1 12.8 %collective-permute-start.10 = (f32[512,128]{1,0:T(8,128)S(1)}, f32[512,128]{1,0:T(8,128)S(1)}, u32[]{:S(2)}, u32[]{:S(2)}) collective-permute-start(f32[512,128]{1,0:T(8,128)S(1)} %slice.247), channel_id=1, source_target_pairs={{0,4},{4,0},{8,12},{12,8},{1,5},{5,1},{9,13},{13,9},{2,6},{6,2},{1... | collective-permute-start | bytes 786440 | tf_op jit(solution)/shard_map/ppermute | solution.py:184
  47.1 11.9 %collective-permute-start.6 = (f32[512,128]{1,0:T(8,128)S(1)}, f32[512,128]{1,0:T(8,128)S(1)}, u32[]{:S(2)}, u32[]{:S(2)}) collective-permute-start(f32[512,128]{1,0:T(8,128)S(1)} %slice.241), channel_id=1, source_target_pairs={{0,128},{128,0},{1,129},{129,1},{2,130},{130,2},{3,131},{131,3},{4... | collective-permute-start | bytes 786440 | tf_op jit(solution)/shard_map/ppermute | solution.py:186
  47.2 11.9 %collective-permute-start.2 = (f32[512,128]{1,0:T(8,128)S(1)}, f32[512,128]{1,0:T(8,128)S(1)}, u32[]{:S(2)}, u32[]{:S(2)}) collective-permute-start(f32[512,128]{1,0:T(8,128)S(1)} %slice.235), channel_id=1, source_target_pairs={{0,1},{1,0},{2,3},{3,2},{4,5},{5,4},{6,7},{7,6},{8,9},{9,8},{10,11... | collective-permute-start | bytes 786440 | tf_op jit(solution)/shard_map/ppermute | solution.py:184
  48.9 10.4 %collective-permute-start.21 = (f32[576,128]{1,0:T(8,128)S(1)}, f32[576,128]{1,0:T(8,128)S(1)}, u32[]{:S(2)}, u32[]{:S(2)}) collective-permute-start(f32[576,128]{1,0:T(8,128)S(1)} %slice.269), channel_id=1, source_target_pairs={{0,12},{4,8},{8,4},{12,0},{1,13},{5,9},{9,5},{13,1},{2,14},{6,10},... | collective-permute-start | bytes 884744 | tf_op jit(solution)/shard_map/ppermute | solution.py:184
  52.7 7.5 %collective-permute-start.18 = (f32[576,128]{1,0:T(8,128)S(1)}, f32[576,128]{1,0:T(8,128)S(1)}, u32[]{:S(2)}, u32[]{:S(2)}) collective-permute-start(f32[576,128]{1,0:T(8,128)S(1)} %slice.263), channel_id=1, source_target_pairs={{128,16},{16,128},{144,32},{32,144},{160,48},{48,160},{176,0},{0,1... | collective-permute-start | bytes 884744 | tf_op jit(solution)/shard_map/ppermute | solution.py:190
  55.9 7.4 %collective-permute-start.15 = (f32[576,128]{1,0:T(8,128)S(1)}, f32[576,128]{1,0:T(8,128)S(1)}, u32[]{:S(2)}, u32[]{:S(2)}) collective-permute-start(f32[576,128]{1,0:T(8,128)S(1)} %slice.257), channel_id=1, source_target_pairs={{0,3},{1,2},{2,1},{3,0},{4,7},{5,6},{6,5},{7,4},{8,11},{9,10},{10,... | collective-permute-start | bytes 884744 | tf_op jit(solution)/shard_map/ppermute | solution.py:184
  59.0 6.9 %collective-permute-start.11 = (f32[256,128]{1,0:T(8,128)S(1)}, f32[256,128]{1,0:T(8,128)S(1)}, u32[]{:S(2)}, u32[]{:S(2)}) collective-permute-start(f32[256,128]{1,0:T(8,128)S(1)} %slice.249), channel_id=1, source_target_pairs={{0,1},{1,0},{2,3},{3,2},{4,5},{5,4},{6,7},{7,6},{8,9},{9,8},{10,11... | collective-permute-start | bytes 393224 | tf_op jit(solution)/shard_map/ppermute | solution.py:184
  59.2 9.5 %collective-permute-start.7 = (f32[256,128]{1,0:T(8,128)S(1)}, f32[256,128]{1,0:T(8,128)S(1)}, u32[]{:S(2)}, u32[]{:S(2)}) collective-permute-start(f32[256,128]{1,0:T(8,128)S(1)} %slice.243), channel_id=1, source_target_pairs={{0,4},{4,0},{8,12},{12,8},{1,5},{5,1},{9,13},{13,9},{2,6},{6,2},{1... | collective-permute-start | bytes 393224 | tf_op jit(solution)/shard_map/ppermute | solution.py:184
  59.3 9.4 %collective-permute-start.3 = (f32[256,128]{1,0:T(8,128)S(1)}, f32[256,128]{1,0:T(8,128)S(1)}, u32[]{:S(2)}, u32[]{:S(2)}) collective-permute-start(f32[256,128]{1,0:T(8,128)S(1)} %slice.237), channel_id=1, source_target_pairs={{0,128},{128,0},{1,129},{129,1},{2,130},{130,2},{3,131},{131,3},{4... | collective-permute-start | bytes 393224 | tf_op jit(solution)/shard_map/ppermute | solution.py:186
  60.2 8.9 %collective-permute-start.22 = (f32[288,128]{1,0:T(8,128)S(1)}, f32[288,128]{1,0:T(8,128)S(1)}, u32[]{:S(2)}, u32[]{:S(2)}) collective-permute-start(f32[288,128]{1,0:T(8,128)S(1)} %slice.271), channel_id=1, source_target_pairs={{0,3},{1,2},{2,1},{3,0},{4,7},{5,6},{6,5},{7,4},{8,11},{9,10},{10,... | collective-permute-start | bytes 442376 | tf_op jit(solution)/shard_map/ppermute | solution.py:184
  63.3 5.8 %collective-permute-start.19 = (f32[288,128]{1,0:T(8,128)S(1)}, f32[288,128]{1,0:T(8,128)S(1)}, u32[]{:S(2)}, u32[]{:S(2)}) collective-permute-start(f32[288,128]{1,0:T(8,128)S(1)} %slice.265), channel_id=1, source_target_pairs={{0,12},{4,8},{8,4},{12,0},{1,13},{5,9},{9,5},{13,1},{2,14},{6,10},... | collective-permute-start | bytes 442376 | tf_op jit(solution)/shard_map/ppermute | solution.py:184
  65.9 5.3 %collective-permute-start.16 = (f32[288,128]{1,0:T(8,128)S(1)}, f32[288,128]{1,0:T(8,128)S(1)}, u32[]{:S(2)}, u32[]{:S(2)}) collective-permute-start(f32[288,128]{1,0:T(8,128)S(1)} %slice.259), channel_id=1, source_target_pairs={{128,16},{16,128},{144,32},{32,144},{160,48},{48,160},{176,0},{0,1... | collective-permute-start | bytes 442376 | tf_op jit(solution)/shard_map/ppermute | solution.py:190
  68.8 7.6 %collective-permute-start.12 = (f32[3,128,128]{2,1,0:T(8,128)S(1)}, f32[3,128,128]{2,1,0:T(8,128)S(1)}, u32[]{:S(2)}, u32[]{:S(2)}) collective-permute-start(f32[3,128,128]{2,1,0:T(8,128)S(1)} %slice.251), channel_id=1, source_target_pairs={{0,12},{4,8},{8,4},{12,0},{1,13},{5,9},{9,5},{13,1},{2,14},{6,10},... | collective-permute-start | bytes 589832 | tf_op jit(solution)/shard_map/ppermute | solution.py:184
  71.3 5.3 %collective-permute-start.23 = (f32[3,144,128]{2,1,0:T(8,128)S(1)}, f32[3,144,128]{2,1,0:T(8,128)S(1)}, u32[]{:S(2)}, u32[]{:S(2)}) collective-permute-start(f32[3,144,128]{2,1,0:T(8,128)S(1)} %slice.273), channel_id=1, source_target_pairs={{0,4},{4,0},{8,12},{12,8},{1,5},{5,1},{9,13},{13,9},{2,6},{6,2},{1... | collective-permute-start | bytes 663560 | tf_op jit(solution)/shard_map/ppermute | solution.py:184
  76.4 4.8 %collective-permute-start.13 = (f32[3,64,128]{2,1,0:T(8,128)S(1)}, f32[3,64,128]{2,1,0:T(8,128)S(1)}, u32[]{:S(2)}, u32[]{:S(2)}) collective-permute-start(f32[3,64,128]{2,1,0:T(8,128)S(1)} %slice.253), channel_id=1, source_target_pairs={{0,3},{1,2},{2,1},{3,0},{4,7},{5,6},{6,5},{7,4},{8,11},{9,10},{10,... | collective-permute-start | bytes 294920 | tf_op jit(solution)/shard_map/ppermute | solution.py:184
  (1 other events, 4.6 us)

commit v2 on v1

v2 whole, which is shorter than its diff:
```python
import functools

import jax
import jax.numpy as jnp
from jax import lax
from jax.experimental import pallas as pl
from jax.experimental.pallas import tpu as pltpu
from jax.sharding import Mesh
from jax.sharding import PartitionSpec as P

ITERS = 4
SLABS = 8
UNIT = 136
LANES = (
    (("x1", "y1", "z", "x2", "y2"), False, ((0, 0, 88),)),
    (("x2", "y2", "z", "x1", "y1"), True, ((0, 88, 48), (1, 0, 40))),
    (("y1", "z", "x1", "x2", "y2"), False, ((1, 40, 80),)),
    (("y2", "z", "x2", "x1", "y1"), True, ((1, 120, 16), (2, 0, 64))),
    (("z", "x1", "y1", "x2", "y2"), False, ((2, 64, 72),)),
)
MIB = 1024 * 1024


def pieces_of(part):
    found, base = [], 0
    for lane, (_, _, pieces) in enumerate(LANES):
        for piece in pieces:
            if piece[0] == part:
                found.append((lane, base, piece[1], piece[2]))
                base += 32 * piece[2]
    return found


def place(order, flags):
    at = 0
    for name in order:
        at = at * 2 + flags[name]
    return at


def gram_kernel(part, where_ref, grads_ref, own_ref, away_ref):
    pieces = pieces_of(part)
    col_x, row_y, low_z, core = where_ref[0], where_ref[1], where_ref[2], where_ref[3]
    half = grads_ref.shape[-1] // 2
    slab_rows = half // SLABS
    rows = lax.broadcasted_iota(jnp.int32, (half, half), 0)
    cols = lax.broadcasted_iota(jnp.int32, (half, half), 1)
    upper = rows <= cols
    line_rows = lax.broadcasted_iota(jnp.int32, (slab_rows, 128), 0)
    line_cols = lax.broadcasted_iota(jnp.int32, (slab_rows, 128), 1)
    mult = functools.partial(jnp.dot, preferred_element_type=jnp.float32)
    spots = []
    for slab in range(SLABS):
        from_y = lax.bitwise_xor(row_y, slab // 2)
        high = lax.shift_right_logical(from_y, 1)
        flags = {
            "x1": 0,
            "x2": 0,
            "y1": lax.bitwise_xor(lax.bitwise_and(from_y, 1), high),
            "y2": high,
            "z": lax.bitwise_xor(low_z, slab % 2),
        }
        spots.append([place(LANES[lane][0], flags) for lane, _, _, _ in pieces])

    for step in range(4):
        relative = (step & 1) ^ (3 * (step >> 1))
        block = grads_ref[lax.bitwise_xor(col_x, relative)]
        flipped = block.T
        first = jnp.where(core == 0, block, flipped)
        second = jnp.where(core == 0, flipped, block)
        flags = {"x1": step & 1, "x2": step >> 1, "y1": 0, "y2": 0, "z": 0}
        bases = [base + place(LANES[lane][0], flags) * size for lane, base, _, size in pieces]
        for lhs, rhs, out_ref in ((second, first, away_ref), (first, second, own_ref)):
            corner = mult(lhs[:half], rhs[:, :half])
            right = mult(lhs, rhs[:, half:])
            cross, last = right[:half], right[half:]
            fold = jnp.where(upper, corner, last)
            for slab in range(SLABS):
                mine = slice(slab * slab_rows, (slab + 1) * slab_rows)
                near = slab * slab_rows // 128 * 128
                square = last[mine, near : near + 128]
                line = jnp.sum(
                    jnp.where(line_cols - line_rows == slab * slab_rows - near, square, 0.0), axis=0, keepdims=True
                )
                content = (
                    cross[mine, :128],
                    cross[mine, 128:],
                    fold[mine, :128],
                    fold[mine, 128:],
                    jnp.broadcast_to(line, (8, 128)),
                )
                for spot, base, (_, _, first_row, size) in zip(spots[slab], bases, pieces):
                    start = pl.multiple_of(spot * size + base, 8)
                    for band, value in enumerate(content):
                        low = max(band * slab_rows, first_row)
                        top = min(band * slab_rows + value.shape[0], first_row + size)
                        if low < top:
                            cut = value[low - band * slab_rows : top - band * slab_rows]
                            out_ref[pl.ds(start + low - first_row, top - low), :] = cut


def gram(part, where, grads):
    shape = jax.ShapeDtypeStruct((32 * UNIT, 128), jnp.float32)
    whole = pl.BlockSpec(memory_space=pltpu.VMEM)
    return pl.pallas_call(
        functools.partial(gram_kernel, part),
        out_shape=(shape, shape),
        in_specs=[pl.BlockSpec(memory_space=pltpu.SMEM), whole],
        out_specs=(whole, whole),
        compiler_params=pltpu.CompilerParams(vmem_limit_bytes=16 * MIB),
        name=f"gram_{part}",
    )(where, grads)


def split(value):
    high = value.astype(jnp.bfloat16)
    return high, (value - high.astype(jnp.float32)).astype(jnp.bfloat16)


def product(left, right):
    mult = functools.partial(jnp.dot, preferred_element_type=jnp.float32)
    return mult(left[0], right[0]) + (mult(left[0], right[1]) + mult(left[1], right[0]))


def root_kernel(factor, where_ref, slabs_ref, out_ref, full, picked):
    half = 256
    order = 2 * half
    slab_rows = half // SLABS
    rows = lax.broadcasted_iota(jnp.int32, (half, half), 0)
    cols = lax.broadcasted_iota(jnp.int32, (half, half), 1)

    def gathered(first):
        left = jnp.concatenate([slabs_ref[s, first : first + slab_rows] for s in range(SLABS)], axis=0)
        right = jnp.concatenate(
            [slabs_ref[s, first + slab_rows : first + 2 * slab_rows] for s in range(SLABS)], axis=0
        )
        return jnp.concatenate([left, right], axis=1) * factor

    cross = gathered(0)
    fold = gathered(64)
    line = jnp.concatenate(
        [sum(slabs_ref[s, 128:129] for s in group) for group in (range(4), range(4, 8))], axis=1
    )
    turned = fold.T
    corner = jnp.where(rows <= cols, fold, turned)
    last = jnp.where(rows > cols, fold, jnp.where(rows == cols, line * factor, turned))
    matrix = jnp.concatenate(
        [jnp.concatenate([corner, cross], axis=1), jnp.concatenate([cross.T, last], axis=1)], axis=0
    )
    total = jnp.sum(jnp.sum(matrix * matrix, axis=0, keepdims=True), axis=1, keepdims=True)
    scaling = 2.5 / jnp.sqrt(total)
    coupled = scaling * matrix
    identity = (
        lax.broadcasted_iota(jnp.int32, (order, order), 0) == lax.broadcasted_iota(jnp.int32, (order, order), 1)
    ).astype(jnp.float32)
    row_y, low_z = where_ref[1], where_ref[2]

    def mine(value):
        return jnp.where(low_z == 0, value[:, :half], value[:, half:])

    iterate = None
    for sweep in range(ITERS):
        step_matrix = (5.0 * identity - coupled) * 0.25
        if sweep == 0:
            full[...] = jnp.sqrt(jnp.sqrt(scaling)) * step_matrix
            for chunk in range(16):
                start = pl.multiple_of(32 * chunk + 8 * row_y, 8)
                picked[8 * chunk : 8 * chunk + 8, :] = full[pl.ds(start, 8), :]
            iterate = picked[...]
        else:
            iterate = product(split(iterate), split(step_matrix))
        if sweep < ITERS - 1:
            parts = split(step_matrix)
            squared = split(product(parts, parts))
            fourth = split(product(squared, squared))
            if sweep == ITERS - 2:
                coupled, identity = mine(coupled), mine(identity)
            coupled = product(fourth, split(coupled))
    for core in range(2):
        out_ref[16 * core : 16 * core + 16] = iterate[:, 128 * core : 128 * core + 128].reshape(16, 8, 128)


def inverse_root(where, slabs, factor):
    return pl.pallas_call(
        functools.partial(root_kernel, factor),
        out_shape=jax.ShapeDtypeStruct((32, 8, 128), jnp.float32),
        in_specs=[pl.BlockSpec(memory_space=pltpu.SMEM), pl.BlockSpec(memory_space=pltpu.VMEM)],
        out_specs=pl.BlockSpec(memory_space=pltpu.VMEM),
        scratch_shapes=[pltpu.VMEM((512, 512), jnp.float32), pltpu.VMEM((128, 512), jnp.float32)],
        compiler_params=pltpu.CompilerParams(vmem_limit_bytes=24 * MIB),
        name="inverse_root",
    )(where, slabs)


def swap(value, name, odd):
    if name in ("x1", "x2", "y1", "y2"):
        flip = 1 if name[1] == "1" else 3
        return lax.ppermute(value, name[0], [(i, i ^ flip) for i in range(4)])
    if not odd:
        return lax.ppermute(value, "z_lo", [(0, 1), (1, 0)])
    pairs = []
    for high in range(4):
        pairs += [(4 + high, (high + 1) % 4), ((high + 1) % 4, 4 + high)]
    return lax.ppermute(value, ("z_lo", "z_hi"), pairs)


def body(grads):
    local_grads = grads[0]
    order = local_grads.shape[1]
    where = jnp.stack([lax.axis_index(name).astype(jnp.int32) for name in ("x", "y", "z_lo", "core")])
    factor = 1.0 / (256 * order)
    waiting = local_grads
    kept, sent = [[] for _ in LANES], [[] for _ in LANES]
    for part in range(3):
        own, away = gram(part, where, waiting[4 * part : 4 * part + 4])
        waiting, away = lax.optimization_barrier((waiting, away))
        came = lax.ppermute(away, "core", [(0, 1), (1, 0)])
        for lane, base, _, size in pieces_of(part):
            for halves, first in ((kept, base), (sent, base + 16 * size)):
                rows = slice(first, first + 16 * size)
                halves[lane].append((own[rows] + came[rows]).reshape(16, size, 128))
    done = [[], []]
    for (order, odd, _), keep, send in zip(LANES, kept, sent):
        keep, send = (half[0] if len(half) == 1 else jnp.concatenate(half, axis=1) for half in (keep, send))
        for step in range(3):
            summed = keep + swap(send, order[step], odd)
            middle = summed.shape[0] // 2
            keep, send = summed[:middle], summed[middle:]
        done[odd].append(summed)
    even, odd = (jnp.concatenate(lanes, axis=1) for lanes in done)
    for along in ("x", "y"):
        middle = even.shape[0] // 2
        even_keep, odd_keep, even_send, odd_send = lax.optimization_barrier(
            (even[:middle], odd[:middle], even[middle:], odd[middle:])
        )
        even_came, odd_came = lax.optimization_barrier(
            (swap(even_send, along + "2", False), swap(odd_send, along + "1", True))
        )
        even, odd = even_keep + even_came, odd_keep + odd_came
    even, odd = even[0], odd[0]
    held = {}
    for lanes, total in ((LANES[0::2], even), (LANES[1::2], odd)):
        first = 0
        for _, _, pieces in lanes:
            for piece in pieces:
                held[piece[:2]] = total[first : first + piece[2]]
                first += piece[2]
    parts = [jnp.concatenate([held[key] for key in sorted(held) if key[0] == part]) for part in range(3)]
    parts = jnp.stack(parts + parts[:1])
    high_z = lax.axis_index("z_hi")
    pick = [lax.dynamic_index_in_dim(parts, lax.bitwise_xor(high_z, k), 0, False) for k in range(4)]
    slab = pick[0] + sum(lax.ppermute(pick[k], "z_hi", [(i, i ^ k) for i in range(4)]) for k in (2, 1, 3))
    slabs = lax.all_to_all(
        jnp.broadcast_to(slab[None], (SLABS, UNIT, 128)), ("y", "z_lo"), 0, 0, tiled=True
    )
    pieces = inverse_root(where, slabs, factor)
    arrived = lax.all_to_all(pieces, ("core", "z_hi", "x"), 0, 0, tiled=True)
    return arrived.reshape(2, 16, 8, 128)[:, :12]


def solution(mesh):
    axes = ("z_lo", "core", "z_hi", "x", "y")
    fine = Mesh(mesh.devices.reshape(2, 2, 4, 4, 4), axes)
    return jax.shard_map(
        body,
        mesh=fine,
        in_specs=(P(axes, None, None, None),),
        out_specs=P(None, None, ("z_hi", "x", "y"), ("z_lo", "core")),
        check_vma=False,
    )
```

time: 141 us -> 129 us (0.915)
  waiting for transfers between devices: 19.3 us -> 33.1 us
  blocking collectives: 48.8 us -> 37.2 us
  Pallas kernels: 27.8 us -> 17.5 us
  other arithmetic: 9.86 us -> 1.86 us
  starting transfers between devices: 33.4 us -> 35.8 us
  local copies, waits for them, and re-layouts: 0.92 us -> 3.14 us
    all_to_all x1 -> x0, blocking collectives: 12.8 us -> none  [body(): slab = jnp.sum(lax.all_to_all(parts, 'z_hi', 0, 0, tiled=True), axis=0)]
    ppermute x3, waiting for transfers between devices: 0.75 us -> 11.4 us  [swap(): return lax.ppermute(value, 'z_lo', [(0, 1), (1, 0)])]
    pallas_call x3, Pallas kernels: 18 us -> 7.77 us  [gram(): pl.pallas_call(functools.partial(gram_kernel, part), out_shape=(shape, sh...]
    add x22 -> x27, other arithmetic: 9.58 us -> 1.58 us  [the longest x15 0.76 us: body(): summed = keep + swap(send, order[step], odd)]
    ppermute x0 -> x3, starting transfers between devices: none -> 5.74 us  [body(): lax.ppermute(pick[k], 'z_hi', [(i, i ^ k) for i in range(4)])]
    ppermute x16 -> x14, waiting for transfers between devices: 15.8 us -> 11 us  [swap(): return lax.ppermute(value, name[0], [(i, i ^ flip) for i in range(4)])]
    ppermute x0 -> x3, waiting for transfers between devices: none -> 4.49 us  [body(): lax.ppermute(pick[k], 'z_hi', [(i, i ^ k) for i in range(4)])]
    ppermute x3 -> x2, starting transfers between devices: 10.4 us -> 6.2 us  [swap(): return lax.ppermute(value, ('z_lo', 'z_hi'), pairs)]
  transfers between devices with their start and end apart: 25 -> 25, of which waited for: 8 -> 12; matrix products, arithmetic and copies ran while one was open for 7% -> 2% of each run, Pallas kernels for 9% -> 4%
where the time goes in v2:
time: 129 us
  blocking collectives  37.2 us (29%)
  starting transfers between devices  35.8 us (28%)
  waiting for transfers between devices  33.1 us (26%)
  Pallas kernels  17.5 us (14%)
  local copies, waits for them, and re-layouts  3.14 us (2%)
  other arithmetic  1.86 us (1%)
    all_to_all x1, blocking collectives, body(): arrived = lax.all_to_all(pieces, ('core', 'z_hi', 'x'), 0, 0, tiled=True)  26.6 us
    ppermute x14, starting transfers between devices, swap(): return lax.ppermute(value, name[0], [(i, i ^ flip) for i in range(4)])  18.5 us
    ppermute x3, waiting for transfers between devices, swap(): return lax.ppermute(value, 'z_lo', [(0, 1), (1, 0)])  11.4 us
    ppermute x14, waiting for transfers between devices, swap(): return lax.ppermute(value, name[0], [(i, i ^ flip) for i in range(4)])  11 us
    all_to_all x1, blocking collectives, body(): lax.all_to_all(jnp.broadcast_to(slab[None], (SLABS, UNIT, 128)), ('y', 'z...  10.6 us
    pallas_call x1, Pallas kernels, inverse_root(): pl.pallas_call(functools.partial(root_kernel, factor), out_shape=jax.Shap...  9.76 us
    pallas_call x3, Pallas kernels, gram(): pl.pallas_call(functools.partial(gram_kernel, part), out_shape=(shape, sh...  7.77 us
    ppermute x2, starting transfers between devices, swap(): return lax.ppermute(value, ('z_lo', 'z_hi'), pairs)  6.2 us
  transfers between devices with their start and end apart: 25, of which 12 were waited for; matrix products, arithmetic and copies ran while one was open for 2% of the time, Pallas kernels for 4%

profile of v2, /device:TPU:1, one launch (start us, length us, event | category | flops | bytes accessed | tf_op | source)
XLA Modules:
  0.0 129.1 jit_solution(3214091683413496806)
XLA Ops:
  0.0 1.9 %slice_bitcast_fusion.grads_ref = bf16[4,512,512]{2,1,0:T(8,128)(2,1)S(1)} fusion(bf16[1,12,512,512]{3,2,1,0:T(8,128)(2,1)} %param.1), kind=kLoop, calls=%fused_computation | loop fusion | bytes 4194304 | tf_op jit(solution)/shard_map/slice | solution.py:215
  2.0 2.6 %gram_0.1 = (f32[4352,128]{1,0:T(8,128)S(1)}, f32[4352,128]{1,0:T(8,128)S(1)}) custom-call(s32[4]{0:T(128)S(1)} %pad_add_fusion.where_ref, bf16[4,512,512]{2,1,0:T(8,128)(2,1)S(1)} %slice_bitcast_fusion.grads_ref), custom_call_target="tpu_custom_call" | custom-call | tf_op jit(solution)/shard_map/gram_0/pallas_call | solution.py:105
  4.6 3.3 %collective-permute-start = (f32[4352,128]{1,0:T(8,128)S(1)}, f32[4352,128]{1,0:T(8,128)S(1)}, u32[]{:S(2)}, u32[]{:S(2)}) collective-permute-start(f32[4352,128]{1,0:T(8,128)S(1)} %get-tuple-element.30), channel_id=1, source_target_pairs={{0,64},{64,0},{1,65},{65,1},{2,66},{66,2},{3,67},{67,3},{4,68},{68... | collective-permute-start | bytes 6684680 | tf_op jit(solution)/shard_map/ppermute | solution.py:217
  8.0 2.6 %gram_1.1 = (f32[4352,128]{1,0:T(8,128)S(1)}, f32[4352,128]{1,0:T(8,128)S(1)}) custom-call(s32[4]{0:T(128)S(1)} %pad_add_fusion.where_ref, bf16[4,512,512]{2,1,0:T(8,128)(2,1)S(1)} %slice.235.grads_ref), custom_call_target="tpu_custom_call" | custom-call | tf_op jit(solution)/shard_map/gram_1/pallas_call | solution.py:105
  10.9 2.6 %gram_2.1 = (f32[4352,128]{1,0:T(8,128)S(1)}, f32[4352,128]{1,0:T(8,128)S(1)}) custom-call(s32[4]{0:T(128)S(1)} %pad_add_fusion.where_ref, bf16[4,512,512]{2,1,0:T(8,128)(2,1)S(1)} %slice.244.grads_ref), custom_call_target="tpu_custom_call" | custom-call | tf_op jit(solution)/shard_map/gram_2/pallas_call | solution.py:105
  15.3 3.0 %collective-permute-done.8 = f32[4352,128]{1,0:T(8,128)S(1)} collective-permute-done((f32[4352,128]{1,0:T(8,128)S(1)}, f32[4352,128]{1,0:T(8,128)S(1)}, u32[]{:S(2)}, u32[]{:S(2)}) %collective-permute-start.8) | collective-permute-done | bytes 2228256 | tf_op jit(solution)/shard_map/ppermute | solution.py:217
  18.7 2.7 %collective-permute-start.15 = (f32[16,80,128]{2,1,0:T(8,128)S(1)}, f32[16,80,128]{2,1,0:T(8,128)S(1)}, u32[]{:S(2)}, u32[]{:S(2)}) collective-permute-start(f32[16,80,128]{2,1,0:T(8,128)S(1)} %pad_maximum_fusion.1), channel_id=1, source_target_pairs={{0,3},{1,2},{2,1},{3,0},{4,7},{5,6},{6,5},{7,4},{8,11},{9,10},{10,... | collective-permute-start | bytes 1966088 | tf_op jit(solution)/shard_map/ppermute | solution.py:198
  21.6 2.6 %collective-permute-start.12 = (f32[16,88,128]{2,1,0:T(8,128)S(1)}, f32[16,88,128]{2,1,0:T(8,128)S(1)}, u32[]{:S(2)}, u32[]{:S(2)}) collective-permute-start(f32[16,88,128]{2,1,0:T(8,128)S(1)} %pad_maximum_fusion), channel_id=1, source_target_pairs={{0,12},{4,8},{8,4},{12,0},{1,13},{5,9},{9,5},{13,1},{2,14},{6,10},... | collective-permute-start | bytes 2162696 | tf_op jit(solution)/shard_map/ppermute | solution.py:198
  24.2 8.8 %collective-permute-done.9 = f32[16,72,128]{2,1,0:T(8,128)S(1)} collective-permute-done((f32[16,72,128]{2,1,0:T(8,128)S(1)}, f32[16,72,128]{2,1,0:T(8,128)S(1)}, u32[]{:S(2)}, u32[]{:S(2)}) %collective-permute-start.9) | collective-permute-done | bytes 589856 | tf_op jit(solution)/shard_map/ppermute | solution.py:200
  35.9 4.6 %collective-permute-start.16 = (f32[8,80,128]{2,1,0:T(8,128)S(1)}, f32[8,80,128]{2,1,0:T(8,128)S(1)}, u32[]{:S(2)}, u32[]{:S(2)}) collective-permute-start(f32[8,80,128]{2,1,0:T(8,128)S(1)} %slice.332), channel_id=1, source_target_pairs={{128,16},{16,128},{144,32},{32,144},{160,48},{48,160},{176,0},{0,1... | collective-permute-start | bytes 983048 | tf_op jit(solution)/shard_map/ppermute | solution.py:204
  41.2 2.3 %collective-permute-start.13 = (f32[8,88,128]{2,1,0:T(8,128)S(1)}, f32[8,88,128]{2,1,0:T(8,128)S(1)}, u32[]{:S(2)}, u32[]{:S(2)}) collective-permute-start(f32[8,88,128]{2,1,0:T(8,128)S(1)} %slice.324), channel_id=1, source_target_pairs={{0,3},{1,2},{2,1},{3,0},{4,7},{5,6},{6,5},{7,4},{8,11},{9,10},{10,... | collective-permute-start | bytes 1081352 | tf_op jit(solution)/shard_map/ppermute | solution.py:198
  47.2 2.6 %collective-permute-start.17 = (f32[4,80,128]{2,1,0:T(8,128)S(1)}, f32[4,80,128]{2,1,0:T(8,128)S(1)}, u32[]{:S(2)}, u32[]{:S(2)}) collective-permute-start(f32[4,80,128]{2,1,0:T(8,128)S(1)} %slice.334), channel_id=1, source_target_pairs={{0,12},{4,8},{8,4},{12,0},{1,13},{5,9},{9,5},{13,1},{2,14},{6,10},... | collective-permute-start | bytes 491528 | tf_op jit(solution)/shard_map/ppermute | solution.py:198
  49.7 2.4 %collective-permute-done.11 = f32[4,72,128]{2,1,0:T(8,128)S(1)} collective-permute-done((f32[4,72,128]{2,1,0:T(8,128)S(1)}, f32[4,72,128]{2,1,0:T(8,128)S(1)}, u32[]{:S(2)}, u32[]{:S(2)}) %collective-permute-start.11) | collective-permute-done | bytes 147488 | tf_op jit(solution)/shard_map/ppermute | solution.py:198
  54.0 2.6 %collective-permute-done.3 = f32[4,88,128]{2,1,0:T(8,128)S(1)} collective-permute-done((f32[4,88,128]{2,1,0:T(8,128)S(1)}, f32[4,88,128]{2,1,0:T(8,128)S(1)}, u32[]{:S(2)}, u32[]{:S(2)}) %collective-permute-start.3) | collective-permute-done | bytes 180256 | tf_op jit(solution)/shard_map/ppermute | solution.py:200
  58.1 2.6 %collective-permute-start.18 = (f32[2,240,128]{2,1,0:T(8,128)S(1)}, f32[2,240,128]{2,1,0:T(8,128)S(1)}, u32[]{:S(2)}, u32[]{:S(2)}) collective-permute-start(f32[2,240,128]{2,1,0:T(8,128)S(1)} %get-tuple-element.40), channel_id=1, source_target_pairs={{0,12},{4,8},{8,4},{12,0},{1,13},{5,9},{9,5},{13,1},{2,14},{6,10},... | collective-permute-start | bytes 737288 | tf_op jit(solution)/shard_map/ppermute | solution.py:198
  60.6 4.3 %collective-permute-done.19 = f32[2,168,128]{2,1,0:T(8,128)S(1)} collective-permute-done((f32[2,168,128]{2,1,0:T(8,128)S(1)}, f32[2,168,128]{2,1,0:T(8,128)S(1)}, u32[]{:S(2)}, u32[]{:S(2)}) %collective-permute-start.19) | collective-permute-done | bytes 172064 | tf_op jit(solution)/shard_map/ppermute | solution.py:198
  65.0 2.6 %collective-permute-start.20 = (f32[1,240,128]{2,1,0:T(8,128)S(1)}, f32[1,240,128]{2,1,0:T(8,128)S(1)}, u32[]{:S(2)}, u32[]{:S(2)}) collective-permute-start(f32[1,240,128]{2,1,0:T(8,128)S(1)} %get-tuple-element.46), channel_id=1, source_target_pairs={{0,3},{1,2},{2,1},{3,0},{4,7},{5,6},{6,5},{7,4},{8,11},{9,10},{10,... | collective-permute-start | bytes 368648 | tf_op jit(solution)/shard_map/ppermute | solution.py:198
  67.6 3.3 %collective-permute-done.21 = f32[1,168,128]{2,1,0:T(8,128)S(1)} collective-permute-done((f32[1,168,128]{2,1,0:T(8,128)S(1)}, f32[1,168,128]{2,1,0:T(8,128)S(1)}, u32[]{:S(2)}, u32[]{:S(2)}) %collective-permute-start.21) | collective-permute-done | bytes 86048 | tf_op jit(solution)/shard_map/ppermute | solution.py:198
  72.2 2.1 %collective-permute-start.24 = (f32[136,128]{1,0:T(8,128)S(1)}, f32[136,128]{1,0:T(8,128)S(1)}, u32[]{:S(2)}, u32[]{:S(2)}) collective-permute-start(f32[136,128]{1,0:T(8,128)S(1)} %get-tuple-element.70), channel_id=1, source_target_pairs={{0,48},{16,32},{32,16},{48,0},{1,49},{17,33},{33,17},{49,1},{2,50}... | collective-permute-start | bytes 208904 | tf_op jit(solution)/shard_map/ppermute | solution.py:252
  74.4 2.6 %collective-permute-start.22 = (f32[136,128]{1,0:T(8,128)S(1)}, f32[136,128]{1,0:T(8,128)S(1)}, u32[]{:S(2)}, u32[]{:S(2)}) collective-permute-start(f32[136,128]{1,0:T(8,128)S(1)} %get-tuple-element.71), channel_id=1, source_target_pairs={{0,32},{16,48},{32,0},{48,16},{1,33},{17,49},{33,1},{49,17},{2,34}... | collective-permute-start | bytes 208904 | tf_op jit(solution)/shard_map/ppermute | solution.py:252
  77.6 3.8 %collective-permute-done.22 = f32[136,128]{1,0:T(8,128)S(1)} collective-permute-done((f32[136,128]{1,0:T(8,128)S(1)}, f32[136,128]{1,0:T(8,128)S(1)}, u32[]{:S(2)}, u32[]{:S(2)}) %collective-permute-start.22) | collective-permute-done | bytes 69664 | tf_op jit(solution)/shard_map/ppermute | solution.py:252
  81.5 10.6 %all_to_all.10.slabs_ref = f32[8,136,128]{2,1,0:T(8,128)S(1)} all-to-all(f32[8,136,128]{2,1,0:T(8,128)S(1)} %broadcast_in_dim.2), channel_id=1, replica_groups=mesh['z_lo'=2,'core'=2,'z_hi'=4,'x'=4,'y'=4] {'y','z_lo'}, dimensions={0} | all-to-all | bytes 1114112 | tf_op jit(solution)/shard_map/all_to_all | solution.py:253
  92.1 9.8 %inverse_root.1 = f32[32,8,128]{2,1,0:T(8,128)S(1)} custom-call(s32[4]{0:T(128)S(1)} %pad_add_fusion.where_ref, f32[8,136,128]{2,1,0:T(8,128)S(1)} %all_to_all.10.slabs_ref), custom_call_target="tpu_custom_call" | custom-call | tf_op jit(solution)/shard_map/inverse_root/pallas_call | solution.py:184
  101.9 26.6 %all_to_all.11 = f32[32,8,128]{2,1,0:T(8,128)S(1)} all-to-all(f32[32,8,128]{2,1,0:T(8,128)S(1)} %inverse_root.1), channel_id=1, replica_groups=mesh['z_lo'=2,'core'=2,'z_hi'=4,'x'=4,'y'=4] {'core','z_hi','x'}, dimensions={0} | all-to-all | bytes 262144 | tf_op jit(solution)/shard_map/all_to_all | solution.py:257
  (95 shorter events, 15.9 us)
Async XLA Ops:
  4.6 9.5 %collective-permute-start = (f32[4352,128]{1,0:T(8,128)S(1)}, f32[4352,128]{1,0:T(8,128)S(1)}, u32[]{:S(2)}, u32[]{:S(2)}) collective-permute-start(f32[4352,128]{1,0:T(8,128)S(1)} %get-tuple-element.30), channel_id=1, source_target_pairs={{0,64},{64,0},{1,65},{65,1},{2,66},{66,2},{3,67},{67,3},{4,68},{68... | collective-permute-start | bytes 6684680 | tf_op jit(solution)/shard_map/ppermute | solution.py:217
  10.6 4.4 %collective-permute-start.4 = (f32[4352,128]{1,0:T(8,128)S(1)}, f32[4352,128]{1,0:T(8,128)S(1)}, u32[]{:S(2)}, u32[]{:S(2)}) collective-permute-start(f32[4352,128]{1,0:T(8,128)S(1)} %get-tuple-element.34), channel_id=1, source_target_pairs={{0,64},{64,0},{1,65},{65,1},{2,66},{66,2},{3,67},{67,3},{4,68},{68... | collective-permute-start | bytes 6684680 | tf_op jit(solution)/shard_map/ppermute | solution.py:217
  13.5 4.8 %collective-permute-start.8 = (f32[4352,128]{1,0:T(8,128)S(1)}, f32[4352,128]{1,0:T(8,128)S(1)}, u32[]{:S(2)}, u32[]{:S(2)}) collective-permute-start(f32[4352,128]{1,0:T(8,128)S(1)} %get-tuple-element.38), channel_id=1, source_target_pairs={{0,64},{64,0},{1,65},{65,1},{2,66},{66,2},{3,67},{67,3},{4,68},{68... | collective-permute-start | bytes 6684680 | tf_op jit(solution)/shard_map/ppermute | solution.py:217
  14.2 26.3 %collective-permute-start.1 = (f32[16,88,128]{2,1,0:T(8,128)S(1)}, f32[16,88,128]{2,1,0:T(8,128)S(1)}, u32[]{:S(2)}, u32[]{:S(2)}) collective-permute-start(f32[16,88,128]{2,1,0:T(8,128)S(1)} %bitcast.61), channel_id=1, source_target_pairs={{0,4},{4,0},{8,12},{12,8},{1,5},{5,1},{9,13},{13,9},{2,6},{6,2},{1... | collective-permute-start | bytes 2162696 | tf_op jit(solution)/shard_map/ppermute | solution.py:198
  15.2 18.2 %collective-permute-start.5 = (f32[16,80,128]{2,1,0:T(8,128)S(1)}, f32[16,80,128]{2,1,0:T(8,128)S(1)}, u32[]{:S(2)}, u32[]{:S(2)}) collective-permute-start(f32[16,80,128]{2,1,0:T(8,128)S(1)} %bitcast.62), channel_id=1, source_target_pairs={{0,1},{1,0},{2,3},{3,2},{4,5},{5,4},{6,7},{7,6},{8,9},{9,8},{10,11... | collective-permute-start | bytes 1966088 | tf_op jit(solution)/shard_map/ppermute | solution.py:198
  18.4 14.6 %collective-permute-start.9 = (f32[16,72,128]{2,1,0:T(8,128)S(1)}, f32[16,72,128]{2,1,0:T(8,128)S(1)}, u32[]{:S(2)}, u32[]{:S(2)}) collective-permute-start(f32[16,72,128]{2,1,0:T(8,128)S(1)} %bitcast.63), channel_id=1, source_target_pairs={{0,128},{128,0},{1,129},{129,1},{2,130},{130,2},{3,131},{131,3},{4... | collective-permute-start | bytes 1769480 | tf_op jit(solution)/shard_map/ppermute | solution.py:200
  18.7 17.1 %collective-permute-start.15 = (f32[16,80,128]{2,1,0:T(8,128)S(1)}, f32[16,80,128]{2,1,0:T(8,128)S(1)}, u32[]{:S(2)}, u32[]{:S(2)}) collective-permute-start(f32[16,80,128]{2,1,0:T(8,128)S(1)} %pad_maximum_fusion.1), channel_id=1, source_target_pairs={{0,3},{1,2},{2,1},{3,0},{4,7},{5,6},{6,5},{7,4},{8,11},{9,10},{10,... | collective-permute-start | bytes 1966088 | tf_op jit(solution)/shard_map/ppermute | solution.py:198
  21.6 19.5 %collective-permute-start.12 = (f32[16,88,128]{2,1,0:T(8,128)S(1)}, f32[16,88,128]{2,1,0:T(8,128)S(1)}, u32[]{:S(2)}, u32[]{:S(2)}) collective-permute-start(f32[16,88,128]{2,1,0:T(8,128)S(1)} %pad_maximum_fusion), channel_id=1, source_target_pairs={{0,12},{4,8},{8,4},{12,0},{1,13},{5,9},{9,5},{13,1},{2,14},{6,10},... | collective-permute-start | bytes 2162696 | tf_op jit(solution)/shard_map/ppermute | solution.py:198
  33.1 10.4 %collective-permute-start.10 = (f32[8,72,128]{2,1,0:T(8,128)S(1)}, f32[8,72,128]{2,1,0:T(8,128)S(1)}, u32[]{:S(2)}, u32[]{:S(2)}) collective-permute-start(f32[8,72,128]{2,1,0:T(8,128)S(1)} %slice.315), channel_id=1, source_target_pairs={{0,4},{4,0},{8,12},{12,8},{1,5},{5,1},{9,13},{13,9},{2,6},{6,2},{1... | collective-permute-start | bytes 884744 | tf_op jit(solution)/shard_map/ppermute | solution.py:198
  33.6 11.0 %collective-permute-start.6 = (f32[8,80,128]{2,1,0:T(8,128)S(1)}, f32[8,80,128]{2,1,0:T(8,128)S(1)}, u32[]{:S(2)}, u32[]{:S(2)}) collective-permute-start(f32[8,80,128]{2,1,0:T(8,128)S(1)} %slice.309), channel_id=1, source_target_pairs={{0,128},{128,0},{1,129},{129,1},{2,130},{130,2},{3,131},{131,3},{4... | collective-permute-start | bytes 983048 | tf_op jit(solution)/shard_map/ppermute | solution.py:200
  35.9 11.2 %collective-permute-start.16 = (f32[8,80,128]{2,1,0:T(8,128)S(1)}, f32[8,80,128]{2,1,0:T(8,128)S(1)}, u32[]{:S(2)}, u32[]{:S(2)}) collective-permute-start(f32[8,80,128]{2,1,0:T(8,128)S(1)} %slice.332), channel_id=1, source_target_pairs={{128,16},{16,128},{144,32},{32,144},{160,48},{48,160},{176,0},{0,1... | collective-permute-start | bytes 983048 | tf_op jit(solution)/shard_map/ppermute | solution.py:204
  40.7 11.5 %collective-permute-start.2 = (f32[8,88,128]{2,1,0:T(8,128)S(1)}, f32[8,88,128]{2,1,0:T(8,128)S(1)}, u32[]{:S(2)}, u32[]{:S(2)}) collective-permute-start(f32[8,88,128]{2,1,0:T(8,128)S(1)} %slice.303), channel_id=1, source_target_pairs={{0,1},{1,0},{2,3},{3,2},{4,5},{5,4},{6,7},{7,6},{8,9},{9,8},{10,11... | collective-permute-start | bytes 1081352 | tf_op jit(solution)/shard_map/ppermute | solution.py:198
  41.2 11.1 %collective-permute-start.13 = (f32[8,88,128]{2,1,0:T(8,128)S(1)}, f32[8,88,128]{2,1,0:T(8,128)S(1)}, u32[]{:S(2)}, u32[]{:S(2)}) collective-permute-start(f32[8,88,128]{2,1,0:T(8,128)S(1)} %slice.324), channel_id=1, source_target_pairs={{0,3},{1,2},{2,1},{3,0},{4,7},{5,6},{6,5},{7,4},{8,11},{9,10},{10,... | collective-permute-start | bytes 1081352 | tf_op jit(solution)/shard_map/ppermute | solution.py:198
  43.6 8.5 %collective-permute-start.11 = (f32[4,72,128]{2,1,0:T(8,128)S(1)}, f32[4,72,128]{2,1,0:T(8,128)S(1)}, u32[]{:S(2)}, u32[]{:S(2)}) collective-permute-start(f32[4,72,128]{2,1,0:T(8,128)S(1)} %slice.317), channel_id=1, source_target_pairs={{0,1},{1,0},{2,3},{3,2},{4,5},{5,4},{6,7},{7,6},{8,9},{9,8},{10,11... | collective-permute-start | bytes 442376 | tf_op jit(solution)/shard_map/ppermute | solution.py:198
  44.6 9.3 %collective-permute-start.7 = (f32[4,80,128]{2,1,0:T(8,128)S(1)}, f32[4,80,128]{2,1,0:T(8,128)S(1)}, u32[]{:S(2)}, u32[]{:S(2)}) collective-permute-start(f32[4,80,128]{2,1,0:T(8,128)S(1)} %slice.311), channel_id=1, source_target_pairs={{0,4},{4,0},{8,12},{12,8},{1,5},{5,1},{9,13},{13,9},{2,6},{6,2},{1... | collective-permute-start | bytes 491528 | tf_op jit(solution)/shard_map/ppermute | solution.py:198
  47.2 6.8 %collective-permute-start.17 = (f32[4,80,128]{2,1,0:T(8,128)S(1)}, f32[4,80,128]{2,1,0:T(8,128)S(1)}, u32[]{:S(2)}, u32[]{:S(2)}) collective-permute-start(f32[4,80,128]{2,1,0:T(8,128)S(1)} %slice.334), channel_id=1, source_target_pairs={{0,12},{4,8},{8,4},{12,0},{1,13},{5,9},{9,5},{13,1},{2,14},{6,10},... | collective-permute-start | bytes 491528 | tf_op jit(solution)/shard_map/ppermute | solution.py:198
  52.2 4.4 %collective-permute-start.3 = (f32[4,88,128]{2,1,0:T(8,128)S(1)}, f32[4,88,128]{2,1,0:T(8,128)S(1)}, u32[]{:S(2)}, u32[]{:S(2)}) collective-permute-start(f32[4,88,128]{2,1,0:T(8,128)S(1)} %slice.305), channel_id=1, source_target_pairs={{0,128},{128,0},{1,129},{129,1},{2,130},{130,2},{3,131},{131,3},{4... | collective-permute-start | bytes 540680 | tf_op jit(solution)/shard_map/ppermute | solution.py:200
  52.4 5.6 %collective-permute-start.14 = (f32[4,88,128]{2,1,0:T(8,128)S(1)}, f32[4,88,128]{2,1,0:T(8,128)S(1)}, u32[]{:S(2)}, u32[]{:S(2)}) collective-permute-start(f32[4,88,128]{2,1,0:T(8,128)S(1)} %slice.326), channel_id=1, source_target_pairs={{128,16},{16,128},{144,32},{32,144},{160,48},{48,160},{176,0},{0,1... | collective-permute-start | bytes 540680 | tf_op jit(solution)/shard_map/ppermute | solution.py:204
  58.1 6.8 %collective-permute-start.18 = (f32[2,240,128]{2,1,0:T(8,128)S(1)}, f32[2,240,128]{2,1,0:T(8,128)S(1)}, u32[]{:S(2)}, u32[]{:S(2)}) collective-permute-start(f32[2,240,128]{2,1,0:T(8,128)S(1)} %get-tuple-element.40), channel_id=1, source_target_pairs={{0,12},{4,8},{8,4},{12,0},{1,13},{5,9},{9,5},{13,1},{2,14},{6,10},... | collective-permute-start | bytes 737288 | tf_op jit(solution)/shard_map/ppermute | solution.py:198
  60.6 4.3 %collective-permute-start.19 = (f32[2,168,128]{2,1,0:T(8,128)S(1)}, f32[2,168,128]{2,1,0:T(8,128)S(1)}, u32[]{:S(2)}, u32[]{:S(2)}) collective-permute-start(f32[2,168,128]{2,1,0:T(8,128)S(1)} %get-tuple-element.41), channel_id=1, source_target_pairs={{0,4},{4,0},{8,12},{12,8},{1,5},{5,1},{9,13},{13,9},{2,6},{6,2},{1... | collective-permute-start | bytes 516104 | tf_op jit(solution)/shard_map/ppermute | solution.py:198
  65.0 6.0 %collective-permute-start.20 = (f32[1,240,128]{2,1,0:T(8,128)S(1)}, f32[1,240,128]{2,1,0:T(8,128)S(1)}, u32[]{:S(2)}, u32[]{:S(2)}) collective-permute-start(f32[1,240,128]{2,1,0:T(8,128)S(1)} %get-tuple-element.46), channel_id=1, source_target_pairs={{0,3},{1,2},{2,1},{3,0},{4,7},{5,6},{6,5},{7,4},{8,11},{9,10},{10,... | collective-permute-start | bytes 368648 | tf_op jit(solution)/shard_map/ppermute | solution.py:198
  71.2 5.7 %collective-permute-start.23 = (f32[136,128]{1,0:T(8,128)S(1)}, f32[136,128]{1,0:T(8,128)S(1)}, u32[]{:S(2)}, u32[]{:S(2)}) collective-permute-start(f32[136,128]{1,0:T(8,128)S(1)} %get-tuple-element.69), channel_id=1, source_target_pairs={{0,16},{16,0},{32,48},{48,32},{1,17},{17,1},{33,49},{49,33},{2,18}... | collective-permute-start | bytes 208904 | tf_op jit(solution)/shard_map/ppermute | solution.py:252
  72.2 5.4 %collective-permute-start.24 = (f32[136,128]{1,0:T(8,128)S(1)}, f32[136,128]{1,0:T(8,128)S(1)}, u32[]{:S(2)}, u32[]{:S(2)}) collective-permute-start(f32[136,128]{1,0:T(8,128)S(1)} %get-tuple-element.70), channel_id=1, source_target_pairs={{0,48},{16,32},{32,16},{48,0},{1,49},{17,33},{33,17},{49,1},{2,50}... | collective-permute-start | bytes 208904 | tf_op jit(solution)/shard_map/ppermute | solution.py:252
  74.4 7.1 %collective-permute-start.22 = (f32[136,128]{1,0:T(8,128)S(1)}, f32[136,128]{1,0:T(8,128)S(1)}, u32[]{:S(2)}, u32[]{:S(2)}) collective-permute-start(f32[136,128]{1,0:T(8,128)S(1)} %get-tuple-element.71), channel_id=1, source_target_pairs={{0,32},{16,48},{32,0},{48,16},{1,33},{17,49},{33,1},{49,17},{2,34}... | collective-permute-start | bytes 208904 | tf_op jit(solution)/shard_map/ppermute | solution.py:252
  (2 other events, 11.2 us)

commit v3 on v2

--- a/solution.py
+++ b/solution.py
@@ -12,11 +12,11 @@
 SLABS = 8
 UNIT = 136
 LANES = (
-    (("x1", "y1", "z", "x2", "y2"), False, ((0, 0, 88),)),
-    (("x2", "y2", "z", "x1", "y1"), True, ((0, 88, 48), (1, 0, 40))),
-    (("y1", "z", "x1", "x2", "y2"), False, ((1, 40, 80),)),
-    (("y2", "z", "x2", "x1", "y1"), True, ((1, 120, 16), (2, 0, 64))),
-    (("z", "x1", "y1", "x2", "y2"), False, ((2, 64, 72),)),
+    (("x1", "y1", "z", "x2", "y2"), False, ((0, 0, 80),)),
+    (("x2", "y2", "z", "x1", "y1"), True, ((0, 80, 56), (1, 0, 24),)),
+    (("y1", "z", "x1", "x2", "y2"), False, ((1, 24, 88),)),
+    (("y2", "z", "x2", "x1", "y1"), True, ((1, 112, 24), (2, 0, 56),)),
+    (("z", "x2", "y2", "x1", "y1"), False, ((2, 56, 80),)),
 )
 MIB = 1024 * 1024
 
@@ -122,6 +122,26 @@
     return mult(left[0], right[0]) + (mult(left[0], right[1]) + mult(left[1], right[0]))
 
 
+def symmetric(left, right):
+    top = product([half[:256] for half in left], right)
+    last = product([half[256:] for half in left], [half[:, 256:] for half in right])
+    return jnp.concatenate([top, jnp.concatenate([top[:, 256:].T, last], axis=1)], axis=0)
+
+
+def square(parts):
+    mult = functools.partial(jnp.dot, preferred_element_type=jnp.float32)
+    high, low = parts
+    mixed = mult(high, low)
+    top = mult(high[:256], high)
+    last = mult(high[256:], high[:, 256:])
+    first = top[:, :256] + (mixed[:256, :256] + mixed[:256, :256].T)
+    cross = top[:, 256:] + (mixed[:256, 256:] + mixed[256:, :256].T)
+    last = last + (mixed[256:, 256:] + mixed[256:, 256:].T)
+    return jnp.concatenate(
+        [jnp.concatenate([first, cross], axis=1), jnp.concatenate([cross.T, last], axis=1)], axis=0
+    )
+
+
 def root_kernel(factor, where_ref, slabs_ref, out_ref, full, picked):
     half = 256
     order = 2 * half
@@ -171,11 +191,13 @@
             iterate = product(split(iterate), split(step_matrix))
         if sweep < ITERS - 1:
             parts = split(step_matrix)
-            squared = split(product(parts, parts))
-            fourth = split(product(squared, squared))
+            squared = split(square(parts))
+            fourth = split(square(squared))
             if sweep == ITERS - 2:
                 coupled, identity = mine(coupled), mine(identity)
-            coupled = product(fourth, split(coupled))
+                coupled = product(fourth, split(coupled))
+            else:
+                coupled = symmetric(fourth, split(coupled))
     for core in range(2):
         out_ref[16 * core : 16 * core + 16] = iterate[:, 128 * core : 128 * core + 128].reshape(16, 8, 128)
 
@@ -204,29 +226,54 @@
     return lax.ppermute(value, ("z_lo", "z_hi"), pairs)
 
 
+def after(value, before):
+    return lax.optimization_barrier((value, before))[0]
+
+
 def body(grads):
     local_grads = grads[0]
     order = local_grads.shape[1]
     where = jnp.stack([lax.axis_index(name).astype(jnp.int32) for name in ("x", "y", "z_lo", "core")])
     factor = 1.0 / (256 * order)
-    waiting = local_grads
-    kept, sent = [[] for _ in LANES], [[] for _ in LANES]
-    for part in range(3):
-        own, away = gram(part, where, waiting[4 * part : 4 * part + 4])
-        waiting, away = lax.optimization_barrier((waiting, away))
-        came = lax.ppermute(away, "core", [(0, 1), (1, 0)])
-        for lane, base, _, size in pieces_of(part):
-            for halves, first in ((kept, base), (sent, base + 16 * size)):
-                rows = slice(first, first + 16 * size)
-                halves[lane].append((own[rows] + came[rows]).reshape(16, size, 128))
+    own, came, keeps, sends = [], [], [], []
+
+    def enter(part):
+        blocks = local_grads[4 * part : 4 * part + 4]
+        if part:
+            blocks = after(local_grads, away_of[-1])[4 * part : 4 * part + 4]
+        stays, away = gram(part, where, blocks)
+        away_of.append(away)
+        own.append(stays)
+        came.append(lax.ppermute(away, "core", [(0, 1), (1, 0)]))
+
+    def depart(lane):
+        halves = [[], []]
+        for part in range(3):
+            for which, base, _, size in pieces_of(part):
+                if which == lane:
+                    other = came[part]
+                    for half, first in zip(halves, (base, base + 16 * size)):
+                        rows = slice(first, first + 16 * size)
+                        half.append((own[part][rows] + other[rows]).reshape(16, size, 128))
+        keep, send = (half[0] if len(half) == 1 else jnp.concatenate(half, axis=1) for half in halves)
+        keeps.append(keep)
+        sends.append(send)
+
+    away_of = []
+    enter(0)
+    enter(1)
+    depart(0)
+    enter(2)
+    for lane in range(1, len(LANES)):
+        depart(lane)
+    for step in range(3):
+        for lane, (order, odd, _) in enumerate(LANES):
+            summed = keeps[lane] + swap(sends[lane], order[step], odd)
+            middle = summed.shape[0] // 2
+            keeps[lane], sends[lane] = summed[:middle], summed[middle:]
     done = [[], []]
-    for (order, odd, _), keep, send in zip(LANES, kept, sent):
-        keep, send = (half[0] if len(half) == 1 else jnp.concatenate(half, axis=1) for half in (keep, send))
-        for step in range(3):
-            summed = keep + swap(send, order[step], odd)
-            middle = summed.shape[0] // 2
-            keep, send = summed[:middle], summed[middle:]
-        done[odd].append(summed)
+    for (order, _, _), keep, send in zip(LANES, keeps, sends):
+        done[order[3] == "x1"].append(jnp.concatenate([keep, send]))
     even, odd = (jnp.concatenate(lanes, axis=1) for lanes in done)
     for along in ("x", "y"):
         middle = even.shape[0] // 2
@@ -239,9 +286,11 @@
         even, odd = even_keep + even_came, odd_keep + odd_came
     even, odd = even[0], odd[0]
     held = {}
-    for lanes, total in ((LANES[0::2], even), (LANES[1::2], odd)):
+    for total, last in ((even, "x2"), (odd, "x1")):
         first = 0
-        for _, _, pieces in lanes:
+        for order, _, pieces in LANES:
+            if order[3] != last:
+                continue
             for piece in pieces:
                 held[piece[:2]] = total[first : first + piece[2]]
                 first += piece[2]

time: 129 us -> 126 us (0.977)
  waiting for transfers between devices: 33.1 us -> 29.7 us
  starting transfers between devices: 35.8 us -> 37.9 us
  Pallas kernels: 17.5 us -> 15.9 us
    ppermute x3, waiting for transfers between devices: 11.4 us -> 0.01 us  [swap(): return lax.ppermute(value, 'z_lo', [(0, 1), (1, 0)])]
    ppermute x14, waiting for transfers between devices: 11 us -> 22.3 us  [swap(): return lax.ppermute(value, name[0], [(i, i ^ flip) for i in range(4)])]
    ppermute x2, waiting for transfers between devices: 2.44 us -> 0.01 us  [swap(): return lax.ppermute(value, ('z_lo', 'z_hi'), pairs)]
    ppermute x3, waiting for transfers between devices: 3.72 us -> 1.38 us  [enter(): came.append(lax.ppermute(away, 'core', [(0, 1), (1, 0)]))]
    ppermute x3, starting transfers between devices: 1.36 us -> 3.35 us  [swap(): return lax.ppermute(value, 'z_lo', [(0, 1), (1, 0)])]
    pallas_call x1, Pallas kernels: 9.76 us -> 8.15 us  [inverse_root(): pl.pallas_call(functools.partial(root_kernel, factor), out_shape=jax.Shap...]
    ppermute x3, waiting for transfers between devices: 4.49 us -> 6.04 us  [body(): lax.ppermute(pick[k], 'z_hi', [(i, i ^ k) for i in range(4)])]
    all_to_all x1, blocking collectives: 26.6 us -> 25.3 us  [body(): arrived = lax.all_to_all(pieces, ('core', 'z_hi', 'x'), 0, 0, tiled=True)]
  transfers between devices with their start and end apart: 25 -> 25, of which waited for: 12 -> 13; matrix products, arithmetic and copies ran while one was open for 2% -> 2% of each run, Pallas kernels for 4% -> 4%
where the time goes in v3:
time: 126 us; the launch traced here: 125 us
  starting transfers between devices  37.9 us (30%)
  blocking collectives  36.5 us (29%)
  waiting for transfers between devices  29.7 us (24%)
  Pallas kernels  15.9 us (13%)
  local copies, waits for them, and re-layouts  3.13 us (2%)
  other arithmetic  1.89 us (2%)
    all_to_all x1, blocking collectives, body(): arrived = lax.all_to_all(pieces, ('core', 'z_hi', 'x'), 0, 0, tiled=True)  25.3 us
    ppermute x14, waiting for transfers between devices, swap(): return lax.ppermute(value, name[0], [(i, i ^ flip) for i in range(4)])  22.3 us
    ppermute x14, starting transfers between devices, swap(): return lax.ppermute(value, name[0], [(i, i ^ flip) for i in range(4)])  17.4 us
    all_to_all x1, blocking collectives, body(): lax.all_to_all(jnp.broadcast_to(slab[None], (SLABS, UNIT, 128)), ('y', 'z...  11.2 us
    pallas_call x1, Pallas kernels, inverse_root(): pl.pallas_call(functools.partial(root_kernel, factor), out_shape=jax.Shap...  8.15 us
    pallas_call x3, Pallas kernels, gram(): pl.pallas_call(functools.partial(gram_kernel, part), out_shape=(shape, sh...  7.74 us
    ppermute x2, starting transfers between devices, swap(): return lax.ppermute(value, ('z_lo', 'z_hi'), pairs)  7.45 us
    ppermute x3, waiting for transfers between devices, body(): lax.ppermute(pick[k], 'z_hi', [(i, i ^ k) for i in range(4)])  6.04 us
  transfers between devices with their start and end apart: 25, of which 13 were waited for; matrix products, arithmetic and copies ran while one was open for 2% of the time, Pallas kernels for 4%

profile of v3, /device:TPU:1, one launch (start us, length us, event | category | flops | bytes accessed | tf_op | source)
XLA Modules:
  0.0 125.4 jit_solution(6831138974458546285)
XLA Ops:
  0.0 1.9 %slice_bitcast_fusion.grads_ref = bf16[4,512,512]{2,1,0:T(8,128)(2,1)S(1)} fusion(bf16[1,12,512,512]{3,2,1,0:T(8,128)(2,1)} %param.1), kind=kLoop, calls=%fused_computation | loop fusion | bytes 4194304 | tf_op jit(solution)/shard_map/slice | solution.py:241
  2.0 2.6 %gram_0.1 = (f32[4352,128]{1,0:T(8,128)S(1)}, f32[4352,128]{1,0:T(8,128)S(1)}) custom-call(s32[4]{0:T(128)S(1)} %pad_add_fusion.where_ref, bf16[4,512,512]{2,1,0:T(8,128)(2,1)S(1)} %slice_bitcast_fusion.grads_ref), custom_call_target="tpu_custom_call" | custom-call | tf_op jit(solution)/shard_map/gram_0/pallas_call | solution.py:105
  4.6 3.3 %collective-permute-start = (f32[4352,128]{1,0:T(8,128)S(1)}, f32[4352,128]{1,0:T(8,128)S(1)}, u32[]{:S(2)}, u32[]{:S(2)}) collective-permute-start(f32[4352,128]{1,0:T(8,128)S(1)} %get-tuple-element.26), channel_id=1, source_target_pairs={{0,64},{64,0},{1,65},{65,1},{2,66},{66,2},{3,67},{67,3},{4,68},{68... | collective-permute-start | bytes 6684680 | tf_op jit(solution)/shard_map/ppermute | solution.py:247
  8.0 2.6 %gram_1.1 = (f32[4352,128]{1,0:T(8,128)S(1)}, f32[4352,128]{1,0:T(8,128)S(1)}) custom-call(s32[4]{0:T(128)S(1)} %pad_add_fusion.where_ref, bf16[4,512,512]{2,1,0:T(8,128)(2,1)S(1)} %slice.250.grads_ref), custom_call_target="tpu_custom_call" | custom-call | tf_op jit(solution)/shard_map/gram_1/pallas_call | solution.py:105
  10.9 2.6 %gram_2.1 = (f32[4352,128]{1,0:T(8,128)S(1)}, f32[4352,128]{1,0:T(8,128)S(1)}) custom-call(s32[4]{0:T(128)S(1)} %pad_add_fusion.where_ref, bf16[4,512,512]{2,1,0:T(8,128)(2,1)S(1)} %slice.274.grads_ref), custom_call_target="tpu_custom_call" | custom-call | tf_op jit(solution)/shard_map/gram_2/pallas_call | solution.py:105
  20.0 1.7 %collective-permute-start.15 = (f32[16,80,128]{2,1,0:T(8,128)S(1)}, f32[16,80,128]{2,1,0:T(8,128)S(1)}, u32[]{:S(2)}, u32[]{:S(2)}) collective-permute-start(f32[16,80,128]{2,1,0:T(8,128)S(1)} %bitcast.65), channel_id=1, source_target_pairs={{0,128},{128,0},{1,129},{129,1},{2,130},{130,2},{3,131},{131,3},{4... | collective-permute-start | bytes 1966088 | tf_op jit(solution)/shard_map/ppermute | solution.py:222
  21.7 8.9 %collective-permute-done.1 = f32[16,80,128]{2,1,0:T(8,128)S(1)} collective-permute-done((f32[16,80,128]{2,1,0:T(8,128)S(1)}, f32[16,80,128]{2,1,0:T(8,128)S(1)}, u32[]{:S(2)}, u32[]{:S(2)}) %collective-permute-start.1) | collective-permute-done | bytes 655392 | tf_op jit(solution)/shard_map/ppermute | solution.py:220
  31.0 1.6 %collective-permute-done.8 = f32[16,80,128]{2,1,0:T(8,128)S(1)} collective-permute-done((f32[16,80,128]{2,1,0:T(8,128)S(1)}, f32[16,80,128]{2,1,0:T(8,128)S(1)}, u32[]{:S(2)}, u32[]{:S(2)}) %collective-permute-start.8) | collective-permute-done | bytes 655392 | tf_op jit(solution)/shard_map/ppermute | solution.py:220
  32.6 1.6 %collective-permute-start.9 = (f32[8,80,128]{2,1,0:T(8,128)S(1)}, f32[8,80,128]{2,1,0:T(8,128)S(1)}, u32[]{:S(2)}, u32[]{:S(2)}) collective-permute-start(f32[8,80,128]{2,1,0:T(8,128)S(1)} %slice.334), channel_id=1, source_target_pairs={{0,3},{1,2},{2,1},{3,0},{4,7},{5,6},{6,5},{7,4},{8,11},{9,10},{10,... | collective-permute-start | bytes 983048 | tf_op jit(solution)/shard_map/ppermute | solution.py:220
  35.8 4.4 %collective-permute-start.13 = (f32[8,80,128]{2,1,0:T(8,128)S(1)}, f32[8,80,128]{2,1,0:T(8,128)S(1)}, u32[]{:S(2)}, u32[]{:S(2)}) collective-permute-start(f32[8,80,128]{2,1,0:T(8,128)S(1)} %slice.342), channel_id=1, source_target_pairs={{128,16},{16,128},{144,32},{32,144},{160,48},{48,160},{176,0},{0,1... | collective-permute-start | bytes 983048 | tf_op jit(solution)/shard_map/ppermute | solution.py:226
  40.3 2.2 %collective-permute-start.16 = (f32[8,80,128]{2,1,0:T(8,128)S(1)}, f32[8,80,128]{2,1,0:T(8,128)S(1)}, u32[]{:S(2)}, u32[]{:S(2)}) collective-permute-start(f32[8,80,128]{2,1,0:T(8,128)S(1)} %slice.348), channel_id=1, source_target_pairs={{0,12},{4,8},{8,4},{12,0},{1,13},{5,9},{9,5},{13,1},{2,14},{6,10},... | collective-permute-start | bytes 983048 | tf_op jit(solution)/shard_map/ppermute | solution.py:220
  44.4 3.0 %collective-permute-start.10 = (f32[4,80,128]{2,1,0:T(8,128)S(1)}, f32[4,80,128]{2,1,0:T(8,128)S(1)}, u32[]{:S(2)}, u32[]{:S(2)}) collective-permute-start(f32[4,80,128]{2,1,0:T(8,128)S(1)} %slice.336), channel_id=1, source_target_pairs={{128,16},{16,128},{144,32},{32,144},{160,48},{48,160},{176,0},{0,1... | collective-permute-start | bytes 491528 | tf_op jit(solution)/shard_map/ppermute | solution.py:226
  47.5 1.8 %collective-permute-start.14 = (f32[4,80,128]{2,1,0:T(8,128)S(1)}, f32[4,80,128]{2,1,0:T(8,128)S(1)}, u32[]{:S(2)}, u32[]{:S(2)}) collective-permute-start(f32[4,80,128]{2,1,0:T(8,128)S(1)} %slice.344), channel_id=1, source_target_pairs={{0,12},{4,8},{8,4},{12,0},{1,13},{5,9},{9,5},{13,1},{2,14},{6,10},... | collective-permute-start | bytes 491528 | tf_op jit(solution)/shard_map/ppermute | solution.py:220
  49.4 2.6 %collective-permute-start.17 = (f32[4,80,128]{2,1,0:T(8,128)S(1)}, f32[4,80,128]{2,1,0:T(8,128)S(1)}, u32[]{:S(2)}, u32[]{:S(2)}) collective-permute-start(f32[4,80,128]{2,1,0:T(8,128)S(1)} %slice.350), channel_id=1, source_target_pairs={{0,3},{1,2},{2,1},{3,0},{4,7},{5,6},{6,5},{7,4},{8,11},{9,10},{10,... | collective-permute-start | bytes 491528 | tf_op jit(solution)/shard_map/ppermute | solution.py:220
  53.0 2.2 %collective-permute-done.17 = f32[4,80,128]{2,1,0:T(8,128)S(1)} collective-permute-done((f32[4,80,128]{2,1,0:T(8,128)S(1)}, f32[4,80,128]{2,1,0:T(8,128)S(1)}, u32[]{:S(2)}, u32[]{:S(2)}) %collective-permute-start.17) | collective-permute-done | bytes 163872 | tf_op jit(solution)/shard_map/ppermute | solution.py:220
  57.1 2.2 %collective-permute-start.18 = (f32[2,168,128]{2,1,0:T(8,128)S(1)}, f32[2,168,128]{2,1,0:T(8,128)S(1)}, u32[]{:S(2)}, u32[]{:S(2)}) collective-permute-start(f32[2,168,128]{2,1,0:T(8,128)S(1)} %get-tuple-element.34), channel_id=1, source_target_pairs={{0,12},{4,8},{8,4},{12,0},{1,13},{5,9},{9,5},{13,1},{2,14},{6,10},... | collective-permute-start | bytes 516104 | tf_op jit(solution)/shard_map/ppermute | solution.py:220
  59.3 3.3 %collective-permute-done.18 = f32[2,168,128]{2,1,0:T(8,128)S(1)} collective-permute-done((f32[2,168,128]{2,1,0:T(8,128)S(1)}, f32[2,168,128]{2,1,0:T(8,128)S(1)}, u32[]{:S(2)}, u32[]{:S(2)}) %collective-permute-start.18) | collective-permute-done | bytes 172064 | tf_op jit(solution)/shard_map/ppermute | solution.py:220
  63.1 2.6 %collective-permute-start.20 = (f32[1,168,128]{2,1,0:T(8,128)S(1)}, f32[1,168,128]{2,1,0:T(8,128)S(1)}, u32[]{:S(2)}, u32[]{:S(2)}) collective-permute-start(f32[1,168,128]{2,1,0:T(8,128)S(1)} %get-tuple-element.40), channel_id=1, source_target_pairs={{0,3},{1,2},{2,1},{3,0},{4,7},{5,6},{6,5},{7,4},{8,11},{9,10},{10,... | collective-permute-start | bytes 258056 | tf_op jit(solution)/shard_map/ppermute | solution.py:220
  65.7 2.4 %collective-permute-done.20 = f32[1,168,128]{2,1,0:T(8,128)S(1)} collective-permute-done((f32[1,168,128]{2,1,0:T(8,128)S(1)}, f32[1,168,128]{2,1,0:T(8,128)S(1)}, u32[]{:S(2)}, u32[]{:S(2)}) %collective-permute-start.20) | collective-permute-done | bytes 86048 | tf_op jit(solution)/shard_map/ppermute | solution.py:220
  68.8 3.7 %collective-permute-start.24 = (f32[136,128]{1,0:T(8,128)S(1)}, f32[136,128]{1,0:T(8,128)S(1)}, u32[]{:S(2)}, u32[]{:S(2)}) collective-permute-start(f32[136,128]{1,0:T(8,128)S(1)} %get-tuple-element.64), channel_id=1, source_target_pairs={{0,48},{16,32},{32,16},{48,0},{1,49},{17,33},{33,17},{49,1},{2,50}... | collective-permute-start | bytes 208904 | tf_op jit(solution)/shard_map/ppermute | solution.py:301
  74.9 5.1 %collective-permute-done.22 = f32[136,128]{1,0:T(8,128)S(1)} collective-permute-done((f32[136,128]{1,0:T(8,128)S(1)}, f32[136,128]{1,0:T(8,128)S(1)}, u32[]{:S(2)}, u32[]{:S(2)}) %collective-permute-start.22) | collective-permute-done | bytes 69664 | tf_op jit(solution)/shard_map/ppermute | solution.py:301
  80.1 11.2 %all_to_all.10.slabs_ref = f32[8,136,128]{2,1,0:T(8,128)S(1)} all-to-all(f32[8,136,128]{2,1,0:T(8,128)S(1)} %broadcast_in_dim.2), channel_id=1, replica_groups=mesh['z_lo'=2,'core'=2,'z_hi'=4,'x'=4,'y'=4] {'y','z_lo'}, dimensions={0} | all-to-all | bytes 1114112 | tf_op jit(solution)/shard_map/all_to_all | solution.py:302
  91.3 8.2 %inverse_root.1 = f32[32,8,128]{2,1,0:T(8,128)S(1)} custom-call(s32[4]{0:T(128)S(1)} %pad_add_fusion.where_ref, f32[8,136,128]{2,1,0:T(8,128)S(1)} %all_to_all.10.slabs_ref), custom_call_target="tpu_custom_call" | custom-call | tf_op jit(solution)/shard_map/inverse_root/pallas_call | solution.py:206
  99.5 25.3 %all_to_all.11 = f32[32,8,128]{2,1,0:T(8,128)S(1)} all-to-all(f32[32,8,128]{2,1,0:T(8,128)S(1)} %inverse_root.1), channel_id=1, replica_groups=mesh['z_lo'=2,'core'=2,'z_hi'=4,'x'=4,'y'=4] {'core','z_hi','x'}, dimensions={0} | all-to-all | bytes 262144 | tf_op jit(solution)/shard_map/all_to_all | solution.py:306
  (92 shorter events, 18.2 us)
Async XLA Ops:
  4.6 9.5 %collective-permute-start = (f32[4352,128]{1,0:T(8,128)S(1)}, f32[4352,128]{1,0:T(8,128)S(1)}, u32[]{:S(2)}, u32[]{:S(2)}) collective-permute-start(f32[4352,128]{1,0:T(8,128)S(1)} %get-tuple-element.26), channel_id=1, source_target_pairs={{0,64},{64,0},{1,65},{65,1},{2,66},{66,2},{3,67},{67,3},{4,68},{68... | collective-permute-start | bytes 6684680 | tf_op jit(solution)/shard_map/ppermute | solution.py:247
  13.5 4.8 %collective-permute-start.11 = (f32[4352,128]{1,0:T(8,128)S(1)}, f32[4352,128]{1,0:T(8,128)S(1)}, u32[]{:S(2)}, u32[]{:S(2)}) collective-permute-start(f32[4352,128]{1,0:T(8,128)S(1)} %get-tuple-element.32), channel_id=1, source_target_pairs={{0,64},{64,0},{1,65},{65,1},{2,66},{66,2},{3,67},{67,3},{4,68},{68... | collective-permute-start | bytes 6684680 | tf_op jit(solution)/shard_map/ppermute | solution.py:247
  14.2 16.4 %collective-permute-start.1 = (f32[16,80,128]{2,1,0:T(8,128)S(1)}, f32[16,80,128]{2,1,0:T(8,128)S(1)}, u32[]{:S(2)}, u32[]{:S(2)}) collective-permute-start(f32[16,80,128]{2,1,0:T(8,128)S(1)} %bitcast.64), channel_id=1, source_target_pairs={{0,4},{4,0},{8,12},{12,8},{1,5},{5,1},{9,13},{13,9},{2,6},{6,2},{1... | collective-permute-start | bytes 1966088 | tf_op jit(solution)/shard_map/ppermute | solution.py:220
  15.3 17.2 %collective-permute-start.8 = (f32[16,80,128]{2,1,0:T(8,128)S(1)}, f32[16,80,128]{2,1,0:T(8,128)S(1)}, u32[]{:S(2)}, u32[]{:S(2)}) collective-permute-start(f32[16,80,128]{2,1,0:T(8,128)S(1)} %pad_maximum_fusion), channel_id=1, source_target_pairs={{0,12},{4,8},{8,4},{12,0},{1,13},{5,9},{9,5},{13,1},{2,14},{6,10},... | collective-permute-start | bytes 1966088 | tf_op jit(solution)/shard_map/ppermute | solution.py:220
  16.3 26.3 %collective-permute-start.5 = (f32[16,88,128]{2,1,0:T(8,128)S(1)}, f32[16,88,128]{2,1,0:T(8,128)S(1)}, u32[]{:S(2)}, u32[]{:S(2)}) collective-permute-start(f32[16,88,128]{2,1,0:T(8,128)S(1)} %bitcast.63), channel_id=1, source_target_pairs={{0,1},{1,0},{2,3},{3,2},{4,5},{5,4},{6,7},{7,6},{8,9},{9,8},{10,11... | collective-permute-start | bytes 2162696 | tf_op jit(solution)/shard_map/ppermute | solution.py:220
  18.4 17.2 %collective-permute-start.12 = (f32[16,80,128]{2,1,0:T(8,128)S(1)}, f32[16,80,128]{2,1,0:T(8,128)S(1)}, u32[]{:S(2)}, u32[]{:S(2)}) collective-permute-start(f32[16,80,128]{2,1,0:T(8,128)S(1)} %pad_maximum_fusion.1), channel_id=1, source_target_pairs={{0,3},{1,2},{2,1},{3,0},{4,7},{5,6},{6,5},{7,4},{8,11},{9,10},{10,... | collective-permute-start | bytes 1966088 | tf_op jit(solution)/shard_map/ppermute | solution.py:220
  20.0 20.2 %collective-permute-start.15 = (f32[16,80,128]{2,1,0:T(8,128)S(1)}, f32[16,80,128]{2,1,0:T(8,128)S(1)}, u32[]{:S(2)}, u32[]{:S(2)}) collective-permute-start(f32[16,80,128]{2,1,0:T(8,128)S(1)} %bitcast.65), channel_id=1, source_target_pairs={{0,128},{128,0},{1,129},{129,1},{2,130},{130,2},{3,131},{131,3},{4... | collective-permute-start | bytes 1966088 | tf_op jit(solution)/shard_map/ppermute | solution.py:222
  30.7 12.1 %collective-permute-start.2 = (f32[8,80,128]{2,1,0:T(8,128)S(1)}, f32[8,80,128]{2,1,0:T(8,128)S(1)}, u32[]{:S(2)}, u32[]{:S(2)}) collective-permute-start(f32[8,80,128]{2,1,0:T(8,128)S(1)} %slice.318), channel_id=1, source_target_pairs={{0,1},{1,0},{2,3},{3,2},{4,5},{5,4},{6,7},{7,6},{8,9},{9,8},{10,11... | collective-permute-start | bytes 983048 | tf_op jit(solution)/shard_map/ppermute | solution.py:220
  32.6 11.7 %collective-permute-start.9 = (f32[8,80,128]{2,1,0:T(8,128)S(1)}, f32[8,80,128]{2,1,0:T(8,128)S(1)}, u32[]{:S(2)}, u32[]{:S(2)}) collective-permute-start(f32[8,80,128]{2,1,0:T(8,128)S(1)} %slice.334), channel_id=1, source_target_pairs={{0,3},{1,2},{2,1},{3,0},{4,7},{5,6},{6,5},{7,4},{8,11},{9,10},{10,... | collective-permute-start | bytes 983048 | tf_op jit(solution)/shard_map/ppermute | solution.py:220
  35.8 11.7 %collective-permute-start.13 = (f32[8,80,128]{2,1,0:T(8,128)S(1)}, f32[8,80,128]{2,1,0:T(8,128)S(1)}, u32[]{:S(2)}, u32[]{:S(2)}) collective-permute-start(f32[8,80,128]{2,1,0:T(8,128)S(1)} %slice.342), channel_id=1, source_target_pairs={{128,16},{16,128},{144,32},{32,144},{160,48},{48,160},{176,0},{0,1... | collective-permute-start | bytes 983048 | tf_op jit(solution)/shard_map/ppermute | solution.py:226
  40.3 9.0 %collective-permute-start.16 = (f32[8,80,128]{2,1,0:T(8,128)S(1)}, f32[8,80,128]{2,1,0:T(8,128)S(1)}, u32[]{:S(2)}, u32[]{:S(2)}) collective-permute-start(f32[8,80,128]{2,1,0:T(8,128)S(1)} %slice.348), channel_id=1, source_target_pairs={{0,12},{4,8},{8,4},{12,0},{1,13},{5,9},{9,5},{13,1},{2,14},{6,10},... | collective-permute-start | bytes 983048 | tf_op jit(solution)/shard_map/ppermute | solution.py:220
  42.6 9.4 %collective-permute-start.6 = (f32[8,88,128]{2,1,0:T(8,128)S(1)}, f32[8,88,128]{2,1,0:T(8,128)S(1)}, u32[]{:S(2)}, u32[]{:S(2)}) collective-permute-start(f32[8,88,128]{2,1,0:T(8,128)S(1)} %slice.324), channel_id=1, source_target_pairs={{0,128},{128,0},{1,129},{129,1},{2,130},{130,2},{3,131},{131,3},{4... | collective-permute-start | bytes 1081352 | tf_op jit(solution)/shard_map/ppermute | solution.py:222
  42.8 12.5 %collective-permute-start.3 = (f32[4,80,128]{2,1,0:T(8,128)S(1)}, f32[4,80,128]{2,1,0:T(8,128)S(1)}, u32[]{:S(2)}, u32[]{:S(2)}) collective-permute-start(f32[4,80,128]{2,1,0:T(8,128)S(1)} %slice.320), channel_id=1, source_target_pairs={{0,128},{128,0},{1,129},{129,1},{2,130},{130,2},{3,131},{131,3},{4... | collective-permute-start | bytes 491528 | tf_op jit(solution)/shard_map/ppermute | solution.py:222
  44.4 7.9 %collective-permute-start.10 = (f32[4,80,128]{2,1,0:T(8,128)S(1)}, f32[4,80,128]{2,1,0:T(8,128)S(1)}, u32[]{:S(2)}, u32[]{:S(2)}) collective-permute-start(f32[4,80,128]{2,1,0:T(8,128)S(1)} %slice.336), channel_id=1, source_target_pairs={{128,16},{16,128},{144,32},{32,144},{160,48},{48,160},{176,0},{0,1... | collective-permute-start | bytes 491528 | tf_op jit(solution)/shard_map/ppermute | solution.py:226
  47.5 5.5 %collective-permute-start.14 = (f32[4,80,128]{2,1,0:T(8,128)S(1)}, f32[4,80,128]{2,1,0:T(8,128)S(1)}, u32[]{:S(2)}, u32[]{:S(2)}) collective-permute-start(f32[4,80,128]{2,1,0:T(8,128)S(1)} %slice.344), channel_id=1, source_target_pairs={{0,12},{4,8},{8,4},{12,0},{1,13},{5,9},{9,5},{13,1},{2,14},{6,10},... | collective-permute-start | bytes 491528 | tf_op jit(solution)/shard_map/ppermute | solution.py:220
  49.4 5.8 %collective-permute-start.17 = (f32[4,80,128]{2,1,0:T(8,128)S(1)}, f32[4,80,128]{2,1,0:T(8,128)S(1)}, u32[]{:S(2)}, u32[]{:S(2)}) collective-permute-start(f32[4,80,128]{2,1,0:T(8,128)S(1)} %slice.350), channel_id=1, source_target_pairs={{0,3},{1,2},{2,1},{3,0},{4,7},{5,6},{6,5},{7,4},{8,11},{9,10},{10,... | collective-permute-start | bytes 491528 | tf_op jit(solution)/shard_map/ppermute | solution.py:220
  52.1 4.7 %collective-permute-start.7 = (f32[4,88,128]{2,1,0:T(8,128)S(1)}, f32[4,88,128]{2,1,0:T(8,128)S(1)}, u32[]{:S(2)}, u32[]{:S(2)}) collective-permute-start(f32[4,88,128]{2,1,0:T(8,128)S(1)} %slice.326), channel_id=1, source_target_pairs={{0,4},{4,0},{8,12},{12,8},{1,5},{5,1},{9,13},{13,9},{2,6},{6,2},{1... | collective-permute-start | bytes 540680 | tf_op jit(solution)/shard_map/ppermute | solution.py:220
  56.9 6.0 %collective-permute-start.19 = (f32[2,240,128]{2,1,0:T(8,128)S(1)}, f32[2,240,128]{2,1,0:T(8,128)S(1)}, u32[]{:S(2)}, u32[]{:S(2)}) collective-permute-start(f32[2,240,128]{2,1,0:T(8,128)S(1)} %get-tuple-element.35), channel_id=1, source_target_pairs={{0,4},{4,0},{8,12},{12,8},{1,5},{5,1},{9,13},{13,9},{2,6},{6,2},{1... | collective-permute-start | bytes 737288 | tf_op jit(solution)/shard_map/ppermute | solution.py:220
  57.1 5.5 %collective-permute-start.18 = (f32[2,168,128]{2,1,0:T(8,128)S(1)}, f32[2,168,128]{2,1,0:T(8,128)S(1)}, u32[]{:S(2)}, u32[]{:S(2)}) collective-permute-start(f32[2,168,128]{2,1,0:T(8,128)S(1)} %get-tuple-element.34), channel_id=1, source_target_pairs={{0,12},{4,8},{8,4},{12,0},{1,13},{5,9},{9,5},{13,1},{2,14},{6,10},... | collective-permute-start | bytes 516104 | tf_op jit(solution)/shard_map/ppermute | solution.py:220
  63.0 5.0 %collective-permute-start.21 = (f32[1,240,128]{2,1,0:T(8,128)S(1)}, f32[1,240,128]{2,1,0:T(8,128)S(1)}, u32[]{:S(2)}, u32[]{:S(2)}) collective-permute-start(f32[1,240,128]{2,1,0:T(8,128)S(1)} %get-tuple-element.41), channel_id=1, source_target_pairs={{0,1},{1,0},{2,3},{3,2},{4,5},{5,4},{6,7},{7,6},{8,9},{9,8},{10,11... | collective-permute-start | bytes 368648 | tf_op jit(solution)/shard_map/ppermute | solution.py:220
  63.1 4.9 %collective-permute-start.20 = (f32[1,168,128]{2,1,0:T(8,128)S(1)}, f32[1,168,128]{2,1,0:T(8,128)S(1)}, u32[]{:S(2)}, u32[]{:S(2)}) collective-permute-start(f32[1,168,128]{2,1,0:T(8,128)S(1)} %get-tuple-element.40), channel_id=1, source_target_pairs={{0,3},{1,2},{2,1},{3,0},{4,7},{5,6},{6,5},{7,4},{8,11},{9,10},{10,... | collective-permute-start | bytes 258056 | tf_op jit(solution)/shard_map/ppermute | solution.py:220
  68.2 5.7 %collective-permute-start.23 = (f32[136,128]{1,0:T(8,128)S(1)}, f32[136,128]{1,0:T(8,128)S(1)}, u32[]{:S(2)}, u32[]{:S(2)}) collective-permute-start(f32[136,128]{1,0:T(8,128)S(1)} %get-tuple-element.63), channel_id=1, source_target_pairs={{0,16},{16,0},{32,48},{48,32},{1,17},{17,1},{33,49},{49,33},{2,18}... | collective-permute-start | bytes 208904 | tf_op jit(solution)/shard_map/ppermute | solution.py:301
  68.8 6.2 %collective-permute-start.24 = (f32[136,128]{1,0:T(8,128)S(1)}, f32[136,128]{1,0:T(8,128)S(1)}, u32[]{:S(2)}, u32[]{:S(2)}) collective-permute-start(f32[136,128]{1,0:T(8,128)S(1)} %get-tuple-element.64), channel_id=1, source_target_pairs={{0,48},{16,32},{32,16},{48,0},{1,49},{17,33},{33,17},{49,1},{2,50}... | collective-permute-start | bytes 208904 | tf_op jit(solution)/shard_map/ppermute | solution.py:301
  72.5 7.5 %collective-permute-start.22 = (f32[136,128]{1,0:T(8,128)S(1)}, f32[136,128]{1,0:T(8,128)S(1)}, u32[]{:S(2)}, u32[]{:S(2)}) collective-permute-start(f32[136,128]{1,0:T(8,128)S(1)} %get-tuple-element.65), channel_id=1, source_target_pairs={{0,32},{16,48},{32,0},{48,16},{1,33},{17,49},{33,1},{49,17},{2,34}... | collective-permute-start | bytes 208904 | tf_op jit(solution)/shard_map/ppermute | solution.py:301
  (2 other events, 12.3 us)

commit v4 on v3

--- a/solution.py
+++ b/solution.py
@@ -12,9 +12,9 @@
 SLABS = 8
 UNIT = 136
 LANES = (
-    (("x1", "y1", "z", "x2", "y2"), False, ((0, 0, 80),)),
-    (("x2", "y2", "z", "x1", "y1"), True, ((0, 80, 56), (1, 0, 24),)),
-    (("y1", "z", "x1", "x2", "y2"), False, ((1, 24, 88),)),
+    (("x1", "y1", "z", "x2", "y2"), False, ((0, 0, 88),)),
+    (("x2", "y2", "z", "x1", "y1"), True, ((0, 88, 48), (1, 0, 32),)),
+    (("y1", "z", "x1", "x2", "y2"), False, ((1, 32, 80),)),
     (("y2", "z", "x2", "x1", "y1"), True, ((1, 112, 24), (2, 0, 56),)),
     (("z", "x2", "y2", "x1", "y1"), False, ((2, 56, 80),)),
 )
@@ -277,9 +277,8 @@
     even, odd = (jnp.concatenate(lanes, axis=1) for lanes in done)
     for along in ("x", "y"):
         middle = even.shape[0] // 2
-        even_keep, odd_keep, even_send, odd_send = lax.optimization_barrier(
-            (even[:middle], odd[:middle], even[middle:], odd[middle:])
-        )
+        even_keep, even_send = lax.optimization_barrier((even[:middle], even[middle:]))
+        odd_keep, odd_send = lax.optimization_barrier((odd[:middle], odd[middle:]))
         even_came, odd_came = lax.optimization_barrier(
             (swap(even_send, along + "2", False), swap(odd_send, along + "1", True))
         )

time: 126 us -> 122 us (0.968)
  blocking collectives: 36.5 us -> 33.8 us
    all_to_all x1, blocking collectives: 25.3 us -> 23.5 us  [body(): arrived = lax.all_to_all(pieces, ('core', 'z_hi', 'x'), 0, 0, tiled=True)]
    ppermute x14, waiting for transfers between devices: 22.3 us -> 20.5 us  [swap(): return lax.ppermute(value, name[0], [(i, i ^ flip) for i in range(4)])]
  transfers between devices with their start and end apart: 25 -> 25, of which waited for: 13 -> 11; matrix products, arithmetic and copies ran while one was open for 2% -> 2% of each run, Pallas kernels for 4% -> 4%
where the time goes in v4:
time: 122 us
  starting transfers between devices  38.1 us (31%)
  blocking collectives  33.8 us (28%)
  waiting for transfers between devices  28.9 us (24%)
  Pallas kernels  15.9 us (13%)
  local copies, waits for them, and re-layouts  3.14 us (3%)
  other arithmetic  1.85 us (2%)
    all_to_all x1, blocking collectives, body(): arrived = lax.all_to_all(pieces, ('core', 'z_hi', 'x'), 0, 0, tiled=True)  23.5 us
    ppermute x14, waiting for transfers between devices, swap(): return lax.ppermute(value, name[0], [(i, i ^ flip) for i in range(4)])  20.5 us
    ppermute x14, starting transfers between devices, swap(): return lax.ppermute(value, name[0], [(i, i ^ flip) for i in range(4)])  16.4 us
    all_to_all x1, blocking collectives, body(): lax.all_to_all(jnp.broadcast_to(slab[None], (SLABS, UNIT, 128)), ('y', 'z...  10.3 us
    ppermute x2, starting transfers between devices, swap(): return lax.ppermute(value, ('z_lo', 'z_hi'), pairs)  8.46 us
    pallas_call x1, Pallas kernels, inverse_root(): pl.pallas_call(functools.partial(root_kernel, factor), out_shape=jax.Shap...  8.14 us
    pallas_call x3, Pallas kernels, gram(): pl.pallas_call(functools.partial(gram_kernel, part), out_shape=(shape, sh...  7.74 us
    ppermute x3, waiting for transfers between devices, body(): lax.ppermute(pick[k], 'z_hi', [(i, i ^ k) for i in range(4)])  5.86 us
  transfers between devices with their start and end apart: 25, of which 11 were waited for; matrix products, arithmetic and copies ran while one was open for 2% of the time, Pallas kernels for 4%

profile of v4, /device:TPU:1, one launch (start us, length us, event | category | flops | bytes accessed | tf_op | source)
XLA Modules:
  0.0 122.2 jit_solution(11927949914542826152)
XLA Ops:
  0.0 1.9 %slice_bitcast_fusion.grads_ref = bf16[4,512,512]{2,1,0:T(8,128)(2,1)S(1)} fusion(bf16[1,12,512,512]{3,2,1,0:T(8,128)(2,1)} %param.1), kind=kLoop, calls=%fused_computation | loop fusion | bytes 4194304 | tf_op jit(solution)/shard_map/slice | solution.py:241
  2.0 2.6 %gram_0.1 = (f32[4352,128]{1,0:T(8,128)S(1)}, f32[4352,128]{1,0:T(8,128)S(1)}) custom-call(s32[4]{0:T(128)S(1)} %pad_add_fusion.where_ref, bf16[4,512,512]{2,1,0:T(8,128)(2,1)S(1)} %slice_bitcast_fusion.grads_ref), custom_call_target="tpu_custom_call" | custom-call | tf_op jit(solution)/shard_map/gram_0/pallas_call | solution.py:105
  4.6 3.3 %collective-permute-start = (f32[4352,128]{1,0:T(8,128)S(1)}, f32[4352,128]{1,0:T(8,128)S(1)}, u32[]{:S(2)}, u32[]{:S(2)}) collective-permute-start(f32[4352,128]{1,0:T(8,128)S(1)} %get-tuple-element.26), channel_id=1, source_target_pairs={{0,64},{64,0},{1,65},{65,1},{2,66},{66,2},{3,67},{67,3},{4,68},{68... | collective-permute-start | bytes 6684680 | tf_op jit(solution)/shard_map/ppermute | solution.py:247
  8.0 2.6 %gram_1.1 = (f32[4352,128]{1,0:T(8,128)S(1)}, f32[4352,128]{1,0:T(8,128)S(1)}) custom-call(s32[4]{0:T(128)S(1)} %pad_add_fusion.where_ref, bf16[4,512,512]{2,1,0:T(8,128)(2,1)S(1)} %slice.250.grads_ref), custom_call_target="tpu_custom_call" | custom-call | tf_op jit(solution)/shard_map/gram_1/pallas_call | solution.py:105
  10.9 2.6 %gram_2.1 = (f32[4352,128]{1,0:T(8,128)S(1)}, f32[4352,128]{1,0:T(8,128)S(1)}) custom-call(s32[4]{0:T(128)S(1)} %pad_add_fusion.where_ref, bf16[4,512,512]{2,1,0:T(8,128)(2,1)S(1)} %slice.275.grads_ref), custom_call_target="tpu_custom_call" | custom-call | tf_op jit(solution)/shard_map/gram_2/pallas_call | solution.py:105
  21.7 10.8 %collective-permute-done.9 = f32[16,80,128]{2,1,0:T(8,128)S(1)} collective-permute-done((f32[16,80,128]{2,1,0:T(8,128)S(1)}, f32[16,80,128]{2,1,0:T(8,128)S(1)}, u32[]{:S(2)}, u32[]{:S(2)}) %collective-permute-start.9) | collective-permute-done | bytes 655392 | tf_op jit(solution)/shard_map/ppermute | solution.py:220
  32.6 1.8 %collective-permute-start.10 = (f32[8,80,128]{2,1,0:T(8,128)S(1)}, f32[8,80,128]{2,1,0:T(8,128)S(1)}, u32[]{:S(2)}, u32[]{:S(2)}) collective-permute-start(f32[8,80,128]{2,1,0:T(8,128)S(1)} %slice.334), channel_id=1, source_target_pairs={{0,3},{1,2},{2,1},{3,0},{4,7},{5,6},{6,5},{7,4},{8,11},{9,10},{10,... | collective-permute-start | bytes 983048 | tf_op jit(solution)/shard_map/ppermute | solution.py:220
  34.5 1.7 %collective-permute-start.6 = (f32[8,80,128]{2,1,0:T(8,128)S(1)}, f32[8,80,128]{2,1,0:T(8,128)S(1)}, u32[]{:S(2)}, u32[]{:S(2)}) collective-permute-start(f32[8,80,128]{2,1,0:T(8,128)S(1)} %slice.324), channel_id=1, source_target_pairs={{0,128},{128,0},{1,129},{129,1},{2,130},{130,2},{3,131},{131,3},{4... | collective-permute-start | bytes 983048 | tf_op jit(solution)/shard_map/ppermute | solution.py:222
  36.3 4.8 %collective-permute-start.14 = (f32[8,80,128]{2,1,0:T(8,128)S(1)}, f32[8,80,128]{2,1,0:T(8,128)S(1)}, u32[]{:S(2)}, u32[]{:S(2)}) collective-permute-start(f32[8,80,128]{2,1,0:T(8,128)S(1)} %slice.342), channel_id=1, source_target_pairs={{128,16},{16,128},{144,32},{32,144},{160,48},{48,160},{176,0},{0,1... | collective-permute-start | bytes 983048 | tf_op jit(solution)/shard_map/ppermute | solution.py:226
  41.2 2.1 %collective-permute-start.17 = (f32[8,80,128]{2,1,0:T(8,128)S(1)}, f32[8,80,128]{2,1,0:T(8,128)S(1)}, u32[]{:S(2)}, u32[]{:S(2)}) collective-permute-start(f32[8,80,128]{2,1,0:T(8,128)S(1)} %slice.348), channel_id=1, source_target_pairs={{0,12},{4,8},{8,4},{12,0},{1,13},{5,9},{9,5},{13,1},{2,14},{6,10},... | collective-permute-start | bytes 983048 | tf_op jit(solution)/shard_map/ppermute | solution.py:220
  43.6 3.7 %collective-permute-start.11 = (f32[4,80,128]{2,1,0:T(8,128)S(1)}, f32[4,80,128]{2,1,0:T(8,128)S(1)}, u32[]{:S(2)}, u32[]{:S(2)}) collective-permute-start(f32[4,80,128]{2,1,0:T(8,128)S(1)} %slice.336), channel_id=1, source_target_pairs={{128,16},{16,128},{144,32},{32,144},{160,48},{48,160},{176,0},{0,1... | collective-permute-start | bytes 491528 | tf_op jit(solution)/shard_map/ppermute | solution.py:226
  48.2 1.8 %collective-permute-start.15 = (f32[4,80,128]{2,1,0:T(8,128)S(1)}, f32[4,80,128]{2,1,0:T(8,128)S(1)}, u32[]{:S(2)}, u32[]{:S(2)}) collective-permute-start(f32[4,80,128]{2,1,0:T(8,128)S(1)} %slice.344), channel_id=1, source_target_pairs={{0,12},{4,8},{8,4},{12,0},{1,13},{5,9},{9,5},{13,1},{2,14},{6,10},... | collective-permute-start | bytes 491528 | tf_op jit(solution)/shard_map/ppermute | solution.py:220
  50.0 2.7 %collective-permute-start.18 = (f32[4,80,128]{2,1,0:T(8,128)S(1)}, f32[4,80,128]{2,1,0:T(8,128)S(1)}, u32[]{:S(2)}, u32[]{:S(2)}) collective-permute-start(f32[4,80,128]{2,1,0:T(8,128)S(1)} %slice.350), channel_id=1, source_target_pairs={{0,3},{1,2},{2,1},{3,0},{4,7},{5,6},{6,5},{7,4},{8,11},{9,10},{10,... | collective-permute-start | bytes 491528 | tf_op jit(solution)/shard_map/ppermute | solution.py:220
  53.7 2.1 %collective-permute-done.18 = f32[4,80,128]{2,1,0:T(8,128)S(1)} collective-permute-done((f32[4,80,128]{2,1,0:T(8,128)S(1)}, f32[4,80,128]{2,1,0:T(8,128)S(1)}, u32[]{:S(2)}, u32[]{:S(2)}) %collective-permute-start.18) | collective-permute-done | bytes 163872 | tf_op jit(solution)/shard_map/ppermute | solution.py:220
  57.3 1.8 %collective-permute-start.8 = (f32[2,168,128]{2,1,0:T(8,128)S(1)}, f32[2,168,128]{2,1,0:T(8,128)S(1)}, u32[]{:S(2)}, u32[]{:S(2)}) collective-permute-start(f32[2,168,128]{2,1,0:T(8,128)S(1)} %get-tuple-element.31), channel_id=1, source_target_pairs={{0,12},{4,8},{8,4},{12,0},{1,13},{5,9},{9,5},{13,1},{2,14},{6,10},... | collective-permute-start | bytes 516104 | tf_op jit(solution)/shard_map/ppermute | solution.py:220
  59.1 1.9 %collective-permute-done.19 = f32[2,240,128]{2,1,0:T(8,128)S(1)} collective-permute-done((f32[2,240,128]{2,1,0:T(8,128)S(1)}, f32[2,240,128]{2,1,0:T(8,128)S(1)}, u32[]{:S(2)}, u32[]{:S(2)}) %collective-permute-start.19) | collective-permute-done | bytes 245792 | tf_op jit(solution)/shard_map/ppermute | solution.py:220
  61.0 1.8 %collective-permute-done.8 = f32[2,168,128]{2,1,0:T(8,128)S(1)} collective-permute-done((f32[2,168,128]{2,1,0:T(8,128)S(1)}, f32[2,168,128]{2,1,0:T(8,128)S(1)}, u32[]{:S(2)}, u32[]{:S(2)}) %collective-permute-start.8) | collective-permute-done | bytes 172064 | tf_op jit(solution)/shard_map/ppermute | solution.py:220
  64.6 3.1 %collective-permute-done.20 = f32[1,168,128]{2,1,0:T(8,128)S(1)} collective-permute-done((f32[1,168,128]{2,1,0:T(8,128)S(1)}, f32[1,168,128]{2,1,0:T(8,128)S(1)}, u32[]{:S(2)}, u32[]{:S(2)}) %collective-permute-start.20) | collective-permute-done | bytes 86048 | tf_op jit(solution)/shard_map/ppermute | solution.py:220
  68.4 3.2 %collective-permute-start.24 = (f32[136,128]{1,0:T(8,128)S(1)}, f32[136,128]{1,0:T(8,128)S(1)}, u32[]{:S(2)}, u32[]{:S(2)}) collective-permute-start(f32[136,128]{1,0:T(8,128)S(1)} %get-tuple-element.64), channel_id=1, source_target_pairs={{0,48},{16,32},{32,16},{48,0},{1,49},{17,33},{33,17},{49,1},{2,50}... | collective-permute-start | bytes 208904 | tf_op jit(solution)/shard_map/ppermute | solution.py:300
  71.6 2.0 %collective-permute-start.22 = (f32[136,128]{1,0:T(8,128)S(1)}, f32[136,128]{1,0:T(8,128)S(1)}, u32[]{:S(2)}, u32[]{:S(2)}) collective-permute-start(f32[136,128]{1,0:T(8,128)S(1)} %get-tuple-element.65), channel_id=1, source_target_pairs={{0,32},{16,48},{32,0},{48,16},{1,33},{17,49},{33,1},{49,17},{2,34}... | collective-permute-start | bytes 208904 | tf_op jit(solution)/shard_map/ppermute | solution.py:300
  74.4 5.1 %collective-permute-done.22 = f32[136,128]{1,0:T(8,128)S(1)} collective-permute-done((f32[136,128]{1,0:T(8,128)S(1)}, f32[136,128]{1,0:T(8,128)S(1)}, u32[]{:S(2)}, u32[]{:S(2)}) %collective-permute-start.22) | collective-permute-done | bytes 69664 | tf_op jit(solution)/shard_map/ppermute | solution.py:300
  79.6 10.3 %all_to_all.10.slabs_ref = f32[8,136,128]{2,1,0:T(8,128)S(1)} all-to-all(f32[8,136,128]{2,1,0:T(8,128)S(1)} %broadcast_in_dim.2), channel_id=1, replica_groups=mesh['z_lo'=2,'core'=2,'z_hi'=4,'x'=4,'y'=4] {'y','z_lo'}, dimensions={0} | all-to-all | bytes 1114112 | tf_op jit(solution)/shard_map/all_to_all | solution.py:301
  89.9 8.1 %inverse_root.1 = f32[32,8,128]{2,1,0:T(8,128)S(1)} custom-call(s32[4]{0:T(128)S(1)} %pad_add_fusion.where_ref, f32[8,136,128]{2,1,0:T(8,128)S(1)} %all_to_all.10.slabs_ref), custom_call_target="tpu_custom_call" | custom-call | tf_op jit(solution)/shard_map/inverse_root/pallas_call | solution.py:206
  98.0 23.5 %all_to_all.11 = f32[32,8,128]{2,1,0:T(8,128)S(1)} all-to-all(f32[32,8,128]{2,1,0:T(8,128)S(1)} %inverse_root.1), channel_id=1, replica_groups=mesh['z_lo'=2,'core'=2,'z_hi'=4,'x'=4,'y'=4] {'core','z_hi','x'}, dimensions={0} | all-to-all | bytes 262144 | tf_op jit(solution)/shard_map/all_to_all | solution.py:305
  (95 shorter events, 16.5 us)
Async XLA Ops:
  4.6 9.5 %collective-permute-start = (f32[4352,128]{1,0:T(8,128)S(1)}, f32[4352,128]{1,0:T(8,128)S(1)}, u32[]{:S(2)}, u32[]{:S(2)}) collective-permute-start(f32[4352,128]{1,0:T(8,128)S(1)} %get-tuple-element.26), channel_id=1, source_target_pairs={{0,64},{64,0},{1,65},{65,1},{2,66},{66,2},{3,67},{67,3},{4,68},{68... | collective-permute-start | bytes 6684680 | tf_op jit(solution)/shard_map/ppermute | solution.py:247
  10.6 4.4 %collective-permute-start.4 = (f32[4352,128]{1,0:T(8,128)S(1)}, f32[4352,128]{1,0:T(8,128)S(1)}, u32[]{:S(2)}, u32[]{:S(2)}) collective-permute-start(f32[4352,128]{1,0:T(8,128)S(1)} %get-tuple-element.29), channel_id=1, source_target_pairs={{0,64},{64,0},{1,65},{65,1},{2,66},{66,2},{3,67},{67,3},{4,68},{68... | collective-permute-start | bytes 6684680 | tf_op jit(solution)/shard_map/ppermute | solution.py:247
  13.5 4.8 %collective-permute-start.12 = (f32[4352,128]{1,0:T(8,128)S(1)}, f32[4352,128]{1,0:T(8,128)S(1)}, u32[]{:S(2)}, u32[]{:S(2)}) collective-permute-start(f32[4352,128]{1,0:T(8,128)S(1)} %get-tuple-element.34), channel_id=1, source_target_pairs={{0,64},{64,0},{1,65},{65,1},{2,66},{66,2},{3,67},{67,3},{4,68},{68... | collective-permute-start | bytes 6684680 | tf_op jit(solution)/shard_map/ppermute | solution.py:247
  14.2 29.1 %collective-permute-start.1 = (f32[16,88,128]{2,1,0:T(8,128)S(1)}, f32[16,88,128]{2,1,0:T(8,128)S(1)}, u32[]{:S(2)}, u32[]{:S(2)}) collective-permute-start(f32[16,88,128]{2,1,0:T(8,128)S(1)} %bitcast.63), channel_id=1, source_target_pairs={{0,4},{4,0},{8,12},{12,8},{1,5},{5,1},{9,13},{13,9},{2,6},{6,2},{1... | collective-permute-start | bytes 2162696 | tf_op jit(solution)/shard_map/ppermute | solution.py:220
  15.3 17.2 %collective-permute-start.9 = (f32[16,80,128]{2,1,0:T(8,128)S(1)}, f32[16,80,128]{2,1,0:T(8,128)S(1)}, u32[]{:S(2)}, u32[]{:S(2)}) collective-permute-start(f32[16,80,128]{2,1,0:T(8,128)S(1)} %pad_maximum_fusion), channel_id=1, source_target_pairs={{0,12},{4,8},{8,4},{12,0},{1,13},{5,9},{9,5},{13,1},{2,14},{6,10},... | collective-permute-start | bytes 1966088 | tf_op jit(solution)/shard_map/ppermute | solution.py:220
  16.2 18.1 %collective-permute-start.5 = (f32[16,80,128]{2,1,0:T(8,128)S(1)}, f32[16,80,128]{2,1,0:T(8,128)S(1)}, u32[]{:S(2)}, u32[]{:S(2)}) collective-permute-start(f32[16,80,128]{2,1,0:T(8,128)S(1)} %bitcast.65), channel_id=1, source_target_pairs={{0,1},{1,0},{2,3},{3,2},{4,5},{5,4},{6,7},{7,6},{8,9},{9,8},{10,11... | collective-permute-start | bytes 1966088 | tf_op jit(solution)/shard_map/ppermute | solution.py:220
  18.4 17.8 %collective-permute-start.13 = (f32[16,80,128]{2,1,0:T(8,128)S(1)}, f32[16,80,128]{2,1,0:T(8,128)S(1)}, u32[]{:S(2)}, u32[]{:S(2)}) collective-permute-start(f32[16,80,128]{2,1,0:T(8,128)S(1)} %pad_maximum_fusion.1), channel_id=1, source_target_pairs={{0,3},{1,2},{2,1},{3,0},{4,7},{5,6},{6,5},{7,4},{8,11},{9,10},{10,... | collective-permute-start | bytes 1966088 | tf_op jit(solution)/shard_map/ppermute | solution.py:220
  20.0 21.1 %collective-permute-start.16 = (f32[16,80,128]{2,1,0:T(8,128)S(1)}, f32[16,80,128]{2,1,0:T(8,128)S(1)}, u32[]{:S(2)}, u32[]{:S(2)}) collective-permute-start(f32[16,80,128]{2,1,0:T(8,128)S(1)} %bitcast.64), channel_id=1, source_target_pairs={{0,128},{128,0},{1,129},{129,1},{2,130},{130,2},{3,131},{131,3},{4... | collective-permute-start | bytes 1966088 | tf_op jit(solution)/shard_map/ppermute | solution.py:222
  32.6 10.9 %collective-permute-start.10 = (f32[8,80,128]{2,1,0:T(8,128)S(1)}, f32[8,80,128]{2,1,0:T(8,128)S(1)}, u32[]{:S(2)}, u32[]{:S(2)}) collective-permute-start(f32[8,80,128]{2,1,0:T(8,128)S(1)} %slice.334), channel_id=1, source_target_pairs={{0,3},{1,2},{2,1},{3,0},{4,7},{5,6},{6,5},{7,4},{8,11},{9,10},{10,... | collective-permute-start | bytes 983048 | tf_op jit(solution)/shard_map/ppermute | solution.py:220
  34.5 12.8 %collective-permute-start.6 = (f32[8,80,128]{2,1,0:T(8,128)S(1)}, f32[8,80,128]{2,1,0:T(8,128)S(1)}, u32[]{:S(2)}, u32[]{:S(2)}) collective-permute-start(f32[8,80,128]{2,1,0:T(8,128)S(1)} %slice.324), channel_id=1, source_target_pairs={{0,128},{128,0},{1,129},{129,1},{2,130},{130,2},{3,131},{131,3},{4... | collective-permute-start | bytes 983048 | tf_op jit(solution)/shard_map/ppermute | solution.py:222
  36.3 11.8 %collective-permute-start.14 = (f32[8,80,128]{2,1,0:T(8,128)S(1)}, f32[8,80,128]{2,1,0:T(8,128)S(1)}, u32[]{:S(2)}, u32[]{:S(2)}) collective-permute-start(f32[8,80,128]{2,1,0:T(8,128)S(1)} %slice.342), channel_id=1, source_target_pairs={{128,16},{16,128},{144,32},{32,144},{160,48},{48,160},{176,0},{0,1... | collective-permute-start | bytes 983048 | tf_op jit(solution)/shard_map/ppermute | solution.py:226
  41.2 8.8 %collective-permute-start.17 = (f32[8,80,128]{2,1,0:T(8,128)S(1)}, f32[8,80,128]{2,1,0:T(8,128)S(1)}, u32[]{:S(2)}, u32[]{:S(2)}) collective-permute-start(f32[8,80,128]{2,1,0:T(8,128)S(1)} %slice.348), channel_id=1, source_target_pairs={{0,12},{4,8},{8,4},{12,0},{1,13},{5,9},{9,5},{13,1},{2,14},{6,10},... | collective-permute-start | bytes 983048 | tf_op jit(solution)/shard_map/ppermute | solution.py:220
  43.4 9.3 %collective-permute-start.2 = (f32[8,88,128]{2,1,0:T(8,128)S(1)}, f32[8,88,128]{2,1,0:T(8,128)S(1)}, u32[]{:S(2)}, u32[]{:S(2)}) collective-permute-start(f32[8,88,128]{2,1,0:T(8,128)S(1)} %slice.318), channel_id=1, source_target_pairs={{0,1},{1,0},{2,3},{3,2},{4,5},{5,4},{6,7},{7,6},{8,9},{9,8},{10,11... | collective-permute-start | bytes 1081352 | tf_op jit(solution)/shard_map/ppermute | solution.py:220
  43.6 9.3 %collective-permute-start.11 = (f32[4,80,128]{2,1,0:T(8,128)S(1)}, f32[4,80,128]{2,1,0:T(8,128)S(1)}, u32[]{:S(2)}, u32[]{:S(2)}) collective-permute-start(f32[4,80,128]{2,1,0:T(8,128)S(1)} %slice.336), channel_id=1, source_target_pairs={{128,16},{16,128},{144,32},{32,144},{160,48},{48,160},{176,0},{0,1... | collective-permute-start | bytes 491528 | tf_op jit(solution)/shard_map/ppermute | solution.py:226
  47.4 8.6 %collective-permute-start.7 = (f32[4,80,128]{2,1,0:T(8,128)S(1)}, f32[4,80,128]{2,1,0:T(8,128)S(1)}, u32[]{:S(2)}, u32[]{:S(2)}) collective-permute-start(f32[4,80,128]{2,1,0:T(8,128)S(1)} %slice.326), channel_id=1, source_target_pairs={{0,4},{4,0},{8,12},{12,8},{1,5},{5,1},{9,13},{13,9},{2,6},{6,2},{1... | collective-permute-start | bytes 491528 | tf_op jit(solution)/shard_map/ppermute | solution.py:220
  48.2 5.5 %collective-permute-start.15 = (f32[4,80,128]{2,1,0:T(8,128)S(1)}, f32[4,80,128]{2,1,0:T(8,128)S(1)}, u32[]{:S(2)}, u32[]{:S(2)}) collective-permute-start(f32[4,80,128]{2,1,0:T(8,128)S(1)} %slice.344), channel_id=1, source_target_pairs={{0,12},{4,8},{8,4},{12,0},{1,13},{5,9},{9,5},{13,1},{2,14},{6,10},... | collective-permute-start | bytes 491528 | tf_op jit(solution)/shard_map/ppermute | solution.py:220
  50.0 5.8 %collective-permute-start.18 = (f32[4,80,128]{2,1,0:T(8,128)S(1)}, f32[4,80,128]{2,1,0:T(8,128)S(1)}, u32[]{:S(2)}, u32[]{:S(2)}) collective-permute-start(f32[4,80,128]{2,1,0:T(8,128)S(1)} %slice.350), channel_id=1, source_target_pairs={{0,3},{1,2},{2,1},{3,0},{4,7},{5,6},{6,5},{7,4},{8,11},{9,10},{10,... | collective-permute-start | bytes 491528 | tf_op jit(solution)/shard_map/ppermute | solution.py:220
  55.9 5.1 %collective-permute-start.19 = (f32[2,240,128]{2,1,0:T(8,128)S(1)}, f32[2,240,128]{2,1,0:T(8,128)S(1)}, u32[]{:S(2)}, u32[]{:S(2)}) collective-permute-start(f32[2,240,128]{2,1,0:T(8,128)S(1)} %get-tuple-element.35), channel_id=1, source_target_pairs={{0,4},{4,0},{8,12},{12,8},{1,5},{5,1},{9,13},{13,9},{2,6},{6,2},{1... | collective-permute-start | bytes 737288 | tf_op jit(solution)/shard_map/ppermute | solution.py:220
  57.3 5.6 %collective-permute-start.8 = (f32[2,168,128]{2,1,0:T(8,128)S(1)}, f32[2,168,128]{2,1,0:T(8,128)S(1)}, u32[]{:S(2)}, u32[]{:S(2)}) collective-permute-start(f32[2,168,128]{2,1,0:T(8,128)S(1)} %get-tuple-element.31), channel_id=1, source_target_pairs={{0,12},{4,8},{8,4},{12,0},{1,13},{5,9},{9,5},{13,1},{2,14},{6,10},... | collective-permute-start | bytes 516104 | tf_op jit(solution)/shard_map/ppermute | solution.py:220
  62.9 4.8 %collective-permute-start.21 = (f32[1,240,128]{2,1,0:T(8,128)S(1)}, f32[1,240,128]{2,1,0:T(8,128)S(1)}, u32[]{:S(2)}, u32[]{:S(2)}) collective-permute-start(f32[1,240,128]{2,1,0:T(8,128)S(1)} %get-tuple-element.41), channel_id=1, source_target_pairs={{0,1},{1,0},{2,3},{3,2},{4,5},{5,4},{6,7},{7,6},{8,9},{9,8},{10,11... | collective-permute-start | bytes 368648 | tf_op jit(solution)/shard_map/ppermute | solution.py:220
  63.0 4.6 %collective-permute-start.20 = (f32[1,168,128]{2,1,0:T(8,128)S(1)}, f32[1,168,128]{2,1,0:T(8,128)S(1)}, u32[]{:S(2)}, u32[]{:S(2)}) collective-permute-start(f32[1,168,128]{2,1,0:T(8,128)S(1)} %get-tuple-element.38), channel_id=1, source_target_pairs={{0,3},{1,2},{2,1},{3,0},{4,7},{5,6},{6,5},{7,4},{8,11},{9,10},{10,... | collective-permute-start | bytes 258056 | tf_op jit(solution)/shard_map/ppermute | solution.py:220
  67.9 5.7 %collective-permute-start.23 = (f32[136,128]{1,0:T(8,128)S(1)}, f32[136,128]{1,0:T(8,128)S(1)}, u32[]{:S(2)}, u32[]{:S(2)}) collective-permute-start(f32[136,128]{1,0:T(8,128)S(1)} %get-tuple-element.63), channel_id=1, source_target_pairs={{0,16},{16,0},{32,48},{48,32},{1,17},{17,1},{33,49},{49,33},{2,18}... | collective-permute-start | bytes 208904 | tf_op jit(solution)/shard_map/ppermute | solution.py:300
  68.4 6.0 %collective-permute-start.24 = (f32[136,128]{1,0:T(8,128)S(1)}, f32[136,128]{1,0:T(8,128)S(1)}, u32[]{:S(2)}, u32[]{:S(2)}) collective-permute-start(f32[136,128]{1,0:T(8,128)S(1)} %get-tuple-element.64), channel_id=1, source_target_pairs={{0,48},{16,32},{32,16},{48,0},{1,49},{17,33},{33,17},{49,1},{2,50}... | collective-permute-start | bytes 208904 | tf_op jit(solution)/shard_map/ppermute | solution.py:300
  71.6 7.9 %collective-permute-start.22 = (f32[136,128]{1,0:T(8,128)S(1)}, f32[136,128]{1,0:T(8,128)S(1)}, u32[]{:S(2)}, u32[]{:S(2)}) collective-permute-start(f32[136,128]{1,0:T(8,128)S(1)} %get-tuple-element.65), channel_id=1, source_target_pairs={{0,32},{16,48},{32,0},{48,16},{1,33},{17,49},{33,1},{49,17},{2,34}... | collective-permute-start | bytes 208904 | tf_op jit(solution)/shard_map/ppermute | solution.py:300
  (2 other events, 12.3 us)

commit v5 on v4

--- a/solution.py
+++ b/solution.py
@@ -297,7 +297,7 @@
     parts = jnp.stack(parts + parts[:1])
     high_z = lax.axis_index("z_hi")
     pick = [lax.dynamic_index_in_dim(parts, lax.bitwise_xor(high_z, k), 0, False) for k in range(4)]
-    slab = pick[0] + sum(lax.ppermute(pick[k], "z_hi", [(i, i ^ k) for i in range(4)]) for k in (2, 1, 3))
+    slab = pick[0] + sum(lax.ppermute(pick[k], "z_hi", [(i, i ^ k) for i in range(4)]) for k in (1, 2, 3))
     slabs = lax.all_to_all(
         jnp.broadcast_to(slab[None], (SLABS, UNIT, 128)), ("y", "z_lo"), 0, 0, tiled=True
     )

time: 122 us -> 122 us (level)
  waiting for transfers between devices: 28.9 us -> 26 us
  blocking collectives: 33.8 us -> 36.2 us
    ppermute x3, waiting for transfers between devices: 5.86 us -> 2.98 us  [body(): lax.ppermute(pick[k], 'z_hi', [(i, i ^ k) for i in range(4)])]
    all_to_all x1, blocking collectives: 23.5 us -> 24.8 us  [body(): arrived = lax.all_to_all(pieces, ('core', 'z_hi', 'x'), 0, 0, tiled=True)]
where the time goes in v5:
time: 122 us
  starting transfers between devices  38.1 us (31%)
  blocking collectives  36.2 us (30%)
  waiting for transfers between devices  26 us (21%)
  Pallas kernels  15.9 us (13%)
  local copies, waits for them, and re-layouts  3.14 us (3%)
  other arithmetic  1.85 us (2%)
    all_to_all x1, blocking collectives, body(): arrived = lax.all_to_all(pieces, ('core', 'z_hi', 'x'), 0, 0, tiled=True)  24.8 us
    ppermute x14, waiting for transfers between devices, swap(): return lax.ppermute(value, name[0], [(i, i ^ flip) for i in range(4)])  20.5 us
    ppermute x14, starting transfers between devices, swap(): return lax.ppermute(value, name[0], [(i, i ^ flip) for i in range(4)])  16.4 us
    all_to_all x1, blocking collectives, body(): lax.all_to_all(jnp.broadcast_to(slab[None], (SLABS, UNIT, 128)), ('y', 'z...  11.5 us
    ppermute x2, starting transfers between devices, swap(): return lax.ppermute(value, ('z_lo', 'z_hi'), pairs)  8.46 us
    pallas_call x1, Pallas kernels, inverse_root(): pl.pallas_call(functools.partial(root_kernel, factor), out_shape=jax.Shap...  8.15 us
    pallas_call x3, Pallas kernels, gram(): pl.pallas_call(functools.partial(gram_kernel, part), out_shape=(shape, sh...  7.74 us
    ppermute x3, starting transfers between devices, body(): lax.ppermute(pick[k], 'z_hi', [(i, i ^ k) for i in range(4)])  5.74 us
  transfers between devices with their start and end apart: 25, of which 11 were waited for; matrix products, arithmetic and copies ran while one was open for 2% of the time, Pallas kernels for 4%

profile of v5, /device:TPU:1, one launch (start us, length us, event | category | flops | bytes accessed | tf_op | source)
XLA Modules:
  0.0 121.7 jit_solution(12502490639897122667)
XLA Ops:
  0.0 1.9 %slice_bitcast_fusion.grads_ref = bf16[4,512,512]{2,1,0:T(8,128)(2,1)S(1)} fusion(bf16[1,12,512,512]{3,2,1,0:T(8,128)(2,1)} %param.1), kind=kLoop, calls=%fused_computation | loop fusion | bytes 4194304 | tf_op jit(solution)/shard_map/slice | solution.py:241
  2.0 2.6 %gram_0.1 = (f32[4352,128]{1,0:T(8,128)S(1)}, f32[4352,128]{1,0:T(8,128)S(1)}) custom-call(s32[4]{0:T(128)S(1)} %pad_add_fusion.where_ref, bf16[4,512,512]{2,1,0:T(8,128)(2,1)S(1)} %slice_bitcast_fusion.grads_ref), custom_call_target="tpu_custom_call" | custom-call | tf_op jit(solution)/shard_map/gram_0/pallas_call | solution.py:105
  4.6 3.3 %collective-permute-start = (f32[4352,128]{1,0:T(8,128)S(1)}, f32[4352,128]{1,0:T(8,128)S(1)}, u32[]{:S(2)}, u32[]{:S(2)}) collective-permute-start(f32[4352,128]{1,0:T(8,128)S(1)} %get-tuple-element.26), channel_id=1, source_target_pairs={{0,64},{64,0},{1,65},{65,1},{2,66},{66,2},{3,67},{67,3},{4,68},{68... | collective-permute-start | bytes 6684680 | tf_op jit(solution)/shard_map/ppermute | solution.py:247
  8.0 2.6 %gram_1.1 = (f32[4352,128]{1,0:T(8,128)S(1)}, f32[4352,128]{1,0:T(8,128)S(1)}) custom-call(s32[4]{0:T(128)S(1)} %pad_add_fusion.where_ref, bf16[4,512,512]{2,1,0:T(8,128)(2,1)S(1)} %slice.250.grads_ref), custom_call_target="tpu_custom_call" | custom-call | tf_op jit(solution)/shard_map/gram_1/pallas_call | solution.py:105
  10.9 2.6 %gram_2.1 = (f32[4352,128]{1,0:T(8,128)S(1)}, f32[4352,128]{1,0:T(8,128)S(1)}) custom-call(s32[4]{0:T(128)S(1)} %pad_add_fusion.where_ref, bf16[4,512,512]{2,1,0:T(8,128)(2,1)S(1)} %slice.275.grads_ref), custom_call_target="tpu_custom_call" | custom-call | tf_op jit(solution)/shard_map/gram_2/pallas_call | solution.py:105
  20.0 1.7 %collective-permute-start.16 = (f32[16,80,128]{2,1,0:T(8,128)S(1)}, f32[16,80,128]{2,1,0:T(8,128)S(1)}, u32[]{:S(2)}, u32[]{:S(2)}) collective-permute-start(f32[16,80,128]{2,1,0:T(8,128)S(1)} %bitcast.64), channel_id=1, source_target_pairs={{0,128},{128,0},{1,129},{129,1},{2,130},{130,2},{3,131},{131,3},{4... | collective-permute-start | bytes 1966088 | tf_op jit(solution)/shard_map/ppermute | solution.py:222
  21.7 10.8 %collective-permute-done.9 = f32[16,80,128]{2,1,0:T(8,128)S(1)} collective-permute-done((f32[16,80,128]{2,1,0:T(8,128)S(1)}, f32[16,80,128]{2,1,0:T(8,128)S(1)}, u32[]{:S(2)}, u32[]{:S(2)}) %collective-permute-start.9) | collective-permute-done | bytes 655392 | tf_op jit(solution)/shard_map/ppermute | solution.py:220
  32.6 1.8 %collective-permute-start.10 = (f32[8,80,128]{2,1,0:T(8,128)S(1)}, f32[8,80,128]{2,1,0:T(8,128)S(1)}, u32[]{:S(2)}, u32[]{:S(2)}) collective-permute-start(f32[8,80,128]{2,1,0:T(8,128)S(1)} %slice.334), channel_id=1, source_target_pairs={{0,3},{1,2},{2,1},{3,0},{4,7},{5,6},{6,5},{7,4},{8,11},{9,10},{10,... | collective-permute-start | bytes 983048 | tf_op jit(solution)/shard_map/ppermute | solution.py:220
  34.5 1.7 %collective-permute-start.6 = (f32[8,80,128]{2,1,0:T(8,128)S(1)}, f32[8,80,128]{2,1,0:T(8,128)S(1)}, u32[]{:S(2)}, u32[]{:S(2)}) collective-permute-start(f32[8,80,128]{2,1,0:T(8,128)S(1)} %slice.324), channel_id=1, source_target_pairs={{0,128},{128,0},{1,129},{129,1},{2,130},{130,2},{3,131},{131,3},{4... | collective-permute-start | bytes 983048 | tf_op jit(solution)/shard_map/ppermute | solution.py:222
  36.3 4.8 %collective-permute-start.14 = (f32[8,80,128]{2,1,0:T(8,128)S(1)}, f32[8,80,128]{2,1,0:T(8,128)S(1)}, u32[]{:S(2)}, u32[]{:S(2)}) collective-permute-start(f32[8,80,128]{2,1,0:T(8,128)S(1)} %slice.342), channel_id=1, source_target_pairs={{128,16},{16,128},{144,32},{32,144},{160,48},{48,160},{176,0},{0,1... | collective-permute-start | bytes 983048 | tf_op jit(solution)/shard_map/ppermute | solution.py:226
  41.2 2.1 %collective-permute-start.17 = (f32[8,80,128]{2,1,0:T(8,128)S(1)}, f32[8,80,128]{2,1,0:T(8,128)S(1)}, u32[]{:S(2)}, u32[]{:S(2)}) collective-permute-start(f32[8,80,128]{2,1,0:T(8,128)S(1)} %slice.348), channel_id=1, source_target_pairs={{0,12},{4,8},{8,4},{12,0},{1,13},{5,9},{9,5},{13,1},{2,14},{6,10},... | collective-permute-start | bytes 983048 | tf_op jit(solution)/shard_map/ppermute | solution.py:220
  43.6 3.7 %collective-permute-start.11 = (f32[4,80,128]{2,1,0:T(8,128)S(1)}, f32[4,80,128]{2,1,0:T(8,128)S(1)}, u32[]{:S(2)}, u32[]{:S(2)}) collective-permute-start(f32[4,80,128]{2,1,0:T(8,128)S(1)} %slice.336), channel_id=1, source_target_pairs={{128,16},{16,128},{144,32},{32,144},{160,48},{48,160},{176,0},{0,1... | collective-permute-start | bytes 491528 | tf_op jit(solution)/shard_map/ppermute | solution.py:226
  48.2 1.8 %collective-permute-start.15 = (f32[4,80,128]{2,1,0:T(8,128)S(1)}, f32[4,80,128]{2,1,0:T(8,128)S(1)}, u32[]{:S(2)}, u32[]{:S(2)}) collective-permute-start(f32[4,80,128]{2,1,0:T(8,128)S(1)} %slice.344), channel_id=1, source_target_pairs={{0,12},{4,8},{8,4},{12,0},{1,13},{5,9},{9,5},{13,1},{2,14},{6,10},... | collective-permute-start | bytes 491528 | tf_op jit(solution)/shard_map/ppermute | solution.py:220
  50.0 2.7 %collective-permute-start.18 = (f32[4,80,128]{2,1,0:T(8,128)S(1)}, f32[4,80,128]{2,1,0:T(8,128)S(1)}, u32[]{:S(2)}, u32[]{:S(2)}) collective-permute-start(f32[4,80,128]{2,1,0:T(8,128)S(1)} %slice.350), channel_id=1, source_target_pairs={{0,3},{1,2},{2,1},{3,0},{4,7},{5,6},{6,5},{7,4},{8,11},{9,10},{10,... | collective-permute-start | bytes 491528 | tf_op jit(solution)/shard_map/ppermute | solution.py:220
  53.7 2.1 %collective-permute-done.18 = f32[4,80,128]{2,1,0:T(8,128)S(1)} collective-permute-done((f32[4,80,128]{2,1,0:T(8,128)S(1)}, f32[4,80,128]{2,1,0:T(8,128)S(1)}, u32[]{:S(2)}, u32[]{:S(2)}) %collective-permute-start.18) | collective-permute-done | bytes 163872 | tf_op jit(solution)/shard_map/ppermute | solution.py:220
  57.3 1.8 %collective-permute-start.8 = (f32[2,168,128]{2,1,0:T(8,128)S(1)}, f32[2,168,128]{2,1,0:T(8,128)S(1)}, u32[]{:S(2)}, u32[]{:S(2)}) collective-permute-start(f32[2,168,128]{2,1,0:T(8,128)S(1)} %get-tuple-element.31), channel_id=1, source_target_pairs={{0,12},{4,8},{8,4},{12,0},{1,13},{5,9},{9,5},{13,1},{2,14},{6,10},... | collective-permute-start | bytes 516104 | tf_op jit(solution)/shard_map/ppermute | solution.py:220
  59.1 1.9 %collective-permute-done.19 = f32[2,240,128]{2,1,0:T(8,128)S(1)} collective-permute-done((f32[2,240,128]{2,1,0:T(8,128)S(1)}, f32[2,240,128]{2,1,0:T(8,128)S(1)}, u32[]{:S(2)}, u32[]{:S(2)}) %collective-permute-start.19) | collective-permute-done | bytes 245792 | tf_op jit(solution)/shard_map/ppermute | solution.py:220
  61.0 1.8 %collective-permute-done.8 = f32[2,168,128]{2,1,0:T(8,128)S(1)} collective-permute-done((f32[2,168,128]{2,1,0:T(8,128)S(1)}, f32[2,168,128]{2,1,0:T(8,128)S(1)}, u32[]{:S(2)}, u32[]{:S(2)}) %collective-permute-start.8) | collective-permute-done | bytes 172064 | tf_op jit(solution)/shard_map/ppermute | solution.py:220
  64.6 3.1 %collective-permute-done.20 = f32[1,168,128]{2,1,0:T(8,128)S(1)} collective-permute-done((f32[1,168,128]{2,1,0:T(8,128)S(1)}, f32[1,168,128]{2,1,0:T(8,128)S(1)}, u32[]{:S(2)}, u32[]{:S(2)}) %collective-permute-start.20) | collective-permute-done | bytes 86048 | tf_op jit(solution)/shard_map/ppermute | solution.py:220
  67.9 3.4 %collective-permute-start.23 = (f32[136,128]{1,0:T(8,128)S(1)}, f32[136,128]{1,0:T(8,128)S(1)}, u32[]{:S(2)}, u32[]{:S(2)}) collective-permute-start(f32[136,128]{1,0:T(8,128)S(1)} %get-tuple-element.63), channel_id=1, source_target_pairs={{0,32},{16,48},{32,0},{48,16},{1,33},{17,49},{33,1},{49,17},{2,34}... | collective-permute-start | bytes 208904 | tf_op jit(solution)/shard_map/ppermute | solution.py:300
  71.7 1.9 %collective-permute-start.22 = (f32[136,128]{1,0:T(8,128)S(1)}, f32[136,128]{1,0:T(8,128)S(1)}, u32[]{:S(2)}, u32[]{:S(2)}) collective-permute-start(f32[136,128]{1,0:T(8,128)S(1)} %get-tuple-element.65), channel_id=1, source_target_pairs={{0,16},{16,0},{32,48},{48,32},{1,17},{17,1},{33,49},{49,33},{2,18}... | collective-permute-start | bytes 208904 | tf_op jit(solution)/shard_map/ppermute | solution.py:300
  76.7 11.5 %all_to_all.10.slabs_ref = f32[8,136,128]{2,1,0:T(8,128)S(1)} all-to-all(f32[8,136,128]{2,1,0:T(8,128)S(1)} %broadcast_in_dim.2), channel_id=1, replica_groups=mesh['z_lo'=2,'core'=2,'z_hi'=4,'x'=4,'y'=4] {'y','z_lo'}, dimensions={0} | all-to-all | bytes 1114112 | tf_op jit(solution)/shard_map/all_to_all | solution.py:301
  88.2 8.2 %inverse_root.1 = f32[32,8,128]{2,1,0:T(8,128)S(1)} custom-call(s32[4]{0:T(128)S(1)} %pad_add_fusion.where_ref, f32[8,136,128]{2,1,0:T(8,128)S(1)} %all_to_all.10.slabs_ref), custom_call_target="tpu_custom_call" | custom-call | tf_op jit(solution)/shard_map/inverse_root/pallas_call | solution.py:206
  96.3 24.8 %all_to_all.11 = f32[32,8,128]{2,1,0:T(8,128)S(1)} all-to-all(f32[32,8,128]{2,1,0:T(8,128)S(1)} %inverse_root.1), channel_id=1, replica_groups=mesh['z_lo'=2,'core'=2,'z_hi'=4,'x'=4,'y'=4] {'core','z_hi','x'}, dimensions={0} | all-to-all | bytes 262144 | tf_op jit(solution)/shard_map/all_to_all | solution.py:305
  (95 shorter events, 16.8 us)
Async XLA Ops:
  4.6 9.5 %collective-permute-start = (f32[4352,128]{1,0:T(8,128)S(1)}, f32[4352,128]{1,0:T(8,128)S(1)}, u32[]{:S(2)}, u32[]{:S(2)}) collective-permute-start(f32[4352,128]{1,0:T(8,128)S(1)} %get-tuple-element.26), channel_id=1, source_target_pairs={{0,64},{64,0},{1,65},{65,1},{2,66},{66,2},{3,67},{67,3},{4,68},{68... | collective-permute-start | bytes 6684680 | tf_op jit(solution)/shard_map/ppermute | solution.py:247
  10.6 4.4 %collective-permute-start.4 = (f32[4352,128]{1,0:T(8,128)S(1)}, f32[4352,128]{1,0:T(8,128)S(1)}, u32[]{:S(2)}, u32[]{:S(2)}) collective-permute-start(f32[4352,128]{1,0:T(8,128)S(1)} %get-tuple-element.29), channel_id=1, source_target_pairs={{0,64},{64,0},{1,65},{65,1},{2,66},{66,2},{3,67},{67,3},{4,68},{68... | collective-permute-start | bytes 6684680 | tf_op jit(solution)/shard_map/ppermute | solution.py:247
  13.5 4.8 %collective-permute-start.12 = (f32[4352,128]{1,0:T(8,128)S(1)}, f32[4352,128]{1,0:T(8,128)S(1)}, u32[]{:S(2)}, u32[]{:S(2)}) collective-permute-start(f32[4352,128]{1,0:T(8,128)S(1)} %get-tuple-element.34), channel_id=1, source_target_pairs={{0,64},{64,0},{1,65},{65,1},{2,66},{66,2},{3,67},{67,3},{4,68},{68... | collective-permute-start | bytes 6684680 | tf_op jit(solution)/shard_map/ppermute | solution.py:247
  14.2 29.1 %collective-permute-start.1 = (f32[16,88,128]{2,1,0:T(8,128)S(1)}, f32[16,88,128]{2,1,0:T(8,128)S(1)}, u32[]{:S(2)}, u32[]{:S(2)}) collective-permute-start(f32[16,88,128]{2,1,0:T(8,128)S(1)} %bitcast.63), channel_id=1, source_target_pairs={{0,4},{4,0},{8,12},{12,8},{1,5},{5,1},{9,13},{13,9},{2,6},{6,2},{1... | collective-permute-start | bytes 2162696 | tf_op jit(solution)/shard_map/ppermute | solution.py:220
  15.3 17.2 %collective-permute-start.9 = (f32[16,80,128]{2,1,0:T(8,128)S(1)}, f32[16,80,128]{2,1,0:T(8,128)S(1)}, u32[]{:S(2)}, u32[]{:S(2)}) collective-permute-start(f32[16,80,128]{2,1,0:T(8,128)S(1)} %pad_maximum_fusion), channel_id=1, source_target_pairs={{0,12},{4,8},{8,4},{12,0},{1,13},{5,9},{9,5},{13,1},{2,14},{6,10},... | collective-permute-start | bytes 1966088 | tf_op jit(solution)/shard_map/ppermute | solution.py:220
  16.2 18.1 %collective-permute-start.5 = (f32[16,80,128]{2,1,0:T(8,128)S(1)}, f32[16,80,128]{2,1,0:T(8,128)S(1)}, u32[]{:S(2)}, u32[]{:S(2)}) collective-permute-start(f32[16,80,128]{2,1,0:T(8,128)S(1)} %bitcast.65), channel_id=1, source_target_pairs={{0,1},{1,0},{2,3},{3,2},{4,5},{5,4},{6,7},{7,6},{8,9},{9,8},{10,11... | collective-permute-start | bytes 1966088 | tf_op jit(solution)/shard_map/ppermute | solution.py:220
  18.4 17.8 %collective-permute-start.13 = (f32[16,80,128]{2,1,0:T(8,128)S(1)}, f32[16,80,128]{2,1,0:T(8,128)S(1)}, u32[]{:S(2)}, u32[]{:S(2)}) collective-permute-start(f32[16,80,128]{2,1,0:T(8,128)S(1)} %pad_maximum_fusion.1), channel_id=1, source_target_pairs={{0,3},{1,2},{2,1},{3,0},{4,7},{5,6},{6,5},{7,4},{8,11},{9,10},{10,... | collective-permute-start | bytes 1966088 | tf_op jit(solution)/shard_map/ppermute | solution.py:220
  20.0 21.1 %collective-permute-start.16 = (f32[16,80,128]{2,1,0:T(8,128)S(1)}, f32[16,80,128]{2,1,0:T(8,128)S(1)}, u32[]{:S(2)}, u32[]{:S(2)}) collective-permute-start(f32[16,80,128]{2,1,0:T(8,128)S(1)} %bitcast.64), channel_id=1, source_target_pairs={{0,128},{128,0},{1,129},{129,1},{2,130},{130,2},{3,131},{131,3},{4... | collective-permute-start | bytes 1966088 | tf_op jit(solution)/shard_map/ppermute | solution.py:222
  32.6 10.9 %collective-permute-start.10 = (f32[8,80,128]{2,1,0:T(8,128)S(1)}, f32[8,80,128]{2,1,0:T(8,128)S(1)}, u32[]{:S(2)}, u32[]{:S(2)}) collective-permute-start(f32[8,80,128]{2,1,0:T(8,128)S(1)} %slice.334), channel_id=1, source_target_pairs={{0,3},{1,2},{2,1},{3,0},{4,7},{5,6},{6,5},{7,4},{8,11},{9,10},{10,... | collective-permute-start | bytes 983048 | tf_op jit(solution)/shard_map/ppermute | solution.py:220
  34.5 12.8 %collective-permute-start.6 = (f32[8,80,128]{2,1,0:T(8,128)S(1)}, f32[8,80,128]{2,1,0:T(8,128)S(1)}, u32[]{:S(2)}, u32[]{:S(2)}) collective-permute-start(f32[8,80,128]{2,1,0:T(8,128)S(1)} %slice.324), channel_id=1, source_target_pairs={{0,128},{128,0},{1,129},{129,1},{2,130},{130,2},{3,131},{131,3},{4... | collective-permute-start | bytes 983048 | tf_op jit(solution)/shard_map/ppermute | solution.py:222
  36.3 11.8 %collective-permute-start.14 = (f32[8,80,128]{2,1,0:T(8,128)S(1)}, f32[8,80,128]{2,1,0:T(8,128)S(1)}, u32[]{:S(2)}, u32[]{:S(2)}) collective-permute-start(f32[8,80,128]{2,1,0:T(8,128)S(1)} %slice.342), channel_id=1, source_target_pairs={{128,16},{16,128},{144,32},{32,144},{160,48},{48,160},{176,0},{0,1... | collective-permute-start | bytes 983048 | tf_op jit(solution)/shard_map/ppermute | solution.py:226
  41.2 8.8 %collective-permute-start.17 = (f32[8,80,128]{2,1,0:T(8,128)S(1)}, f32[8,80,128]{2,1,0:T(8,128)S(1)}, u32[]{:S(2)}, u32[]{:S(2)}) collective-permute-start(f32[8,80,128]{2,1,0:T(8,128)S(1)} %slice.348), channel_id=1, source_target_pairs={{0,12},{4,8},{8,4},{12,0},{1,13},{5,9},{9,5},{13,1},{2,14},{6,10},... | collective-permute-start | bytes 983048 | tf_op jit(solution)/shard_map/ppermute | solution.py:220
  43.4 9.3 %collective-permute-start.2 = (f32[8,88,128]{2,1,0:T(8,128)S(1)}, f32[8,88,128]{2,1,0:T(8,128)S(1)}, u32[]{:S(2)}, u32[]{:S(2)}) collective-permute-start(f32[8,88,128]{2,1,0:T(8,128)S(1)} %slice.318), channel_id=1, source_target_pairs={{0,1},{1,0},{2,3},{3,2},{4,5},{5,4},{6,7},{7,6},{8,9},{9,8},{10,11... | collective-permute-start | bytes 1081352 | tf_op jit(solution)/shard_map/ppermute | solution.py:220
  43.6 9.3 %collective-permute-start.11 = (f32[4,80,128]{2,1,0:T(8,128)S(1)}, f32[4,80,128]{2,1,0:T(8,128)S(1)}, u32[]{:S(2)}, u32[]{:S(2)}) collective-permute-start(f32[4,80,128]{2,1,0:T(8,128)S(1)} %slice.336), channel_id=1, source_target_pairs={{128,16},{16,128},{144,32},{32,144},{160,48},{48,160},{176,0},{0,1... | collective-permute-start | bytes 491528 | tf_op jit(solution)/shard_map/ppermute | solution.py:226
  47.4 8.6 %collective-permute-start.7 = (f32[4,80,128]{2,1,0:T(8,128)S(1)}, f32[4,80,128]{2,1,0:T(8,128)S(1)}, u32[]{:S(2)}, u32[]{:S(2)}) collective-permute-start(f32[4,80,128]{2,1,0:T(8,128)S(1)} %slice.326), channel_id=1, source_target_pairs={{0,4},{4,0},{8,12},{12,8},{1,5},{5,1},{9,13},{13,9},{2,6},{6,2},{1... | collective-permute-start | bytes 491528 | tf_op jit(solution)/shard_map/ppermute | solution.py:220
  48.2 5.5 %collective-permute-start.15 = (f32[4,80,128]{2,1,0:T(8,128)S(1)}, f32[4,80,128]{2,1,0:T(8,128)S(1)}, u32[]{:S(2)}, u32[]{:S(2)}) collective-permute-start(f32[4,80,128]{2,1,0:T(8,128)S(1)} %slice.344), channel_id=1, source_target_pairs={{0,12},{4,8},{8,4},{12,0},{1,13},{5,9},{9,5},{13,1},{2,14},{6,10},... | collective-permute-start | bytes 491528 | tf_op jit(solution)/shard_map/ppermute | solution.py:220
  50.0 5.8 %collective-permute-start.18 = (f32[4,80,128]{2,1,0:T(8,128)S(1)}, f32[4,80,128]{2,1,0:T(8,128)S(1)}, u32[]{:S(2)}, u32[]{:S(2)}) collective-permute-start(f32[4,80,128]{2,1,0:T(8,128)S(1)} %slice.350), channel_id=1, source_target_pairs={{0,3},{1,2},{2,1},{3,0},{4,7},{5,6},{6,5},{7,4},{8,11},{9,10},{10,... | collective-permute-start | bytes 491528 | tf_op jit(solution)/shard_map/ppermute | solution.py:220
  55.9 5.1 %collective-permute-start.19 = (f32[2,240,128]{2,1,0:T(8,128)S(1)}, f32[2,240,128]{2,1,0:T(8,128)S(1)}, u32[]{:S(2)}, u32[]{:S(2)}) collective-permute-start(f32[2,240,128]{2,1,0:T(8,128)S(1)} %get-tuple-element.35), channel_id=1, source_target_pairs={{0,4},{4,0},{8,12},{12,8},{1,5},{5,1},{9,13},{13,9},{2,6},{6,2},{1... | collective-permute-start | bytes 737288 | tf_op jit(solution)/shard_map/ppermute | solution.py:220
  57.3 5.6 %collective-permute-start.8 = (f32[2,168,128]{2,1,0:T(8,128)S(1)}, f32[2,168,128]{2,1,0:T(8,128)S(1)}, u32[]{:S(2)}, u32[]{:S(2)}) collective-permute-start(f32[2,168,128]{2,1,0:T(8,128)S(1)} %get-tuple-element.31), channel_id=1, source_target_pairs={{0,12},{4,8},{8,4},{12,0},{1,13},{5,9},{9,5},{13,1},{2,14},{6,10},... | collective-permute-start | bytes 516104 | tf_op jit(solution)/shard_map/ppermute | solution.py:220
  62.9 4.8 %collective-permute-start.21 = (f32[1,240,128]{2,1,0:T(8,128)S(1)}, f32[1,240,128]{2,1,0:T(8,128)S(1)}, u32[]{:S(2)}, u32[]{:S(2)}) collective-permute-start(f32[1,240,128]{2,1,0:T(8,128)S(1)} %get-tuple-element.41), channel_id=1, source_target_pairs={{0,1},{1,0},{2,3},{3,2},{4,5},{5,4},{6,7},{7,6},{8,9},{9,8},{10,11... | collective-permute-start | bytes 368648 | tf_op jit(solution)/shard_map/ppermute | solution.py:220
  63.0 4.6 %collective-permute-start.20 = (f32[1,168,128]{2,1,0:T(8,128)S(1)}, f32[1,168,128]{2,1,0:T(8,128)S(1)}, u32[]{:S(2)}, u32[]{:S(2)}) collective-permute-start(f32[1,168,128]{2,1,0:T(8,128)S(1)} %get-tuple-element.38), channel_id=1, source_target_pairs={{0,3},{1,2},{2,1},{3,0},{4,7},{5,6},{6,5},{7,4},{8,11},{9,10},{10,... | collective-permute-start | bytes 258056 | tf_op jit(solution)/shard_map/ppermute | solution.py:220
  67.9 7.2 %collective-permute-start.23 = (f32[136,128]{1,0:T(8,128)S(1)}, f32[136,128]{1,0:T(8,128)S(1)}, u32[]{:S(2)}, u32[]{:S(2)}) collective-permute-start(f32[136,128]{1,0:T(8,128)S(1)} %get-tuple-element.63), channel_id=1, source_target_pairs={{0,32},{16,48},{32,0},{48,16},{1,33},{17,49},{33,1},{49,17},{2,34}... | collective-permute-start | bytes 208904 | tf_op jit(solution)/shard_map/ppermute | solution.py:300
  71.3 5.3 %collective-permute-start.24 = (f32[136,128]{1,0:T(8,128)S(1)}, f32[136,128]{1,0:T(8,128)S(1)}, u32[]{:S(2)}, u32[]{:S(2)}) collective-permute-start(f32[136,128]{1,0:T(8,128)S(1)} %get-tuple-element.64), channel_id=1, source_target_pairs={{0,48},{16,32},{32,16},{48,0},{1,49},{17,33},{33,17},{49,1},{2,50}... | collective-permute-start | bytes 208904 | tf_op jit(solution)/shard_map/ppermute | solution.py:300
  71.7 4.9 %collective-permute-start.22 = (f32[136,128]{1,0:T(8,128)S(1)}, f32[136,128]{1,0:T(8,128)S(1)}, u32[]{:S(2)}, u32[]{:S(2)}) collective-permute-start(f32[136,128]{1,0:T(8,128)S(1)} %get-tuple-element.65), channel_id=1, source_target_pairs={{0,16},{16,0},{32,48},{48,32},{1,17},{17,1},{33,49},{49,33},{2,18}... | collective-permute-start | bytes 208904 | tf_op jit(solution)/shard_map/ppermute | solution.py:300
  (2 other events, 12.3 us)

commit v6 on v5

--- a/solution.py
+++ b/solution.py
@@ -279,9 +279,9 @@
         middle = even.shape[0] // 2
         even_keep, even_send = lax.optimization_barrier((even[:middle], even[middle:]))
         odd_keep, odd_send = lax.optimization_barrier((odd[:middle], odd[middle:]))
-        even_came, odd_came = lax.optimization_barrier(
-            (swap(even_send, along + "2", False), swap(odd_send, along + "1", True))
-        )
+        even_came, odd_came = swap(even_send, along + "2", False), swap(odd_send, along + "1", True)
+        if along == "y":
+            even_came, odd_came = lax.optimization_barrier((even_came, odd_came))
         even, odd = even_keep + even_came, odd_keep + odd_came
     even, odd = even[0], odd[0]
     held = {}

time: 122 us -> 122 us (level)
  transfers between devices with their start and end apart: 25 -> 25, of which waited for: 11 -> 12; matrix products, arithmetic and copies ran while one was open for 2% -> 2% of each run, Pallas kernels for 4% -> 4%
where the time goes in v6:
time: 122 us; the launch traced here: 121 us
  starting transfers between devices  38.1 us (31%)
  blocking collectives  35.1 us (29%)
  waiting for transfers between devices  26.8 us (22%)
  Pallas kernels  15.9 us (13%)
  local copies, waits for them, and re-layouts  3.14 us (3%)
  other arithmetic  1.85 us (2%)
    all_to_all x1, blocking collectives, body(): arrived = lax.all_to_all(pieces, ('core', 'z_hi', 'x'), 0, 0, tiled=True)  24.5 us
    ppermute x14, waiting for transfers between devices, swap(): return lax.ppermute(value, name[0], [(i, i ^ flip) for i in range(4)])  20.3 us
    ppermute x14, starting transfers between devices, swap(): return lax.ppermute(value, name[0], [(i, i ^ flip) for i in range(4)])  16.4 us
    all_to_all x1, blocking collectives, body(): lax.all_to_all(jnp.broadcast_to(slab[None], (SLABS, UNIT, 128)), ('y', 'z...  10.6 us
    ppermute x2, starting transfers between devices, swap(): return lax.ppermute(value, ('z_lo', 'z_hi'), pairs)  8.46 us
    pallas_call x1, Pallas kernels, inverse_root(): pl.pallas_call(functools.partial(root_kernel, factor), out_shape=jax.Shap...  8.15 us
    pallas_call x3, Pallas kernels, gram(): pl.pallas_call(functools.partial(gram_kernel, part), out_shape=(shape, sh...  7.74 us
    ppermute x3, starting transfers between devices, body(): lax.ppermute(pick[k], 'z_hi', [(i, i ^ k) for i in range(4)])  5.74 us
  transfers between devices with their start and end apart: 25, of which 12 were waited for; matrix products, arithmetic and copies ran while one was open for 2% of the time, Pallas kernels for 4%

profile of v6, /device:TPU:1, one launch (start us, length us, event | category | flops | bytes accessed | tf_op | source)
XLA Modules:
  0.0 121.4 jit_solution(9396396877709848880)
XLA Ops:
  0.0 1.9 %slice_bitcast_fusion.grads_ref = bf16[4,512,512]{2,1,0:T(8,128)(2,1)S(1)} fusion(bf16[1,12,512,512]{3,2,1,0:T(8,128)(2,1)} %param.1), kind=kLoop, calls=%fused_computation | loop fusion | bytes 4194304 | tf_op jit(solution)/shard_map/slice | solution.py:241
  2.0 2.6 %gram_0.1 = (f32[4352,128]{1,0:T(8,128)S(1)}, f32[4352,128]{1,0:T(8,128)S(1)}) custom-call(s32[4]{0:T(128)S(1)} %pad_add_fusion.where_ref, bf16[4,512,512]{2,1,0:T(8,128)(2,1)S(1)} %slice_bitcast_fusion.grads_ref), custom_call_target="tpu_custom_call" | custom-call | tf_op jit(solution)/shard_map/gram_0/pallas_call | solution.py:105
  4.6 3.3 %collective-permute-start = (f32[4352,128]{1,0:T(8,128)S(1)}, f32[4352,128]{1,0:T(8,128)S(1)}, u32[]{:S(2)}, u32[]{:S(2)}) collective-permute-start(f32[4352,128]{1,0:T(8,128)S(1)} %get-tuple-element.24), channel_id=1, source_target_pairs={{0,64},{64,0},{1,65},{65,1},{2,66},{66,2},{3,67},{67,3},{4,68},{68... | collective-permute-start | bytes 6684680 | tf_op jit(solution)/shard_map/ppermute | solution.py:247
  8.0 2.6 %gram_1.1 = (f32[4352,128]{1,0:T(8,128)S(1)}, f32[4352,128]{1,0:T(8,128)S(1)}) custom-call(s32[4]{0:T(128)S(1)} %pad_add_fusion.where_ref, bf16[4,512,512]{2,1,0:T(8,128)(2,1)S(1)} %slice.250.grads_ref), custom_call_target="tpu_custom_call" | custom-call | tf_op jit(solution)/shard_map/gram_1/pallas_call | solution.py:105
  10.9 2.6 %gram_2.1 = (f32[4352,128]{1,0:T(8,128)S(1)}, f32[4352,128]{1,0:T(8,128)S(1)}) custom-call(s32[4]{0:T(128)S(1)} %pad_add_fusion.where_ref, bf16[4,512,512]{2,1,0:T(8,128)(2,1)S(1)} %slice.277.grads_ref), custom_call_target="tpu_custom_call" | custom-call | tf_op jit(solution)/shard_map/gram_2/pallas_call | solution.py:105
  20.0 1.7 %collective-permute-start.17 = (f32[16,80,128]{2,1,0:T(8,128)S(1)}, f32[16,80,128]{2,1,0:T(8,128)S(1)}, u32[]{:S(2)}, u32[]{:S(2)}) collective-permute-start(f32[16,80,128]{2,1,0:T(8,128)S(1)} %bitcast.64), channel_id=1, source_target_pairs={{0,128},{128,0},{1,129},{129,1},{2,130},{130,2},{3,131},{131,3},{4... | collective-permute-start | bytes 1966088 | tf_op jit(solution)/shard_map/ppermute | solution.py:222
  21.7 10.8 %collective-permute-done.10 = f32[16,80,128]{2,1,0:T(8,128)S(1)} collective-permute-done((f32[16,80,128]{2,1,0:T(8,128)S(1)}, f32[16,80,128]{2,1,0:T(8,128)S(1)}, u32[]{:S(2)}, u32[]{:S(2)}) %collective-permute-start.10) | collective-permute-done | bytes 655392 | tf_op jit(solution)/shard_map/ppermute | solution.py:220
  32.6 1.8 %collective-permute-start.11 = (f32[8,80,128]{2,1,0:T(8,128)S(1)}, f32[8,80,128]{2,1,0:T(8,128)S(1)}, u32[]{:S(2)}, u32[]{:S(2)}) collective-permute-start(f32[8,80,128]{2,1,0:T(8,128)S(1)} %slice.336), channel_id=1, source_target_pairs={{0,3},{1,2},{2,1},{3,0},{4,7},{5,6},{6,5},{7,4},{8,11},{9,10},{10,... | collective-permute-start | bytes 983048 | tf_op jit(solution)/shard_map/ppermute | solution.py:220
  34.5 1.7 %collective-permute-start.6 = (f32[8,80,128]{2,1,0:T(8,128)S(1)}, f32[8,80,128]{2,1,0:T(8,128)S(1)}, u32[]{:S(2)}, u32[]{:S(2)}) collective-permute-start(f32[8,80,128]{2,1,0:T(8,128)S(1)} %slice.324), channel_id=1, source_target_pairs={{0,128},{128,0},{1,129},{129,1},{2,130},{130,2},{3,131},{131,3},{4... | collective-permute-start | bytes 983048 | tf_op jit(solution)/shard_map/ppermute | solution.py:222
  36.3 4.8 %collective-permute-start.15 = (f32[8,80,128]{2,1,0:T(8,128)S(1)}, f32[8,80,128]{2,1,0:T(8,128)S(1)}, u32[]{:S(2)}, u32[]{:S(2)}) collective-permute-start(f32[8,80,128]{2,1,0:T(8,128)S(1)} %slice.344), channel_id=1, source_target_pairs={{128,16},{16,128},{144,32},{32,144},{160,48},{48,160},{176,0},{0,1... | collective-permute-start | bytes 983048 | tf_op jit(solution)/shard_map/ppermute | solution.py:226
  41.2 2.1 %collective-permute-start.18 = (f32[8,80,128]{2,1,0:T(8,128)S(1)}, f32[8,80,128]{2,1,0:T(8,128)S(1)}, u32[]{:S(2)}, u32[]{:S(2)}) collective-permute-start(f32[8,80,128]{2,1,0:T(8,128)S(1)} %slice.350), channel_id=1, source_target_pairs={{0,12},{4,8},{8,4},{12,0},{1,13},{5,9},{9,5},{13,1},{2,14},{6,10},... | collective-permute-start | bytes 983048 | tf_op jit(solution)/shard_map/ppermute | solution.py:220
  43.6 3.7 %collective-permute-start.12 = (f32[4,80,128]{2,1,0:T(8,128)S(1)}, f32[4,80,128]{2,1,0:T(8,128)S(1)}, u32[]{:S(2)}, u32[]{:S(2)}) collective-permute-start(f32[4,80,128]{2,1,0:T(8,128)S(1)} %slice.338), channel_id=1, source_target_pairs={{128,16},{16,128},{144,32},{32,144},{160,48},{48,160},{176,0},{0,1... | collective-permute-start | bytes 491528 | tf_op jit(solution)/shard_map/ppermute | solution.py:226
  48.2 1.8 %collective-permute-start.16 = (f32[4,80,128]{2,1,0:T(8,128)S(1)}, f32[4,80,128]{2,1,0:T(8,128)S(1)}, u32[]{:S(2)}, u32[]{:S(2)}) collective-permute-start(f32[4,80,128]{2,1,0:T(8,128)S(1)} %slice.346), channel_id=1, source_target_pairs={{0,12},{4,8},{8,4},{12,0},{1,13},{5,9},{9,5},{13,1},{2,14},{6,10},... | collective-permute-start | bytes 491528 | tf_op jit(solution)/shard_map/ppermute | solution.py:220
  50.0 2.7 %collective-permute-start.19 = (f32[4,80,128]{2,1,0:T(8,128)S(1)}, f32[4,80,128]{2,1,0:T(8,128)S(1)}, u32[]{:S(2)}, u32[]{:S(2)}) collective-permute-start(f32[4,80,128]{2,1,0:T(8,128)S(1)} %slice.352), channel_id=1, source_target_pairs={{0,3},{1,2},{2,1},{3,0},{4,7},{5,6},{6,5},{7,4},{8,11},{9,10},{10,... | collective-permute-start | bytes 491528 | tf_op jit(solution)/shard_map/ppermute | solution.py:220
  53.7 2.1 %collective-permute-done.19 = f32[4,80,128]{2,1,0:T(8,128)S(1)} collective-permute-done((f32[4,80,128]{2,1,0:T(8,128)S(1)}, f32[4,80,128]{2,1,0:T(8,128)S(1)}, u32[]{:S(2)}, u32[]{:S(2)}) %collective-permute-start.19) | collective-permute-done | bytes 163872 | tf_op jit(solution)/shard_map/ppermute | solution.py:220
  57.3 1.8 %collective-permute-start.8 = (f32[2,168,128]{2,1,0:T(8,128)S(1)}, f32[2,168,128]{2,1,0:T(8,128)S(1)}, u32[]{:S(2)}, u32[]{:S(2)}) collective-permute-start(f32[2,168,128]{2,1,0:T(8,128)S(1)} %get-tuple-element.29), channel_id=1, source_target_pairs={{0,12},{4,8},{8,4},{12,0},{1,13},{5,9},{9,5},{13,1},{2,14},{6,10},... | collective-permute-start | bytes 516104 | tf_op jit(solution)/shard_map/ppermute | solution.py:220
  59.1 1.9 %collective-permute-done.20 = f32[2,240,128]{2,1,0:T(8,128)S(1)} collective-permute-done((f32[2,240,128]{2,1,0:T(8,128)S(1)}, f32[2,240,128]{2,1,0:T(8,128)S(1)}, u32[]{:S(2)}, u32[]{:S(2)}) %collective-permute-start.20) | collective-permute-done | bytes 245792 | tf_op jit(solution)/shard_map/ppermute | solution.py:220
  65.2 2.3 %collective-permute-done.9 = f32[1,168,128]{2,1,0:T(8,128)S(1)} collective-permute-done((f32[1,168,128]{2,1,0:T(8,128)S(1)}, f32[1,168,128]{2,1,0:T(8,128)S(1)}, u32[]{:S(2)}, u32[]{:S(2)}) %collective-permute-start.9) | collective-permute-done | bytes 86048 | tf_op jit(solution)/shard_map/ppermute | solution.py:220
  67.7 3.6 %collective-permute-start.23 = (f32[136,128]{1,0:T(8,128)S(1)}, f32[136,128]{1,0:T(8,128)S(1)}, u32[]{:S(2)}, u32[]{:S(2)}) collective-permute-start(f32[136,128]{1,0:T(8,128)S(1)} %get-tuple-element.59), channel_id=1, source_target_pairs={{0,32},{16,48},{32,0},{48,16},{1,33},{17,49},{33,1},{49,17},{2,34}... | collective-permute-start | bytes 208904 | tf_op jit(solution)/shard_map/ppermute | solution.py:300
  71.6 1.9 %collective-permute-start.22 = (f32[136,128]{1,0:T(8,128)S(1)}, f32[136,128]{1,0:T(8,128)S(1)}, u32[]{:S(2)}, u32[]{:S(2)}) collective-permute-start(f32[136,128]{1,0:T(8,128)S(1)} %get-tuple-element.61), channel_id=1, source_target_pairs={{0,16},{16,0},{32,48},{48,32},{1,17},{17,1},{33,49},{49,33},{2,18}... | collective-permute-start | bytes 208904 | tf_op jit(solution)/shard_map/ppermute | solution.py:300
  74.9 2.4 %collective-permute-done.24 = f32[136,128]{1,0:T(8,128)S(1)} collective-permute-done((f32[136,128]{1,0:T(8,128)S(1)}, f32[136,128]{1,0:T(8,128)S(1)}, u32[]{:S(2)}, u32[]{:S(2)}) %collective-permute-start.24) | collective-permute-done | bytes 69664 | tf_op jit(solution)/shard_map/ppermute | solution.py:300
  77.4 10.6 %all_to_all.10.slabs_ref = f32[8,136,128]{2,1,0:T(8,128)S(1)} all-to-all(f32[8,136,128]{2,1,0:T(8,128)S(1)} %broadcast_in_dim.2), channel_id=1, replica_groups=mesh['z_lo'=2,'core'=2,'z_hi'=4,'x'=4,'y'=4] {'y','z_lo'}, dimensions={0} | all-to-all | bytes 1114112 | tf_op jit(solution)/shard_map/all_to_all | solution.py:301
  88.0 8.2 %inverse_root.1 = f32[32,8,128]{2,1,0:T(8,128)S(1)} custom-call(s32[4]{0:T(128)S(1)} %pad_add_fusion.where_ref, f32[8,136,128]{2,1,0:T(8,128)S(1)} %all_to_all.10.slabs_ref), custom_call_target="tpu_custom_call" | custom-call | tf_op jit(solution)/shard_map/inverse_root/pallas_call | solution.py:206
  96.2 24.5 %all_to_all.11 = f32[32,8,128]{2,1,0:T(8,128)S(1)} all-to-all(f32[32,8,128]{2,1,0:T(8,128)S(1)} %inverse_root.1), channel_id=1, replica_groups=mesh['z_lo'=2,'core'=2,'z_hi'=4,'x'=4,'y'=4] {'core','z_hi','x'}, dimensions={0} | all-to-all | bytes 262144 | tf_op jit(solution)/shard_map/all_to_all | solution.py:305
  (95 shorter events, 17.6 us)
Async XLA Ops:
  4.6 9.5 %collective-permute-start = (f32[4352,128]{1,0:T(8,128)S(1)}, f32[4352,128]{1,0:T(8,128)S(1)}, u32[]{:S(2)}, u32[]{:S(2)}) collective-permute-start(f32[4352,128]{1,0:T(8,128)S(1)} %get-tuple-element.24), channel_id=1, source_target_pairs={{0,64},{64,0},{1,65},{65,1},{2,66},{66,2},{3,67},{67,3},{4,68},{68... | collective-permute-start | bytes 6684680 | tf_op jit(solution)/shard_map/ppermute | solution.py:247
  10.6 4.4 %collective-permute-start.4 = (f32[4352,128]{1,0:T(8,128)S(1)}, f32[4352,128]{1,0:T(8,128)S(1)}, u32[]{:S(2)}, u32[]{:S(2)}) collective-permute-start(f32[4352,128]{1,0:T(8,128)S(1)} %get-tuple-element.27), channel_id=1, source_target_pairs={{0,64},{64,0},{1,65},{65,1},{2,66},{66,2},{3,67},{67,3},{4,68},{68... | collective-permute-start | bytes 6684680 | tf_op jit(solution)/shard_map/ppermute | solution.py:247
  13.5 4.8 %collective-permute-start.13 = (f32[4352,128]{1,0:T(8,128)S(1)}, f32[4352,128]{1,0:T(8,128)S(1)}, u32[]{:S(2)}, u32[]{:S(2)}) collective-permute-start(f32[4352,128]{1,0:T(8,128)S(1)} %get-tuple-element.34), channel_id=1, source_target_pairs={{0,64},{64,0},{1,65},{65,1},{2,66},{66,2},{3,67},{67,3},{4,68},{68... | collective-permute-start | bytes 6684680 | tf_op jit(solution)/shard_map/ppermute | solution.py:247
  14.2 29.1 %collective-permute-start.1 = (f32[16,88,128]{2,1,0:T(8,128)S(1)}, f32[16,88,128]{2,1,0:T(8,128)S(1)}, u32[]{:S(2)}, u32[]{:S(2)}) collective-permute-start(f32[16,88,128]{2,1,0:T(8,128)S(1)} %bitcast.63), channel_id=1, source_target_pairs={{0,4},{4,0},{8,12},{12,8},{1,5},{5,1},{9,13},{13,9},{2,6},{6,2},{1... | collective-permute-start | bytes 2162696 | tf_op jit(solution)/shard_map/ppermute | solution.py:220
  15.3 17.2 %collective-permute-start.10 = (f32[16,80,128]{2,1,0:T(8,128)S(1)}, f32[16,80,128]{2,1,0:T(8,128)S(1)}, u32[]{:S(2)}, u32[]{:S(2)}) collective-permute-start(f32[16,80,128]{2,1,0:T(8,128)S(1)} %pad_maximum_fusion), channel_id=1, source_target_pairs={{0,12},{4,8},{8,4},{12,0},{1,13},{5,9},{9,5},{13,1},{2,14},{6,10},... | collective-permute-start | bytes 1966088 | tf_op jit(solution)/shard_map/ppermute | solution.py:220
  16.2 18.1 %collective-permute-start.5 = (f32[16,80,128]{2,1,0:T(8,128)S(1)}, f32[16,80,128]{2,1,0:T(8,128)S(1)}, u32[]{:S(2)}, u32[]{:S(2)}) collective-permute-start(f32[16,80,128]{2,1,0:T(8,128)S(1)} %bitcast.65), channel_id=1, source_target_pairs={{0,1},{1,0},{2,3},{3,2},{4,5},{5,4},{6,7},{7,6},{8,9},{9,8},{10,11... | collective-permute-start | bytes 1966088 | tf_op jit(solution)/shard_map/ppermute | solution.py:220
  18.4 17.8 %collective-permute-start.14 = (f32[16,80,128]{2,1,0:T(8,128)S(1)}, f32[16,80,128]{2,1,0:T(8,128)S(1)}, u32[]{:S(2)}, u32[]{:S(2)}) collective-permute-start(f32[16,80,128]{2,1,0:T(8,128)S(1)} %pad_maximum_fusion.1), channel_id=1, source_target_pairs={{0,3},{1,2},{2,1},{3,0},{4,7},{5,6},{6,5},{7,4},{8,11},{9,10},{10,... | collective-permute-start | bytes 1966088 | tf_op jit(solution)/shard_map/ppermute | solution.py:220
  20.0 21.1 %collective-permute-start.17 = (f32[16,80,128]{2,1,0:T(8,128)S(1)}, f32[16,80,128]{2,1,0:T(8,128)S(1)}, u32[]{:S(2)}, u32[]{:S(2)}) collective-permute-start(f32[16,80,128]{2,1,0:T(8,128)S(1)} %bitcast.64), channel_id=1, source_target_pairs={{0,128},{128,0},{1,129},{129,1},{2,130},{130,2},{3,131},{131,3},{4... | collective-permute-start | bytes 1966088 | tf_op jit(solution)/shard_map/ppermute | solution.py:222
  32.6 10.9 %collective-permute-start.11 = (f32[8,80,128]{2,1,0:T(8,128)S(1)}, f32[8,80,128]{2,1,0:T(8,128)S(1)}, u32[]{:S(2)}, u32[]{:S(2)}) collective-permute-start(f32[8,80,128]{2,1,0:T(8,128)S(1)} %slice.336), channel_id=1, source_target_pairs={{0,3},{1,2},{2,1},{3,0},{4,7},{5,6},{6,5},{7,4},{8,11},{9,10},{10,... | collective-permute-start | bytes 983048 | tf_op jit(solution)/shard_map/ppermute | solution.py:220
  34.5 12.8 %collective-permute-start.6 = (f32[8,80,128]{2,1,0:T(8,128)S(1)}, f32[8,80,128]{2,1,0:T(8,128)S(1)}, u32[]{:S(2)}, u32[]{:S(2)}) collective-permute-start(f32[8,80,128]{2,1,0:T(8,128)S(1)} %slice.324), channel_id=1, source_target_pairs={{0,128},{128,0},{1,129},{129,1},{2,130},{130,2},{3,131},{131,3},{4... | collective-permute-start | bytes 983048 | tf_op jit(solution)/shard_map/ppermute | solution.py:222
  36.3 11.8 %collective-permute-start.15 = (f32[8,80,128]{2,1,0:T(8,128)S(1)}, f32[8,80,128]{2,1,0:T(8,128)S(1)}, u32[]{:S(2)}, u32[]{:S(2)}) collective-permute-start(f32[8,80,128]{2,1,0:T(8,128)S(1)} %slice.344), channel_id=1, source_target_pairs={{128,16},{16,128},{144,32},{32,144},{160,48},{48,160},{176,0},{0,1... | collective-permute-start | bytes 983048 | tf_op jit(solution)/shard_map/ppermute | solution.py:226
  41.2 8.8 %collective-permute-start.18 = (f32[8,80,128]{2,1,0:T(8,128)S(1)}, f32[8,80,128]{2,1,0:T(8,128)S(1)}, u32[]{:S(2)}, u32[]{:S(2)}) collective-permute-start(f32[8,80,128]{2,1,0:T(8,128)S(1)} %slice.350), channel_id=1, source_target_pairs={{0,12},{4,8},{8,4},{12,0},{1,13},{5,9},{9,5},{13,1},{2,14},{6,10},... | collective-permute-start | bytes 983048 | tf_op jit(solution)/shard_map/ppermute | solution.py:220
  43.4 9.3 %collective-permute-start.2 = (f32[8,88,128]{2,1,0:T(8,128)S(1)}, f32[8,88,128]{2,1,0:T(8,128)S(1)}, u32[]{:S(2)}, u32[]{:S(2)}) collective-permute-start(f32[8,88,128]{2,1,0:T(8,128)S(1)} %slice.318), channel_id=1, source_target_pairs={{0,1},{1,0},{2,3},{3,2},{4,5},{5,4},{6,7},{7,6},{8,9},{9,8},{10,11... | collective-permute-start | bytes 1081352 | tf_op jit(solution)/shard_map/ppermute | solution.py:220
  43.6 9.3 %collective-permute-start.12 = (f32[4,80,128]{2,1,0:T(8,128)S(1)}, f32[4,80,128]{2,1,0:T(8,128)S(1)}, u32[]{:S(2)}, u32[]{:S(2)}) collective-permute-start(f32[4,80,128]{2,1,0:T(8,128)S(1)} %slice.338), channel_id=1, source_target_pairs={{128,16},{16,128},{144,32},{32,144},{160,48},{48,160},{176,0},{0,1... | collective-permute-start | bytes 491528 | tf_op jit(solution)/shard_map/ppermute | solution.py:226
  47.4 8.6 %collective-permute-start.7 = (f32[4,80,128]{2,1,0:T(8,128)S(1)}, f32[4,80,128]{2,1,0:T(8,128)S(1)}, u32[]{:S(2)}, u32[]{:S(2)}) collective-permute-start(f32[4,80,128]{2,1,0:T(8,128)S(1)} %slice.326), channel_id=1, source_target_pairs={{0,4},{4,0},{8,12},{12,8},{1,5},{5,1},{9,13},{13,9},{2,6},{6,2},{1... | collective-permute-start | bytes 491528 | tf_op jit(solution)/shard_map/ppermute | solution.py:220
  48.2 5.5 %collective-permute-start.16 = (f32[4,80,128]{2,1,0:T(8,128)S(1)}, f32[4,80,128]{2,1,0:T(8,128)S(1)}, u32[]{:S(2)}, u32[]{:S(2)}) collective-permute-start(f32[4,80,128]{2,1,0:T(8,128)S(1)} %slice.346), channel_id=1, source_target_pairs={{0,12},{4,8},{8,4},{12,0},{1,13},{5,9},{9,5},{13,1},{2,14},{6,10},... | collective-permute-start | bytes 491528 | tf_op jit(solution)/shard_map/ppermute | solution.py:220
  50.0 5.8 %collective-permute-start.19 = (f32[4,80,128]{2,1,0:T(8,128)S(1)}, f32[4,80,128]{2,1,0:T(8,128)S(1)}, u32[]{:S(2)}, u32[]{:S(2)}) collective-permute-start(f32[4,80,128]{2,1,0:T(8,128)S(1)} %slice.352), channel_id=1, source_target_pairs={{0,3},{1,2},{2,1},{3,0},{4,7},{5,6},{6,5},{7,4},{8,11},{9,10},{10,... | collective-permute-start | bytes 491528 | tf_op jit(solution)/shard_map/ppermute | solution.py:220
  52.8 4.4 %collective-permute-start.3 = (f32[4,88,128]{2,1,0:T(8,128)S(1)}, f32[4,88,128]{2,1,0:T(8,128)S(1)}, u32[]{:S(2)}, u32[]{:S(2)}) collective-permute-start(f32[4,88,128]{2,1,0:T(8,128)S(1)} %slice.320), channel_id=1, source_target_pairs={{0,128},{128,0},{1,129},{129,1},{2,130},{130,2},{3,131},{131,3},{4... | collective-permute-start | bytes 540680 | tf_op jit(solution)/shard_map/ppermute | solution.py:222
  55.9 5.1 %collective-permute-start.20 = (f32[2,240,128]{2,1,0:T(8,128)S(1)}, f32[2,240,128]{2,1,0:T(8,128)S(1)}, u32[]{:S(2)}, u32[]{:S(2)}) collective-permute-start(f32[2,240,128]{2,1,0:T(8,128)S(1)} %get-tuple-element.36), channel_id=1, source_target_pairs={{0,4},{4,0},{8,12},{12,8},{1,5},{5,1},{9,13},{13,9},{2,6},{6,2},{1... | collective-permute-start | bytes 737288 | tf_op jit(solution)/shard_map/ppermute | solution.py:220
  57.3 5.6 %collective-permute-start.8 = (f32[2,168,128]{2,1,0:T(8,128)S(1)}, f32[2,168,128]{2,1,0:T(8,128)S(1)}, u32[]{:S(2)}, u32[]{:S(2)}) collective-permute-start(f32[2,168,128]{2,1,0:T(8,128)S(1)} %get-tuple-element.29), channel_id=1, source_target_pairs={{0,12},{4,8},{8,4},{12,0},{1,13},{5,9},{9,5},{13,1},{2,14},{6,10},... | collective-permute-start | bytes 516104 | tf_op jit(solution)/shard_map/ppermute | solution.py:220
  62.9 4.6 %collective-permute-start.9 = (f32[1,168,128]{2,1,0:T(8,128)S(1)}, f32[1,168,128]{2,1,0:T(8,128)S(1)}, u32[]{:S(2)}, u32[]{:S(2)}) collective-permute-start(f32[1,168,128]{2,1,0:T(8,128)S(1)} %get-tuple-element.31), channel_id=1, source_target_pairs={{0,3},{1,2},{2,1},{3,0},{4,7},{5,6},{6,5},{7,4},{8,11},{9,10},{10,... | collective-permute-start | bytes 258056 | tf_op jit(solution)/shard_map/ppermute | solution.py:220
  67.7 7.2 %collective-permute-start.23 = (f32[136,128]{1,0:T(8,128)S(1)}, f32[136,128]{1,0:T(8,128)S(1)}, u32[]{:S(2)}, u32[]{:S(2)}) collective-permute-start(f32[136,128]{1,0:T(8,128)S(1)} %get-tuple-element.59), channel_id=1, source_target_pairs={{0,32},{16,48},{32,0},{48,16},{1,33},{17,49},{33,1},{49,17},{2,34}... | collective-permute-start | bytes 208904 | tf_op jit(solution)/shard_map/ppermute | solution.py:300
  71.3 6.0 %collective-permute-start.24 = (f32[136,128]{1,0:T(8,128)S(1)}, f32[136,128]{1,0:T(8,128)S(1)}, u32[]{:S(2)}, u32[]{:S(2)}) collective-permute-start(f32[136,128]{1,0:T(8,128)S(1)} %get-tuple-element.60), channel_id=1, source_target_pairs={{0,48},{16,32},{32,16},{48,0},{1,49},{17,33},{33,17},{49,1},{2,50}... | collective-permute-start | bytes 208904 | tf_op jit(solution)/shard_map/ppermute | solution.py:300
  71.6 5.8 %collective-permute-start.22 = (f32[136,128]{1,0:T(8,128)S(1)}, f32[136,128]{1,0:T(8,128)S(1)}, u32[]{:S(2)}, u32[]{:S(2)}) collective-permute-start(f32[136,128]{1,0:T(8,128)S(1)} %get-tuple-element.61), channel_id=1, source_target_pairs={{0,16},{16,0},{32,48},{48,32},{1,17},{17,1},{33,49},{49,33},{2,18}... | collective-permute-start | bytes 208904 | tf_op jit(solution)/shard_map/ppermute | solution.py:300
  (2 other events, 12.0 us)

commit v7 on v5

--- a/solution.py
+++ b/solution.py
@@ -128,18 +128,27 @@
     return jnp.concatenate([top, jnp.concatenate([top[:, 256:].T, last], axis=1)], axis=0)
 
 
-def square(parts):
+def square(parts, rows=None):
     mult = functools.partial(jnp.dot, preferred_element_type=jnp.float32)
     high, low = parts
-    mixed = mult(high, low)
-    top = mult(high[:256], high)
+    moved = None
+    if rows is None:
+        mixed = mult(high, low)
+        top = mult(high[:256], high)
+    else:
+        count = rows[0].shape[0]
+        mixed = mult(jnp.concatenate([high, rows[0]], axis=0), low)
+        top = mult(jnp.concatenate([high[:256], *rows], axis=0), high)
+        moved = top[256 : 256 + count] + (mixed[512:] + top[256 + count :])
+        top, mixed = top[:256], mixed[:512]
     last = mult(high[256:], high[:, 256:])
     first = top[:, :256] + (mixed[:256, :256] + mixed[:256, :256].T)
     cross = top[:, 256:] + (mixed[:256, 256:] + mixed[256:, :256].T)
     last = last + (mixed[256:, 256:] + mixed[256:, 256:].T)
-    return jnp.concatenate(
+    whole = jnp.concatenate(
         [jnp.concatenate([first, cross], axis=1), jnp.concatenate([cross.T, last], axis=1)], axis=0
     )
+    return whole, moved
 
 
 def root_kernel(factor, where_ref, slabs_ref, out_ref, full, picked):
@@ -187,12 +196,13 @@
                 start = pl.multiple_of(32 * chunk + 8 * row_y, 8)
                 picked[8 * chunk : 8 * chunk + 8, :] = full[pl.ds(start, 8), :]
             iterate = picked[...]
-        else:
+        elif sweep == ITERS - 1:
             iterate = product(split(iterate), split(step_matrix))
         if sweep < ITERS - 1:
-            parts = split(step_matrix)
-            squared = split(square(parts))
-            fourth = split(square(squared))
+            squared, moved = square(split(step_matrix), split(iterate) if sweep else None)
+            iterate = moved if sweep else iterate
+            squared = split(squared)
+            fourth = split(square(squared)[0])
             if sweep == ITERS - 2:
                 coupled, identity = mine(coupled), mine(identity)
                 coupled = product(fourth, split(coupled))

time: 122 us -> 123 us (level)
  no operation moved by 1% of the time
where the time goes in v7:
time: 123 us
  starting transfers between devices  38.1 us (31%)
  blocking collectives  36.2 us (29%)
  waiting for transfers between devices  26 us (21%)
  Pallas kernels  17.1 us (14%)
  local copies, waits for them, and re-layouts  3.14 us (3%)
  other arithmetic  1.85 us (2%)
    all_to_all x1, blocking collectives, body(): arrived = lax.all_to_all(pieces, ('core', 'z_hi', 'x'), 0, 0, tiled=True)  24.8 us
    ppermute x14, waiting for transfers between devices, swap(): return lax.ppermute(value, name[0], [(i, i ^ flip) for i in range(4)])  20.5 us
    ppermute x14, starting transfers between devices, swap(): return lax.ppermute(value, name[0], [(i, i ^ flip) for i in range(4)])  16.4 us
    all_to_all x1, blocking collectives, body(): lax.all_to_all(jnp.broadcast_to(slab[None], (SLABS, UNIT, 128)), ('y', 'z...  11.5 us
    pallas_call x1, Pallas kernels, inverse_root(): pl.pallas_call(functools.partial(root_kernel, factor), out_shape=jax.Shap...  9.33 us
    ppermute x2, starting transfers between devices, swap(): return lax.ppermute(value, ('z_lo', 'z_hi'), pairs)  8.46 us
    pallas_call x3, Pallas kernels, gram(): pl.pallas_call(functools.partial(gram_kernel, part), out_shape=(shape, sh...  7.74 us
    ppermute x3, starting transfers between devices, body(): lax.ppermute(pick[k], 'z_hi', [(i, i ^ k) for i in range(4)])  5.74 us
  transfers between devices with their start and end apart: 25, of which 11 were waited for; matrix products, arithmetic and copies ran while one was open for 2% of the time, Pallas kernels for 4%

profile of v7, /device:TPU:1, one launch (start us, length us, event | category | flops | bytes accessed | tf_op | source)
XLA Modules:
  0.0 122.9 jit_solution(7022167955160548009)
XLA Ops:
  0.0 1.9 %slice_bitcast_fusion.grads_ref = bf16[4,512,512]{2,1,0:T(8,128)(2,1)S(1)} fusion(bf16[1,12,512,512]{3,2,1,0:T(8,128)(2,1)} %param.1), kind=kLoop, calls=%fused_computation | loop fusion | bytes 4194304 | tf_op jit(solution)/shard_map/slice | solution.py:251
  2.0 2.6 %gram_0.1 = (f32[4352,128]{1,0:T(8,128)S(1)}, f32[4352,128]{1,0:T(8,128)S(1)}) custom-call(s32[4]{0:T(128)S(1)} %pad_add_fusion.where_ref, bf16[4,512,512]{2,1,0:T(8,128)(2,1)S(1)} %slice_bitcast_fusion.grads_ref), custom_call_target="tpu_custom_call" | custom-call | tf_op jit(solution)/shard_map/gram_0/pallas_call | solution.py:105
  4.6 3.3 %collective-permute-start = (f32[4352,128]{1,0:T(8,128)S(1)}, f32[4352,128]{1,0:T(8,128)S(1)}, u32[]{:S(2)}, u32[]{:S(2)}) collective-permute-start(f32[4352,128]{1,0:T(8,128)S(1)} %get-tuple-element.26), channel_id=1, source_target_pairs={{0,64},{64,0},{1,65},{65,1},{2,66},{66,2},{3,67},{67,3},{4,68},{68... | collective-permute-start | bytes 6684680 | tf_op jit(solution)/shard_map/ppermute | solution.py:257
  8.0 2.6 %gram_1.1 = (f32[4352,128]{1,0:T(8,128)S(1)}, f32[4352,128]{1,0:T(8,128)S(1)}) custom-call(s32[4]{0:T(128)S(1)} %pad_add_fusion.where_ref, bf16[4,512,512]{2,1,0:T(8,128)(2,1)S(1)} %slice.250.grads_ref), custom_call_target="tpu_custom_call" | custom-call | tf_op jit(solution)/shard_map/gram_1/pallas_call | solution.py:105
  10.9 2.6 %gram_2.1 = (f32[4352,128]{1,0:T(8,128)S(1)}, f32[4352,128]{1,0:T(8,128)S(1)}) custom-call(s32[4]{0:T(128)S(1)} %pad_add_fusion.where_ref, bf16[4,512,512]{2,1,0:T(8,128)(2,1)S(1)} %slice.275.grads_ref), custom_call_target="tpu_custom_call" | custom-call | tf_op jit(solution)/shard_map/gram_2/pallas_call | solution.py:105
  20.0 1.7 %collective-permute-start.16 = (f32[16,80,128]{2,1,0:T(8,128)S(1)}, f32[16,80,128]{2,1,0:T(8,128)S(1)}, u32[]{:S(2)}, u32[]{:S(2)}) collective-permute-start(f32[16,80,128]{2,1,0:T(8,128)S(1)} %bitcast.64), channel_id=1, source_target_pairs={{0,128},{128,0},{1,129},{129,1},{2,130},{130,2},{3,131},{131,3},{4... | collective-permute-start | bytes 1966088 | tf_op jit(solution)/shard_map/ppermute | solution.py:232
  21.7 10.8 %collective-permute-done.9 = f32[16,80,128]{2,1,0:T(8,128)S(1)} collective-permute-done((f32[16,80,128]{2,1,0:T(8,128)S(1)}, f32[16,80,128]{2,1,0:T(8,128)S(1)}, u32[]{:S(2)}, u32[]{:S(2)}) %collective-permute-start.9) | collective-permute-done | bytes 655392 | tf_op jit(solution)/shard_map/ppermute | solution.py:230
  32.6 1.8 %collective-permute-start.10 = (f32[8,80,128]{2,1,0:T(8,128)S(1)}, f32[8,80,128]{2,1,0:T(8,128)S(1)}, u32[]{:S(2)}, u32[]{:S(2)}) collective-permute-start(f32[8,80,128]{2,1,0:T(8,128)S(1)} %slice.334), channel_id=1, source_target_pairs={{0,3},{1,2},{2,1},{3,0},{4,7},{5,6},{6,5},{7,4},{8,11},{9,10},{10,... | collective-permute-start | bytes 983048 | tf_op jit(solution)/shard_map/ppermute | solution.py:230
  34.5 1.7 %collective-permute-start.6 = (f32[8,80,128]{2,1,0:T(8,128)S(1)}, f32[8,80,128]{2,1,0:T(8,128)S(1)}, u32[]{:S(2)}, u32[]{:S(2)}) collective-permute-start(f32[8,80,128]{2,1,0:T(8,128)S(1)} %slice.324), channel_id=1, source_target_pairs={{0,128},{128,0},{1,129},{129,1},{2,130},{130,2},{3,131},{131,3},{4... | collective-permute-start | bytes 983048 | tf_op jit(solution)/shard_map/ppermute | solution.py:232
  36.3 4.8 %collective-permute-start.14 = (f32[8,80,128]{2,1,0:T(8,128)S(1)}, f32[8,80,128]{2,1,0:T(8,128)S(1)}, u32[]{:S(2)}, u32[]{:S(2)}) collective-permute-start(f32[8,80,128]{2,1,0:T(8,128)S(1)} %slice.342), channel_id=1, source_target_pairs={{128,16},{16,128},{144,32},{32,144},{160,48},{48,160},{176,0},{0,1... | collective-permute-start | bytes 983048 | tf_op jit(solution)/shard_map/ppermute | solution.py:236
  41.2 2.1 %collective-permute-start.17 = (f32[8,80,128]{2,1,0:T(8,128)S(1)}, f32[8,80,128]{2,1,0:T(8,128)S(1)}, u32[]{:S(2)}, u32[]{:S(2)}) collective-permute-start(f32[8,80,128]{2,1,0:T(8,128)S(1)} %slice.348), channel_id=1, source_target_pairs={{0,12},{4,8},{8,4},{12,0},{1,13},{5,9},{9,5},{13,1},{2,14},{6,10},... | collective-permute-start | bytes 983048 | tf_op jit(solution)/shard_map/ppermute | solution.py:230
  43.6 3.7 %collective-permute-start.11 = (f32[4,80,128]{2,1,0:T(8,128)S(1)}, f32[4,80,128]{2,1,0:T(8,128)S(1)}, u32[]{:S(2)}, u32[]{:S(2)}) collective-permute-start(f32[4,80,128]{2,1,0:T(8,128)S(1)} %slice.336), channel_id=1, source_target_pairs={{128,16},{16,128},{144,32},{32,144},{160,48},{48,160},{176,0},{0,1... | collective-permute-start | bytes 491528 | tf_op jit(solution)/shard_map/ppermute | solution.py:236
  48.2 1.8 %collective-permute-start.15 = (f32[4,80,128]{2,1,0:T(8,128)S(1)}, f32[4,80,128]{2,1,0:T(8,128)S(1)}, u32[]{:S(2)}, u32[]{:S(2)}) collective-permute-start(f32[4,80,128]{2,1,0:T(8,128)S(1)} %slice.344), channel_id=1, source_target_pairs={{0,12},{4,8},{8,4},{12,0},{1,13},{5,9},{9,5},{13,1},{2,14},{6,10},... | collective-permute-start | bytes 491528 | tf_op jit(solution)/shard_map/ppermute | solution.py:230
  50.0 2.7 %collective-permute-start.18 = (f32[4,80,128]{2,1,0:T(8,128)S(1)}, f32[4,80,128]{2,1,0:T(8,128)S(1)}, u32[]{:S(2)}, u32[]{:S(2)}) collective-permute-start(f32[4,80,128]{2,1,0:T(8,128)S(1)} %slice.350), channel_id=1, source_target_pairs={{0,3},{1,2},{2,1},{3,0},{4,7},{5,6},{6,5},{7,4},{8,11},{9,10},{10,... | collective-permute-start | bytes 491528 | tf_op jit(solution)/shard_map/ppermute | solution.py:230
  53.7 2.1 %collective-permute-done.18 = f32[4,80,128]{2,1,0:T(8,128)S(1)} collective-permute-done((f32[4,80,128]{2,1,0:T(8,128)S(1)}, f32[4,80,128]{2,1,0:T(8,128)S(1)}, u32[]{:S(2)}, u32[]{:S(2)}) %collective-permute-start.18) | collective-permute-done | bytes 163872 | tf_op jit(solution)/shard_map/ppermute | solution.py:230
  57.3 1.8 %collective-permute-start.8 = (f32[2,168,128]{2,1,0:T(8,128)S(1)}, f32[2,168,128]{2,1,0:T(8,128)S(1)}, u32[]{:S(2)}, u32[]{:S(2)}) collective-permute-start(f32[2,168,128]{2,1,0:T(8,128)S(1)} %get-tuple-element.31), channel_id=1, source_target_pairs={{0,12},{4,8},{8,4},{12,0},{1,13},{5,9},{9,5},{13,1},{2,14},{6,10},... | collective-permute-start | bytes 516104 | tf_op jit(solution)/shard_map/ppermute | solution.py:230
  59.1 1.9 %collective-permute-done.19 = f32[2,240,128]{2,1,0:T(8,128)S(1)} collective-permute-done((f32[2,240,128]{2,1,0:T(8,128)S(1)}, f32[2,240,128]{2,1,0:T(8,128)S(1)}, u32[]{:S(2)}, u32[]{:S(2)}) %collective-permute-start.19) | collective-permute-done | bytes 245792 | tf_op jit(solution)/shard_map/ppermute | solution.py:230
  61.0 1.8 %collective-permute-done.8 = f32[2,168,128]{2,1,0:T(8,128)S(1)} collective-permute-done((f32[2,168,128]{2,1,0:T(8,128)S(1)}, f32[2,168,128]{2,1,0:T(8,128)S(1)}, u32[]{:S(2)}, u32[]{:S(2)}) %collective-permute-start.8) | collective-permute-done | bytes 172064 | tf_op jit(solution)/shard_map/ppermute | solution.py:230
  64.6 3.1 %collective-permute-done.20 = f32[1,168,128]{2,1,0:T(8,128)S(1)} collective-permute-done((f32[1,168,128]{2,1,0:T(8,128)S(1)}, f32[1,168,128]{2,1,0:T(8,128)S(1)}, u32[]{:S(2)}, u32[]{:S(2)}) %collective-permute-start.20) | collective-permute-done | bytes 86048 | tf_op jit(solution)/shard_map/ppermute | solution.py:230
  67.9 3.4 %collective-permute-start.23 = (f32[136,128]{1,0:T(8,128)S(1)}, f32[136,128]{1,0:T(8,128)S(1)}, u32[]{:S(2)}, u32[]{:S(2)}) collective-permute-start(f32[136,128]{1,0:T(8,128)S(1)} %get-tuple-element.63), channel_id=1, source_target_pairs={{0,32},{16,48},{32,0},{48,16},{1,33},{17,49},{33,1},{49,17},{2,34}... | collective-permute-start | bytes 208904 | tf_op jit(solution)/shard_map/ppermute | solution.py:310
  71.7 1.9 %collective-permute-start.22 = (f32[136,128]{1,0:T(8,128)S(1)}, f32[136,128]{1,0:T(8,128)S(1)}, u32[]{:S(2)}, u32[]{:S(2)}) collective-permute-start(f32[136,128]{1,0:T(8,128)S(1)} %get-tuple-element.65), channel_id=1, source_target_pairs={{0,16},{16,0},{32,48},{48,32},{1,17},{17,1},{33,49},{49,33},{2,18}... | collective-permute-start | bytes 208904 | tf_op jit(solution)/shard_map/ppermute | solution.py:310
  76.7 11.5 %all_to_all.10.slabs_ref = f32[8,136,128]{2,1,0:T(8,128)S(1)} all-to-all(f32[8,136,128]{2,1,0:T(8,128)S(1)} %broadcast_in_dim.2), channel_id=1, replica_groups=mesh['z_lo'=2,'core'=2,'z_hi'=4,'x'=4,'y'=4] {'y','z_lo'}, dimensions={0} | all-to-all | bytes 1114112 | tf_op jit(solution)/shard_map/all_to_all | solution.py:311
  88.2 9.3 %inverse_root.1 = f32[32,8,128]{2,1,0:T(8,128)S(1)} custom-call(s32[4]{0:T(128)S(1)} %pad_add_fusion.where_ref, f32[8,136,128]{2,1,0:T(8,128)S(1)} %all_to_all.10.slabs_ref), custom_call_target="tpu_custom_call" | custom-call | tf_op jit(solution)/shard_map/inverse_root/pallas_call | solution.py:216
  97.5 24.8 %all_to_all.11 = f32[32,8,128]{2,1,0:T(8,128)S(1)} all-to-all(f32[32,8,128]{2,1,0:T(8,128)S(1)} %inverse_root.1), channel_id=1, replica_groups=mesh['z_lo'=2,'core'=2,'z_hi'=4,'x'=4,'y'=4] {'core','z_hi','x'}, dimensions={0} | all-to-all | bytes 262144 | tf_op jit(solution)/shard_map/all_to_all | solution.py:315
  (95 shorter events, 16.8 us)
Async XLA Ops:
  4.6 9.5 %collective-permute-start = (f32[4352,128]{1,0:T(8,128)S(1)}, f32[4352,128]{1,0:T(8,128)S(1)}, u32[]{:S(2)}, u32[]{:S(2)}) collective-permute-start(f32[4352,128]{1,0:T(8,128)S(1)} %get-tuple-element.26), channel_id=1, source_target_pairs={{0,64},{64,0},{1,65},{65,1},{2,66},{66,2},{3,67},{67,3},{4,68},{68... | collective-permute-start | bytes 6684680 | tf_op jit(solution)/shard_map/ppermute | solution.py:257
  10.6 4.4 %collective-permute-start.4 = (f32[4352,128]{1,0:T(8,128)S(1)}, f32[4352,128]{1,0:T(8,128)S(1)}, u32[]{:S(2)}, u32[]{:S(2)}) collective-permute-start(f32[4352,128]{1,0:T(8,128)S(1)} %get-tuple-element.29), channel_id=1, source_target_pairs={{0,64},{64,0},{1,65},{65,1},{2,66},{66,2},{3,67},{67,3},{4,68},{68... | collective-permute-start | bytes 6684680 | tf_op jit(solution)/shard_map/ppermute | solution.py:257
  13.5 4.8 %collective-permute-start.12 = (f32[4352,128]{1,0:T(8,128)S(1)}, f32[4352,128]{1,0:T(8,128)S(1)}, u32[]{:S(2)}, u32[]{:S(2)}) collective-permute-start(f32[4352,128]{1,0:T(8,128)S(1)} %get-tuple-element.34), channel_id=1, source_target_pairs={{0,64},{64,0},{1,65},{65,1},{2,66},{66,2},{3,67},{67,3},{4,68},{68... | collective-permute-start | bytes 6684680 | tf_op jit(solution)/shard_map/ppermute | solution.py:257
  14.2 29.1 %collective-permute-start.1 = (f32[16,88,128]{2,1,0:T(8,128)S(1)}, f32[16,88,128]{2,1,0:T(8,128)S(1)}, u32[]{:S(2)}, u32[]{:S(2)}) collective-permute-start(f32[16,88,128]{2,1,0:T(8,128)S(1)} %bitcast.63), channel_id=1, source_target_pairs={{0,4},{4,0},{8,12},{12,8},{1,5},{5,1},{9,13},{13,9},{2,6},{6,2},{1... | collective-permute-start | bytes 2162696 | tf_op jit(solution)/shard_map/ppermute | solution.py:230
  15.3 17.2 %collective-permute-start.9 = (f32[16,80,128]{2,1,0:T(8,128)S(1)}, f32[16,80,128]{2,1,0:T(8,128)S(1)}, u32[]{:S(2)}, u32[]{:S(2)}) collective-permute-start(f32[16,80,128]{2,1,0:T(8,128)S(1)} %pad_maximum_fusion), channel_id=1, source_target_pairs={{0,12},{4,8},{8,4},{12,0},{1,13},{5,9},{9,5},{13,1},{2,14},{6,10},... | collective-permute-start | bytes 1966088 | tf_op jit(solution)/shard_map/ppermute | solution.py:230
  16.2 18.1 %collective-permute-start.5 = (f32[16,80,128]{2,1,0:T(8,128)S(1)}, f32[16,80,128]{2,1,0:T(8,128)S(1)}, u32[]{:S(2)}, u32[]{:S(2)}) collective-permute-start(f32[16,80,128]{2,1,0:T(8,128)S(1)} %bitcast.65), channel_id=1, source_target_pairs={{0,1},{1,0},{2,3},{3,2},{4,5},{5,4},{6,7},{7,6},{8,9},{9,8},{10,11... | collective-permute-start | bytes 1966088 | tf_op jit(solution)/shard_map/ppermute | solution.py:230
  18.4 17.8 %collective-permute-start.13 = (f32[16,80,128]{2,1,0:T(8,128)S(1)}, f32[16,80,128]{2,1,0:T(8,128)S(1)}, u32[]{:S(2)}, u32[]{:S(2)}) collective-permute-start(f32[16,80,128]{2,1,0:T(8,128)S(1)} %pad_maximum_fusion.1), channel_id=1, source_target_pairs={{0,3},{1,2},{2,1},{3,0},{4,7},{5,6},{6,5},{7,4},{8,11},{9,10},{10,... | collective-permute-start | bytes 1966088 | tf_op jit(solution)/shard_map/ppermute | solution.py:230
  20.0 21.1 %collective-permute-start.16 = (f32[16,80,128]{2,1,0:T(8,128)S(1)}, f32[16,80,128]{2,1,0:T(8,128)S(1)}, u32[]{:S(2)}, u32[]{:S(2)}) collective-permute-start(f32[16,80,128]{2,1,0:T(8,128)S(1)} %bitcast.64), channel_id=1, source_target_pairs={{0,128},{128,0},{1,129},{129,1},{2,130},{130,2},{3,131},{131,3},{4... | collective-permute-start | bytes 1966088 | tf_op jit(solution)/shard_map/ppermute | solution.py:232
  32.6 10.9 %collective-permute-start.10 = (f32[8,80,128]{2,1,0:T(8,128)S(1)}, f32[8,80,128]{2,1,0:T(8,128)S(1)}, u32[]{:S(2)}, u32[]{:S(2)}) collective-permute-start(f32[8,80,128]{2,1,0:T(8,128)S(1)} %slice.334), channel_id=1, source_target_pairs={{0,3},{1,2},{2,1},{3,0},{4,7},{5,6},{6,5},{7,4},{8,11},{9,10},{10,... | collective-permute-start | bytes 983048 | tf_op jit(solution)/shard_map/ppermute | solution.py:230
  34.5 12.8 %collective-permute-start.6 = (f32[8,80,128]{2,1,0:T(8,128)S(1)}, f32[8,80,128]{2,1,0:T(8,128)S(1)}, u32[]{:S(2)}, u32[]{:S(2)}) collective-permute-start(f32[8,80,128]{2,1,0:T(8,128)S(1)} %slice.324), channel_id=1, source_target_pairs={{0,128},{128,0},{1,129},{129,1},{2,130},{130,2},{3,131},{131,3},{4... | collective-permute-start | bytes 983048 | tf_op jit(solution)/shard_map/ppermute | solution.py:232
  36.3 11.8 %collective-permute-start.14 = (f32[8,80,128]{2,1,0:T(8,128)S(1)}, f32[8,80,128]{2,1,0:T(8,128)S(1)}, u32[]{:S(2)}, u32[]{:S(2)}) collective-permute-start(f32[8,80,128]{2,1,0:T(8,128)S(1)} %slice.342), channel_id=1, source_target_pairs={{128,16},{16,128},{144,32},{32,144},{160,48},{48,160},{176,0},{0,1... | collective-permute-start | bytes 983048 | tf_op jit(solution)/shard_map/ppermute | solution.py:236
  41.2 8.8 %collective-permute-start.17 = (f32[8,80,128]{2,1,0:T(8,128)S(1)}, f32[8,80,128]{2,1,0:T(8,128)S(1)}, u32[]{:S(2)}, u32[]{:S(2)}) collective-permute-start(f32[8,80,128]{2,1,0:T(8,128)S(1)} %slice.348), channel_id=1, source_target_pairs={{0,12},{4,8},{8,4},{12,0},{1,13},{5,9},{9,5},{13,1},{2,14},{6,10},... | collective-permute-start | bytes 983048 | tf_op jit(solution)/shard_map/ppermute | solution.py:230
  43.4 9.3 %collective-permute-start.2 = (f32[8,88,128]{2,1,0:T(8,128)S(1)}, f32[8,88,128]{2,1,0:T(8,128)S(1)}, u32[]{:S(2)}, u32[]{:S(2)}) collective-permute-start(f32[8,88,128]{2,1,0:T(8,128)S(1)} %slice.318), channel_id=1, source_target_pairs={{0,1},{1,0},{2,3},{3,2},{4,5},{5,4},{6,7},{7,6},{8,9},{9,8},{10,11... | collective-permute-start | bytes 1081352 | tf_op jit(solution)/shard_map/ppermute | solution.py:230
  43.6 9.3 %collective-permute-start.11 = (f32[4,80,128]{2,1,0:T(8,128)S(1)}, f32[4,80,128]{2,1,0:T(8,128)S(1)}, u32[]{:S(2)}, u32[]{:S(2)}) collective-permute-start(f32[4,80,128]{2,1,0:T(8,128)S(1)} %slice.336), channel_id=1, source_target_pairs={{128,16},{16,128},{144,32},{32,144},{160,48},{48,160},{176,0},{0,1... | collective-permute-start | bytes 491528 | tf_op jit(solution)/shard_map/ppermute | solution.py:236
  47.4 8.6 %collective-permute-start.7 = (f32[4,80,128]{2,1,0:T(8,128)S(1)}, f32[4,80,128]{2,1,0:T(8,128)S(1)}, u32[]{:S(2)}, u32[]{:S(2)}) collective-permute-start(f32[4,80,128]{2,1,0:T(8,128)S(1)} %slice.326), channel_id=1, source_target_pairs={{0,4},{4,0},{8,12},{12,8},{1,5},{5,1},{9,13},{13,9},{2,6},{6,2},{1... | collective-permute-start | bytes 491528 | tf_op jit(solution)/shard_map/ppermute | solution.py:230
  48.2 5.5 %collective-permute-start.15 = (f32[4,80,128]{2,1,0:T(8,128)S(1)}, f32[4,80,128]{2,1,0:T(8,128)S(1)}, u32[]{:S(2)}, u32[]{:S(2)}) collective-permute-start(f32[4,80,128]{2,1,0:T(8,128)S(1)} %slice.344), channel_id=1, source_target_pairs={{0,12},{4,8},{8,4},{12,0},{1,13},{5,9},{9,5},{13,1},{2,14},{6,10},... | collective-permute-start | bytes 491528 | tf_op jit(solution)/shard_map/ppermute | solution.py:230
  50.0 5.8 %collective-permute-start.18 = (f32[4,80,128]{2,1,0:T(8,128)S(1)}, f32[4,80,128]{2,1,0:T(8,128)S(1)}, u32[]{:S(2)}, u32[]{:S(2)}) collective-permute-start(f32[4,80,128]{2,1,0:T(8,128)S(1)} %slice.350), channel_id=1, source_target_pairs={{0,3},{1,2},{2,1},{3,0},{4,7},{5,6},{6,5},{7,4},{8,11},{9,10},{10,... | collective-permute-start | bytes 491528 | tf_op jit(solution)/shard_map/ppermute | solution.py:230
  55.9 5.1 %collective-permute-start.19 = (f32[2,240,128]{2,1,0:T(8,128)S(1)}, f32[2,240,128]{2,1,0:T(8,128)S(1)}, u32[]{:S(2)}, u32[]{:S(2)}) collective-permute-start(f32[2,240,128]{2,1,0:T(8,128)S(1)} %get-tuple-element.35), channel_id=1, source_target_pairs={{0,4},{4,0},{8,12},{12,8},{1,5},{5,1},{9,13},{13,9},{2,6},{6,2},{1... | collective-permute-start | bytes 737288 | tf_op jit(solution)/shard_map/ppermute | solution.py:230
  57.3 5.6 %collective-permute-start.8 = (f32[2,168,128]{2,1,0:T(8,128)S(1)}, f32[2,168,128]{2,1,0:T(8,128)S(1)}, u32[]{:S(2)}, u32[]{:S(2)}) collective-permute-start(f32[2,168,128]{2,1,0:T(8,128)S(1)} %get-tuple-element.31), channel_id=1, source_target_pairs={{0,12},{4,8},{8,4},{12,0},{1,13},{5,9},{9,5},{13,1},{2,14},{6,10},... | collective-permute-start | bytes 516104 | tf_op jit(solution)/shard_map/ppermute | solution.py:230
  62.9 4.8 %collective-permute-start.21 = (f32[1,240,128]{2,1,0:T(8,128)S(1)}, f32[1,240,128]{2,1,0:T(8,128)S(1)}, u32[]{:S(2)}, u32[]{:S(2)}) collective-permute-start(f32[1,240,128]{2,1,0:T(8,128)S(1)} %get-tuple-element.41), channel_id=1, source_target_pairs={{0,1},{1,0},{2,3},{3,2},{4,5},{5,4},{6,7},{7,6},{8,9},{9,8},{10,11... | collective-permute-start | bytes 368648 | tf_op jit(solution)/shard_map/ppermute | solution.py:230
  63.0 4.6 %collective-permute-start.20 = (f32[1,168,128]{2,1,0:T(8,128)S(1)}, f32[1,168,128]{2,1,0:T(8,128)S(1)}, u32[]{:S(2)}, u32[]{:S(2)}) collective-permute-start(f32[1,168,128]{2,1,0:T(8,128)S(1)} %get-tuple-element.38), channel_id=1, source_target_pairs={{0,3},{1,2},{2,1},{3,0},{4,7},{5,6},{6,5},{7,4},{8,11},{9,10},{10,... | collective-permute-start | bytes 258056 | tf_op jit(solution)/shard_map/ppermute | solution.py:230
  67.9 7.2 %collective-permute-start.23 = (f32[136,128]{1,0:T(8,128)S(1)}, f32[136,128]{1,0:T(8,128)S(1)}, u32[]{:S(2)}, u32[]{:S(2)}) collective-permute-start(f32[136,128]{1,0:T(8,128)S(1)} %get-tuple-element.63), channel_id=1, source_target_pairs={{0,32},{16,48},{32,0},{48,16},{1,33},{17,49},{33,1},{49,17},{2,34}... | collective-permute-start | bytes 208904 | tf_op jit(solution)/shard_map/ppermute | solution.py:310
  71.3 5.3 %collective-permute-start.24 = (f32[136,128]{1,0:T(8,128)S(1)}, f32[136,128]{1,0:T(8,128)S(1)}, u32[]{:S(2)}, u32[]{:S(2)}) collective-permute-start(f32[136,128]{1,0:T(8,128)S(1)} %get-tuple-element.64), channel_id=1, source_target_pairs={{0,48},{16,32},{32,16},{48,0},{1,49},{17,33},{33,17},{49,1},{2,50}... | collective-permute-start | bytes 208904 | tf_op jit(solution)/shard_map/ppermute | solution.py:310
  71.7 4.9 %collective-permute-start.22 = (f32[136,128]{1,0:T(8,128)S(1)}, f32[136,128]{1,0:T(8,128)S(1)}, u32[]{:S(2)}, u32[]{:S(2)}) collective-permute-start(f32[136,128]{1,0:T(8,128)S(1)} %get-tuple-element.65), channel_id=1, source_target_pairs={{0,16},{16,0},{32,48},{48,32},{1,17},{17,1},{33,49},{49,33},{2,18}... | collective-permute-start | bytes 208904 | tf_op jit(solution)/shard_map/ppermute | solution.py:310
  (2 other events, 12.3 us)
